TPU v7x, 128 devices: a whole 4x4x4 slice. The times are simulated.
128 devices in a mesh: gx: 8 (over z, x_hi), gy: 16 (over x_lo, y, core).
Axes of the slice: x: 4 (x_hi: 2, x_lo: 2; x = x_hi * 2 + x_lo), y: 4, z: 4, core: 2. Of those that a mesh axis runs over, the one named last changes fastest.
Arguments:
- source_now: float32 [256, 128, 128], P('gx', 'gy'), may hold values from -6 to 6
- source_next: float32 [256, 128, 128], P('gx', 'gy'), may hold values from -6 to 6
- receiver_now: float32 [256, 128, 128], P('gx', 'gy'), may hold values from -1.5 to 1.5
- receiver_next: float32 [256, 128, 128], P('gx', 'gy'), may hold values from -1.5 to 1.5
- courant: float32 [256, 128, 128], P('gx', 'gy'), may hold values from 0.05 to 0.25
- source_cell: int32 [1], replicated, may hold values from 0 to 4194303
- wavelet: float32 [2], replicated, may hold values from -24 to 24
- receiver_cells: int32 [32768], P(('gx', 'gy')), may hold values from 0 to 4194303
- receiver_traces: float32 [2, 32768], P(None, ('gx', 'gy')), may hold values from -80 to 80
- strip_depth: int32 [128, 256], P('gy', 'gx'), may hold values from 0 to 124
- strip_values: float32 [2, 4, 128, 256], P(None, None, 'gy', 'gx'), may hold values from -6 to 6
Outputs:
- source_field: float32 [256, 128, 128], P('gx', 'gy')
- receiver_field: float32 [256, 128, 128], P('gx', 'gy')
- angle_image: float32 [32, 64, 1024], P('gy', 'gx')
All inputs are finite; a program needn't handle non-finite values.
Results may differ from a plain program's by a relative error of at most 0.00011.
Values sent between devices are 32-bit elements; how exact they have to be, the bound alone decides.
No kernel may reach another device: no remote copies, remote signals or barrier semaphores. Data moves between devices by JAX's collectives and lax.ppermute only.
A program may use at most 128 MiB of HBM per device.

v0:
```python
import math

import jax
import jax.numpy as jnp
from jax import lax
from jax.sharding import PartitionSpec as P

STEPS = 2


COEFS = (-205.0 / 72.0, 8.0 / 5.0, -1.0 / 5.0, 8.0 / 315.0, -1.0 / 560.0)
SLOPES = [math.tan(math.pi * (-60.0 + 120.0 * (angle + 0.5) / 32.0) / 180.0) for angle in range(32)]


def padded_2(array, sides, width):
    for axis, dim in sides:
        size, length = (lax.axis_size(axis), array.shape[dim])
        up = [(i, (i + 1) % size) for i in range(size - 1)]
        down = [(j, i) for i, j in up]
        last = lax.slice_in_dim(array, length - width, length, axis=dim)
        initial = lax.slice_in_dim(array, 0, width, axis=dim)
        before = lax.ppermute(last, axis, up)
        after = lax.ppermute(initial, axis, down)
        array = jnp.concatenate([before, array, after], axis=dim)
    return array


def laplacian(padded):
    size_x = padded.shape[-3] - 8
    size_y = padded.shape[-2] - 8
    size_z = padded.shape[-1] - 8
    core = padded[..., 4 : 4 + size_x, 4 : 4 + size_y, 4 : 4 + size_z]
    total = 3.0 * COEFS[0] * core
    for reach in range(1, 5):
        pairs = (
            padded[..., 4 + reach : 4 + reach + size_x, 4 : 4 + size_y, 4 : 4 + size_z]
            + padded[..., 4 - reach : 4 - reach + size_x, 4 : 4 + size_y, 4 : 4 + size_z]
        )
        pairs = (
            pairs
            + padded[..., 4 : 4 + size_x, 4 + reach : 4 + reach + size_y, 4 : 4 + size_z]
            + padded[..., 4 : 4 + size_x, 4 - reach : 4 - reach + size_y, 4 : 4 + size_z]
        )
        pairs = (
            pairs
            + padded[..., 4 : 4 + size_x, 4 : 4 + size_y, 4 + reach : 4 + reach + size_z]
            + padded[..., 4 : 4 + size_x, 4 : 4 + size_y, 4 - reach : 4 - reach + size_z]
        )
        total = total + COEFS[reach] * pairs
    return total


def slant_table(depth_points):
    offsets = jnp.arange(33, dtype=jnp.int32).astype(jnp.float32) - 16.0
    slopes = jnp.asarray(SLOPES, dtype=jnp.float32)
    depths = jnp.arange(depth_points, dtype=jnp.int32).astype(jnp.float32)
    where_at = depths[None, None, :] + offsets[:, None, None] * slopes[None, :, None] / 4.0
    lower = jnp.floor(where_at)
    frac = where_at - lower
    lower_index = lower.astype(jnp.int32)
    rows = jnp.arange(depth_points, dtype=jnp.int32)[None, :, None, None]
    low_hit = rows == lower_index[:, None, :, :]
    high_hit = rows == (lower_index + 1)[:, None, :, :]
    zero = jnp.zeros((), jnp.float32)
    table = jnp.where(low_hit, (1.0 - frac)[:, None, :, :], zero) + jnp.where(
        high_hit, frac[:, None, :, :], zero
    )
    return table.reshape(33 * depth_points, 32 * depth_points)


def correlate(fields):
    count_x = fields.shape[1] - 32
    terms = []
    for offset in range(-16, 17):
        left = fields[0, 16 - offset : 16 - offset + count_x : 4]
        right = fields[1, 16 + offset : 16 + offset + count_x : 4]
        terms.append(left * right)
    return jnp.stack(terms, axis=2)


def body(
    source_now,
    source_next,
    receiver_now,
    receiver_next,
    courant,
    source_cell,
    wavelet,
    receiver_cells,
    receiver_traces,
    strip_depth,
    strip_values,
):
    tile_x, tile_y, tile_z = source_now.shape
    shape = source_now.shape
    total_cells = tile_x * tile_y * tile_z
    column_cells = tile_y * lax.axis_size("gy") * tile_z
    start_x = lax.axis_index("gx") * tile_x
    start_y = lax.axis_index("gy") * tile_y
    every_cell = lax.all_gather(receiver_cells, ("gx", "gy"), axis=0, tiled=True)
    every_trace = lax.all_gather(receiver_traces, ("gx", "gy"), axis=1, tiled=True)

    def local_index(flat):
        cell_x = flat // column_cells - start_x
        remain = flat % column_cells
        cell_y = remain // tile_z - start_y
        cell_z = remain % tile_z
        within = (cell_x >= 0) & (cell_x < tile_x) & (cell_y >= 0) & (cell_y < tile_y)
        return jnp.where(within, (cell_x * tile_y + cell_y) * tile_z + cell_z, total_cells)

    courant_flat = courant.reshape(-1)
    receiver_local = local_index(every_cell)
    receiver_scale = courant_flat[jnp.minimum(receiver_local, total_cells - 1)]
    source_local = local_index(source_cell)
    source_scale = courant_flat[jnp.minimum(source_local, total_cells - 1)]
    depth_index = jnp.arange(tile_z, dtype=jnp.int32)
    relative = depth_index[None, None, :] - jnp.transpose(strip_depth)[:, :, None]
    inside = (relative >= 0) & (relative < 4)
    lag_image = jnp.zeros((tile_x // 4, tile_y // 4, 33, tile_z // 4), jnp.float32)
    for step in range(STEPS):
        fields = jnp.stack([source_now, receiver_now])
        padded = padded_2(fields, (("gx", 1), ("gy", 2)), 4)
        curvature = laplacian(jnp.pad(padded, ((0, 0), (0, 0), (0, 0), (4, 4))))
        source_new = 2.0 * source_now - source_next + courant * curvature[0]
        source_new = (
            source_new.reshape(-1)
            .at[source_local]
            .add(-source_scale * wavelet[step], mode="drop")
            .reshape(shape)
        )
        strip = strip_values[step]
        filled = jnp.zeros_like(source_new)
        for layer in range(4):
            filled = filled + jnp.where(
                relative == layer, jnp.transpose(strip[layer])[:, :, None], 0.0
            )
        source_new = jnp.where(inside, filled, source_new)
        receiver_new = 2.0 * receiver_now - receiver_next + courant * curvature[1]
        receiver_new = (
            receiver_new.reshape(-1)
            .at[receiver_local]
            .add(receiver_scale * every_trace[step], mode="drop")
            .reshape(shape)
        )
        widened = padded_2(jnp.stack([source_new, receiver_new]), (("gx", 1),), 16)[:, :, ::4, ::4]
        lag_image = lag_image + correlate(widened)
        source_next, source_now = (source_now, source_new)
        receiver_next, receiver_now = (receiver_now, receiver_new)
    depth_points = tile_z // 4
    points_x = tile_x // 4
    points_y = tile_y // 4
    table = slant_table(depth_points)
    angles = jnp.dot(
        lag_image.reshape(points_x * points_y, 33 * depth_points),
        table,
        precision=lax.Precision.HIGHEST,
        preferred_element_type=jnp.float32,
    )
    angles = jnp.transpose(
        angles.reshape(points_x, points_y, 32, depth_points), (2, 0, 1, 3)
    ).reshape(32, points_x, points_y * depth_points)
    arranged = lax.all_to_all(angles, "gy", split_axis=0, concat_axis=2, tiled=True)
    return (source_now, receiver_now, arranged)


def solution(mesh):
    return jax.shard_map(
        body,
        mesh=mesh,
        in_specs=(
            P("gx", "gy", None),
            P("gx", "gy", None),
            P("gx", "gy", None),
            P("gx", "gy", None),
            P("gx", "gy", None),
            P(),
            P(),
            P(("gx", "gy")),
            P(None, ("gx", "gy")),
            P("gy", "gx"),
            P(None, None, "gy", "gx"),
        ),
        out_specs=(P("gx", "gy", None), P("gx", "gy", None), P("gy", "gx", None)),
        check_vma=False,
    )
```

profile of v0, /device:TPU:5, one launch (start us, length us, event | category | flops | bytes accessed | tf_op | source)
XLA Modules:
  0.0 804.6 jit_solution(8363209501960808428)
XLA Ops:
  1.4 3.5 collective-permute-start.1
  9.6 37.4 %all-gather = s32[128,1,256]{2,1,0:T(1,128)S(1)} all-gather(s32[1,1,256]{2,1,0:T(1,128)S(1)} %bitcast.295), channel_id=1, replica_groups=mesh['gx'=8,'gy'=16] {'gx','gy'}, dimensions={0}, use_global_device_ids=true | all-gather | bytes 132096 | tf_op jit(solution)/shard_map/all_gather | solution.py:100
  47.0 33.2 %all_gather.7 = f32[2,32768]{1,0:T(2,128)S(1)} all-gather(f32[2,256]{1,0:T(2,128)S(1)} %copy-done.12), channel_id=1, replica_groups=mesh['gx'=8,'gy'=16] {'gx','gy'}, dimensions={1}, use_global_device_ids=true | all-gather | bytes 264192 | tf_op jit(solution)/shard_map/all_gather | solution.py:101
  80.4 8.2 %eq.125 = s32[33,32,32,32]{3,2,1,0:T(8,128)} broadcast(s32[33,32,32]{2,1,0:T(8,128)S(1)} %get-tuple-element.76), dimensions={0,2,3} | broadcast | bytes 4460544 | tf_op jit(solution)/shard_map/eq | solution.py:62
  88.5 14.0 %eq.126 = s32[1056,1024]{1,0:T(8,128)} reshape(s32[33,32,32,32]{3,2,1,0:T(8,128)} %eq.125) | data formatting | bytes 8650752 | tf_op jit(solution)/shard_map/eq | solution.py:62
  102.5 8.2 %eq.128 = s32[33,32,32,32]{3,2,1,0:T(8,128)} broadcast(s32[33,32,32]{2,1,0:T(8,128)S(1)} %broadcast_add_fusion), dimensions={0,2,3} | broadcast | bytes 4460544 | tf_op jit(solution)/shard_map/eq | solution.py:63
  110.7 14.0 %eq.129 = s32[1056,1024]{1,0:T(8,128)} reshape(s32[33,32,32,32]{3,2,1,0:T(8,128)} %eq.128) | data formatting | bytes 8650752 | tf_op jit(solution)/shard_map/eq | solution.py:63
  124.6 8.2 %broadcast_in_dim.152 = f32[33,32,32,32]{3,2,1,0:T(8,128)} broadcast(f32[33,32,32]{2,1,0:T(8,128)S(1)} %get-tuple-element.77), dimensions={0,2,3} | broadcast | bytes 4460544 | tf_op jit(solution)/shard_map/jit(_where)/broadcast_in_dim | solution.py:65
  132.8 14.0 %broadcast_in_dim.153 = f32[1056,1024]{1,0:T(8,128)} reshape(f32[33,32,32,32]{3,2,1,0:T(8,128)} %broadcast_in_dim.152) | data formatting | bytes 8650752 | tf_op jit(solution)/shard_map/jit(_where)/broadcast_in_dim | solution.py:65
  146.8 8.2 %broadcast_in_dim.155 = f32[33,32,32,32]{3,2,1,0:T(8,128)} broadcast(f32[33,32,32]{2,1,0:T(8,128)S(1)} %get-tuple-element.78), dimensions={0,2,3} | broadcast | bytes 4460544 | tf_op jit(solution)/shard_map/jit(_where)/broadcast_in_dim | solution.py:65
  154.9 14.0 %broadcast_in_dim.156 = f32[1056,1024]{1,0:T(8,128)} reshape(f32[33,32,32,32]{3,2,1,0:T(8,128)} %broadcast_in_dim.155) | data formatting | bytes 8650752 | tf_op jit(solution)/shard_map/jit(_where)/broadcast_in_dim | solution.py:65
  169.8 180.5 %gather_fusion = f32[32768]{0:T(1024)S(1)} fusion(f32[32768]{0:T(1024)S(1)} %bitcast.274, s32[32768]{0:T(1024)S(1)} %get-tuple-element.38), kind=kCustom, calls=%fused_computation | custom fusion | bytes 393216 | tf_op jit(solution)/shard_map/gather | solution.py:113
  350.4 8.7 %add_bitcast_fusion = f32[1024,1056]{0,1:T(8,128)} fusion(f32[1056,1024]{1,0:T(8,128)} %broadcast_in_dim.156, f32[1056,1024]{1,0:T(8,128)} %broadcast_in_dim.153, s32[1056,1024]{1,0:T(8,128)} %eq.129, s32[1056,1024]{1,0:T(8,128)} %eq.126, s32[1056]{0:T(1024)S(1)} %eq.123), kind=kLoop, calls=%fused_computation.3 | loop fusion | flops 5406720 | bytes 21631104 | tf_op jit(solution)/shard_map/dot_general | solution.py:153
  368.7 5.7 copy.95
  376.4 175.1 %scatter_fusion = f32[32768]{0:T(1024)S(1)} fusion(f32[32768]{0:T(1024)S(1)} %get-tuple-element.43, s32[32768]{0:T(1024)S(1)} %compare_select_fusion.1, f32[32768]{0:T(1024)S(1)} %get-tuple-element.67), kind=kCustom, calls=%fused_computation.1 | custom fusion | flops 32768 | bytes 524288 | tf_op jit(solution)/shard_map/scatter-add | solution.py:142
  553.2 3.8 collective-permute-start.5
  560.1 4.7 collective-permute-start.8
  567.0 4.7 collective-permute-start.7
  581.5 175.1 %scatter_fusion.1 = f32[32768]{0:T(1024)S(1)} fusion(f32[32768]{0:T(1024)S(1)} %get-tuple-element.40, s32[32768]{0:T(1024)S(1)} %compare_select_fusion.1, f32[32768]{0:T(1024)S(1)} %get-tuple-element.66), kind=kCustom, calls=%fused_computation.2 | custom fusion | flops 32768 | bytes 524288 | tf_op jit(solution)/shard_map/scatter-add | solution.py:142
  756.9 5.2 collective-permute-start.10
  764.8 5.4 collective-permute-done.11
  774.5 12.0 %convolution_bitcast_fusion = f32[32,8,2,32]{3,1,0,2:T(8,128)S(1)} fusion(f32[32,32,1056,1]{2,1,0,3:T(8,128)} %bitcast.277, f32[8,2,1056,1]{2,0,1,3:T(8,128)S(1)} %reshape.1551), kind=kOutput, calls=%fused_computation.17 | convolution fusion | flops 207618048 | bytes 4458496 | tf_op jit(solution)/shard_map/dot_general | solution.py:153
  787.7 8.9 %all-to-all-start = ((f32[16,1,1024]{2,1,0:T(1,128)}), f32[16,1,1024]{2,1,0:T(1,128)S(1)}, u32[]{:S(2)}, u32[]{:S(2)}) async-start(f32[16,1,1024]{2,1,0:T(1,128)} %reshape.1554), calls=%async_computation | async-start | bytes 131072 | tf_op jit(solution)/shard_map/all_to_all | solution.py:162
  797.5 4.9 all-to-all-done
  (173 shorter events, 44.6 us)
Async XLA Ops:
  0.6 8.9 %copy-start.14 = (s32[256]{0:T(256)S(1)}, s32[256]{0:T(256)}, u32[]{:S(2)}) copy-start(s32[256]{0:T(256)} %param.23) | copy-start | bytes 3076
  0.6 46.3 %copy-start.12 = (f32[2,256]{1,0:T(2,128)S(1)}, f32[2,256]{1,0:T(2,128)}, u32[]{:S(2)}) copy-start(f32[2,256]{1,0:T(2,128)} %param.24) | copy-start | bytes 6148
  1.4 357.7 %collective-permute-start.1 = (f32[2,4,8,128]{3,2,1,0:T(8,128)S(1)}, f32[2,4,8,128]{3,2,1,0:T(8,128)S(1)}, u32[]{:S(2)}, u32[]{:S(2)}) collective-permute-start(f32[2,4,8,128]{3,2,1,0:T(8,128)S(1)} %get-tuple-element.64), channel_id=1, source_target_pairs={{0,16},{16,32},{32,48},{48,64},{64,80},{80,96},{96,112},{1,17},{17... | collective-permute-start | bytes 98312 | tf_op jit(solution)/shard_map/ppermute | solution.py:22
  4.9 354.2 %collective-permute-start = (f32[2,4,8,128]{3,2,1,0:T(8,128)S(1)}, f32[2,4,8,128]{3,2,1,0:T(8,128)S(1)}, u32[]{:S(2)}, u32[]{:S(2)}) collective-permute-start(f32[2,4,8,128]{3,2,1,0:T(8,128)S(1)} %get-tuple-element.65), channel_id=1, source_target_pairs={{16,0},{32,16},{48,32},{64,48},{80,64},{96,80},{112,96},{17,1},{33... | collective-permute-start | bytes 98312 | tf_op jit(solution)/shard_map/ppermute | solution.py:23
  350.4 8.8 %copy-start.2 = (f32[32,8,128]{2,1,0:T(8,128)S(1)}, f32[32,8,128]{2,1,0:T(8,128)}, u32[]{:S(2)}) copy-start(f32[32,8,128]{2,1,0:T(8,128)} %param.18) | copy-start | bytes 393220
  350.4 8.7 %copy-start.3 = (f32[32,8,128]{2,1,0:T(8,128)S(1)}, f32[32,8,128]{2,1,0:T(8,128)}, u32[]{:S(2)}) copy-start(f32[32,8,128]{2,1,0:T(8,128)} %param.16) | copy-start | bytes 393220
  359.1 6.6 copy-start.11
  359.2 15.3 %collective-permute-start.3 = (f32[2,40,4,128]{3,2,1,0:T(4,128)S(1)}, f32[2,40,4,128]{3,2,1,0:T(4,128)S(1)}, u32[]{:S(2)}, u32[]{:S(2)}) collective-permute-start(f32[2,40,4,128]{3,2,1,0:T(4,128)S(1)} %get-tuple-element.50), channel_id=1, source_target_pairs={{0,1},{1,2},{2,3},{3,4},{4,5},{5,6},{6,7},{7,8},{8,9},{9,10},{10,1... | collective-permute-start | bytes 491528 | tf_op jit(solution)/shard_map/ppermute | solution.py:22
  361.5 12.9 %collective-permute-start.2 = (f32[2,40,4,128]{3,2,1,0:T(4,128)S(1)}, f32[2,40,4,128]{3,2,1,0:T(4,128)S(1)}, u32[]{:S(2)}, u32[]{:S(2)}) collective-permute-start(f32[2,40,4,128]{3,2,1,0:T(4,128)S(1)} %get-tuple-element.51), channel_id=1, source_target_pairs={{1,0},{2,1},{3,2},{4,3},{5,4},{6,5},{7,6},{8,7},{9,8},{10,9},{11,1... | collective-permute-start | bytes 491528 | tf_op jit(solution)/shard_map/ppermute | solution.py:23
  376.4 175.1 %copy-start.13 = (f32[2]{0:T(128)S(1)}, f32[2]{0:T(128)}, u32[]{:S(2)}) copy-start(f32[2]{0:T(128)} %param.22) | copy-start | bytes 28
  553.2 13.6 %collective-permute-start.5 = (f32[2,4,8,128]{3,2,1,0:T(8,128)S(1)}, f32[2,4,8,128]{3,2,1,0:T(8,128)S(1)}, u32[]{:S(2)}, u32[]{:S(2)}) collective-permute-start(f32[2,4,8,128]{3,2,1,0:T(8,128)S(1)} %get-tuple-element.60), channel_id=1, source_target_pairs={{0,16},{16,32},{32,48},{48,64},{64,80},{80,96},{96,112},{1,17},{17... | collective-permute-start | bytes 98312 | tf_op jit(solution)/shard_map/ppermute | solution.py:22
  557.0 9.9 %collective-permute-start.4 = (f32[2,4,8,128]{3,2,1,0:T(8,128)S(1)}, f32[2,4,8,128]{3,2,1,0:T(8,128)S(1)}, u32[]{:S(2)}, u32[]{:S(2)}) collective-permute-start(f32[2,4,8,128]{3,2,1,0:T(8,128)S(1)} %get-tuple-element.61), channel_id=1, source_target_pairs={{16,0},{32,16},{48,32},{64,48},{80,64},{96,80},{112,96},{17,1},{33... | collective-permute-start | bytes 98312 | tf_op jit(solution)/shard_map/ppermute | solution.py:23
  560.1 13.6 %collective-permute-start.8 = (f32[2,16,8,128]{3,2,1,0:T(8,128)S(1)}, f32[2,16,8,128]{3,2,1,0:T(8,128)S(1)}, u32[]{:S(2)}, u32[]{:S(2)}) collective-permute-start(f32[2,16,8,128]{3,2,1,0:T(8,128)S(1)} %get-tuple-element.54), channel_id=1, source_target_pairs={{0,16},{16,32},{32,48},{48,64},{64,80},{80,96},{96,112},{1,17},{17... | collective-permute-start | bytes 393224 | tf_op jit(solution)/shard_map/ppermute | solution.py:22
  564.7 9.2 %collective-permute-start.9 = (f32[2,16,8,128]{3,2,1,0:T(8,128)S(1)}, f32[2,16,8,128]{3,2,1,0:T(8,128)S(1)}, u32[]{:S(2)}, u32[]{:S(2)}) collective-permute-start(f32[2,16,8,128]{3,2,1,0:T(8,128)S(1)} %get-tuple-element.55), channel_id=1, source_target_pairs={{16,0},{32,16},{48,32},{64,48},{80,64},{96,80},{112,96},{17,1},{33... | collective-permute-start | bytes 393224 | tf_op jit(solution)/shard_map/ppermute | solution.py:23
  567.0 10.8 %collective-permute-start.7 = (f32[2,40,4,128]{3,2,1,0:T(4,128)S(1)}, f32[2,40,4,128]{3,2,1,0:T(4,128)S(1)}, u32[]{:S(2)}, u32[]{:S(2)}) collective-permute-start(f32[2,40,4,128]{3,2,1,0:T(4,128)S(1)} %get-tuple-element.46), channel_id=1, source_target_pairs={{0,1},{1,2},{2,3},{3,4},{4,5},{5,6},{6,7},{7,8},{8,9},{9,10},{10,1... | collective-permute-start | bytes 491528 | tf_op jit(solution)/shard_map/ppermute | solution.py:22
  571.7 6.6 collective-permute-start.6
  581.4 175.1 %copy-start.4 = (f32[32,8]{1,0:T(8,128)S(1)}, f32[32,8]{1,0:T(8,128)}, u32[]{:S(2)}) copy-start(f32[32,8]{1,0:T(8,128)} %copy.77) | copy-start | bytes 3076
  581.4 175.1 %copy-start.5 = (f32[32,8]{1,0:T(8,128)S(1)}, f32[32,8]{1,0:T(8,128)}, u32[]{:S(2)}) copy-start(f32[32,8]{1,0:T(8,128)} %copy.80) | copy-start | bytes 3076
  581.4 175.1 %copy-start.6 = (f32[32,8]{1,0:T(8,128)S(1)}, f32[32,8]{1,0:T(8,128)}, u32[]{:S(2)}) copy-start(f32[32,8]{1,0:T(8,128)} %copy.79) | copy-start | bytes 3076
  581.4 175.2 %copy-start.7 = (f32[32,8]{1,0:T(8,128)S(1)}, f32[32,8]{1,0:T(8,128)}, u32[]{:S(2)}) copy-start(f32[32,8]{1,0:T(8,128)} %copy.78) | copy-start | bytes 3076
  756.6 17.2 %copy-start = (f32[32768]{0:T(1024)}, f32[32768]{0:T(1024)S(1)}, u32[]{:S(2)}) copy-start(f32[32768]{0:T(1024)S(1)} %scatter_fusion.1) | copy-start | bytes 393220
  756.9 7.9 collective-permute-start.10
  762.1 8.1 %collective-permute-start.11 = (f32[2,16,8,128]{3,2,1,0:T(8,128)S(1)}, f32[2,16,8,128]{3,2,1,0:T(8,128)S(1)}, u32[]{:S(2)}, u32[]{:S(2)}) collective-permute-start(f32[2,16,8,128]{3,2,1,0:T(8,128)S(1)} %get-tuple-element.53), channel_id=1, source_target_pairs={{16,0},{32,16},{48,32},{64,48},{80,64},{96,80},{112,96},{17,1},{33... | collective-permute-start | bytes 393224 | tf_op jit(solution)/shard_map/ppermute | solution.py:23
  787.7 14.7 %all-to-all-start = ((f32[16,1,1024]{2,1,0:T(1,128)}), f32[16,1,1024]{2,1,0:T(1,128)S(1)}, u32[]{:S(2)}, u32[]{:S(2)}) async-start(f32[16,1,1024]{2,1,0:T(1,128)} %reshape.1554), calls=%async_computation | async-start | bytes 131072 | tf_op jit(solution)/shard_map/all_to_all | solution.py:162
  (4 other events, 7.5 us)
where the time goes:
time: 806 us; the launch traced here: 805 us
  other arithmetic  371 us (46%)
  local copies, waits for them, and re-layouts  289 us (36%)
  blocking collectives  70.6 us (9%)
  starting transfers between devices  47.6 us (6%)
  matrix products  12 us (1%)
  waiting for transfers between devices  11.6 us (1%)
    scatter-add x2, other arithmetic, body(): receiver_new = receiver_new.reshape(-1).at[receiver_local].add(receiver_s...  350 us
    gather x1, local copies, waits for them, and re-layouts, body(): receiver_scale = courant_flat[jnp.minimum(receiver_local, total_cells - 1)]  181 us
    all_gather x1, blocking collectives, body(): lax.all_gather(receiver_cells, ('gx', 'gy'), axis=0, tiled=True)  37.4 us
    all_gather x1, blocking collectives, body(): lax.all_gather(receiver_traces, ('gx', 'gy'), axis=1, tiled=True)  33.2 us
    ppermute x6, starting transfers between devices, padded_2(): before = lax.ppermute(last, axis, up)  24.1 us
    eq x4, local copies, waits for them, and re-layouts, slant_table(): low_hit = rows == lower_index[:, None, :, :]  22.2 us
    broadcast_in_dim x2, local copies, waits for them, and re-layouts, slant_table(): jnp.where(low_hit, (1.0 - frac)[:, None, :, :], zero)  22.1 us
    broadcast_in_dim x2, local copies, waits for them, and re-layouts, slant_table(): jnp.where(high_hit, frac[:, None, :, :], zero)  22.1 us
  transfers between devices with their start and end apart: 13, of which 5 were waited for; matrix products, arithmetic and copies ran while one was open for 37% of the time, Pallas kernels for 0%

commit v1 on v0

v1 whole, which is shorter than its diff:
```python
import math

import jax
import jax.numpy as jnp
import numpy as np
from jax import lax
from jax.experimental import pallas as pl
from jax.experimental.pallas import tpu as pltpu
from jax.sharding import PartitionSpec as P

COEFS = (-205.0 / 72.0, 8.0 / 5.0, -1.0 / 5.0, 8.0 / 315.0, -1.0 / 560.0)
SLOPES = np.array(
    [math.tan(math.pi * (-60.0 + 120.0 * (angle + 0.5) / 32.0) / 180.0) for angle in range(32)],
    dtype=np.float32,
)
GX, GY = 8, 16
TX, TY, TZ = 32, 8, 128
DEVICES = GX * GY
RECEIVERS = 256
SLOTS = 16
F32, BF16, I32 = jnp.float32, jnp.bfloat16, jnp.int32
VMEM_LIMIT = 24 * 1024 * 1024


def iota(shape, dim):
    return lax.broadcasted_iota(I32, shape, dim)


def halves(value):
    high = value.astype(BF16)
    return high, (value - high.astype(F32)).astype(BF16)


def dot_nt(left, right):
    return lax.dot_general(left, right, (((1,), (1,)), ((), ())), preferred_element_type=F32)


def routed(cells, traces, first_slot):
    x, y, z = cells >> 14, (cells >> 7) & 127, cells & 127
    tile_x, tile_y, in_x, in_y = x >> 5, y >> 3, x & 31, y & 7
    beside_y = jnp.where(in_y < 4, tile_y - 1, tile_y + 1)
    beside_x = jnp.where(in_x < 4, tile_x - 1, jnp.where(in_x >= 28, tile_x + 1, -1))
    to_y = jnp.where((beside_y >= 0) & (beside_y < GY), tile_x * GY + beside_y, -1)
    to_x = jnp.where((beside_x >= 0) & (beside_x < GX), beside_x * GY + tile_y, -1)
    rim_x = jnp.where(in_x < 4, in_x + 4, in_x - 28)
    classes = (
        (tile_x * GY + tile_y, (in_x * 8 + in_y) * 128 + z, 2),
        (to_y, (in_x * 8 + (in_y ^ 4)) * 128 + z, 1),
        (to_x, (rim_x * 8 + in_y) * 128 + z, 1),
    )
    earlier = jnp.where(
        iota((RECEIVERS, RECEIVERS), 0) < iota((RECEIVERS, RECEIVERS), 1), 1.0, 0.0
    ).astype(BF16)
    device = iota((DEVICES, RECEIVERS), 0)
    slot = iota((SLOTS, RECEIVERS), 0).astype(F32) + first_slot.astype(F32)
    hits, kept, last_rank, row = [], [], None, 0
    for target, place, steps in classes:
        hit = jnp.where(device == target, 1.0, 0.0)
        before = jnp.dot(hit.astype(BF16), earlier, preferred_element_type=F32)
        rank = jnp.sum(hit * before, axis=0, keepdims=True)
        last_rank = rank if last_rank is None else jnp.maximum(last_rank, rank)
        mine = slot == rank
        rows = [jnp.where(mine, place.astype(F32), 0.0)]
        rows += [jnp.where(mine, traces[s : s + 1], 0.0) for s in range(steps)]
        size = SLOTS * len(rows)
        above = [jnp.zeros((row, RECEIVERS), F32)] if row else []
        below = [jnp.zeros((128 - row - size, RECEIVERS), F32)]
        kept.append(jnp.concatenate(above + rows + below, axis=0))
        hits.append(hit.astype(BF16))
        row += size
    hits = jnp.concatenate(hits, axis=1)
    high, low = halves(jnp.concatenate(kept, axis=1))
    sent = dot_nt(hits, high) + dot_nt(hits, low)
    rounds = (jnp.max(last_rank, axis=1, keepdims=True).astype(I32) // SLOTS + 1).astype(F32)
    return jnp.where(iota((DEVICES, 128), 1) >= row, rounds, sent)


def route_kernel(first_ref, cells_ref, traces_ref, sent_ref):
    sent_ref[:, 0, :] = routed(cells_ref[...], traces_ref[...], first_ref[0])


def collected(got):
    rows = got.T
    sums, row = [], 0
    for columns, steps in ((TX * 8, 2), (TX * 8, 1), (64, 1)):
        cell = rows[row : row + SLOTS].astype(I32)
        column, depth = cell >> 7, cell & 127
        at = iota((columns, DEVICES), 0)
        down = iota((TZ, DEVICES), 0)
        one, parts = [], [[] for _ in range(2 * steps)]
        for k in range(SLOTS):
            one.append(jnp.where(at == column[k : k + 1], 1.0, 0.0).astype(BF16))
            same = down == depth[k : k + 1]
            for s in range(steps):
                value = rows[row + (s + 1) * SLOTS + k : row + (s + 1) * SLOTS + k + 1]
                high = value.astype(BF16).astype(F32)
                parts[2 * s].append(jnp.where(same, high, 0.0).astype(BF16))
                parts[2 * s + 1].append(jnp.where(same, value - high, 0.0).astype(BF16))
        one = jnp.concatenate(one, axis=1)
        for s in range(steps):
            high = jnp.concatenate(parts[2 * s], axis=1)
            low = jnp.concatenate(parts[2 * s + 1], axis=1)
            sums.append(dot_nt(one, high) + dot_nt(one, low))
        row += SLOTS * (steps + 1)
    return sums


def collect_kernel(got_ref, own_ref, rim_y_ref, rim_x_ref, rounds_ref):
    got = got_ref[:, 0, :]
    own_0, own_1, rim_y, rim_x = collected(got)
    own_ref[0] = own_0.reshape(TX, 8, 128)
    own_ref[1] = own_1.reshape(TX, 8, 128)
    rim_y_ref[...] = rim_y.reshape(TX, 8, 128)
    rim_x_ref[...] = rim_x.reshape(8, 8, 128)
    rounds_ref[0] = jnp.max(got[:, 112:128]).astype(I32)


def collect_more_kernel(got_ref, own_in, rim_y_in, rim_x_in, own_ref, rim_y_ref, rim_x_ref):
    own_0, own_1, rim_y, rim_x = collected(got_ref[:, 0, :])
    own_ref[0] = own_in[0] + own_0.reshape(TX, 8, 128)
    own_ref[1] = own_in[1] + own_1.reshape(TX, 8, 128)
    rim_y_ref[...] = rim_y_in[...] + rim_y.reshape(TX, 8, 128)
    rim_x_ref[...] = rim_x_in[...] + rim_x.reshape(8, 8, 128)


def strip_values_tile(values, step, rows):
    return jnp.concatenate([values[step, layer][rows] for layer in range(4)], axis=1)


def wide(depth):
    return jnp.concatenate([depth, jnp.zeros((depth.shape[0], 96), depth.dtype)], axis=1)


def pack_y_kernel(
    cells_ref, traces_ref, s0, r0, sm, rm, c, depth, values, sent_ref, up_ref, down_ref
):
    for ref, rows in ((up_ref, slice(4, 8)), (down_ref, slice(0, 4))):
        ref[0:32] = s0[...]
        ref[32:64] = r0[...]
        ref[64:96, 0:4] = sm[:, rows]
        ref[64:96, 4:8] = rm[:, rows]
        ref[96:112, 0:4] = c[0:16, rows]
        ref[96:112, 4:8] = c[16:32, rows]
        ref[112, 0:4] = strip_values_tile(values, 0, rows)
        ref[112, 4:8] = wide(depth[rows].astype(F32))
    sent_ref[:, 0, :] = routed(cells_ref[...], traces_ref[...], jnp.int32(0))


def pack_x_kernel(
    place, s0, r0, sm, rm, c, depth, values, before, after, up_ref, down_ref
):
    keep_before = jnp.where(place[1] > 0, 1.0, 0.0)
    keep_after = jnp.where(place[1] < GY - 1, 1.0, 0.0)
    near = strip_values_tile(values, 0, slice(0, 8))
    depths = wide(depth[...].astype(F32))
    for ref, deep, rim in ((up_ref, 24, 28), (down_ref, 0, 0)):
        for f, field in ((0, s0), (1, r0)):
            ref[8 * f : 8 * f + 8] = field[deep : deep + 8]
            start = 16 + 4 * f
            ref[start : start + 4, 0:4] = before[32 * f + rim : 32 * f + rim + 4, 4:8] * keep_before
            ref[start : start + 4, 4:8] = after[32 * f + rim : 32 * f + rim + 4, 0:4] * keep_after
        ref[24:28] = sm[rim : rim + 4]
        ref[28:32] = rm[rim : rim + 4]
        ref[32:36] = c[rim : rim + 4]
        ref[36] = near
        ref[37] = depths


def depth_pairs(tile, reach):
    lane = iota((8, 128), 1)
    below = jnp.where(lane < 128 - reach, pltpu.roll(tile, 128 - reach, 1), 0.0)
    above = jnp.where(lane >= reach, pltpu.roll(tile, reach, 1), 0.0)
    return below + above


def curvature(ref, f, x, row):
    tile = ref[f, x, row : row + 8]
    total = (3.0 * COEFS[0]) * tile
    for reach in range(1, 5):
        pairs = ref[f, x + reach, row : row + 8] + ref[f, x - reach, row : row + 8]
        pairs = pairs + ref[f, x, row + reach : row + reach + 8]
        pairs = pairs + ref[f, x, row - reach : row - reach + 8]
        pairs = pairs + depth_pairs(tile, reach)
        total = total + COEFS[reach] * pairs
    return tile, total


def overwritten(tile, depths, values, lane_start):
    lane = iota((8, 128), 1)
    column = jnp.full((8, 128), lane_start, I32)
    relative = lane - jnp.take_along_axis(depths, column, axis=1)
    fill = jnp.take_along_axis(values, (relative & 3) * 32 + column, axis=1)
    return jnp.where((relative >= 0) & (relative < 4), fill, tile)


def steps_kernel(
    place, source_cell, wavelet,
    s0, r0, sm, rm, c, depth, values, before, after, left, right, own, rim_y, rim_x,
    s_out, r_out, near_ref, up_ref, down_ref,
    e_ref, m_ref, o_ref, d_ref, v_ref, sub_ref,
):
    keep_before = jnp.where(place[1] > 0, 1.0, 0.0)
    keep_after = jnp.where(place[1] < GY - 1, 1.0, 0.0)
    keep_left = jnp.where(place[0] > 0, 1.0, 0.0)
    keep_right = jnp.where(place[0] < GX - 1, 1.0, 0.0)
    for f, field in ((0, s0), (1, r0)):
        e_ref[f, 8:40, 12:20] = field[...]
        e_ref[f, 8:40, 4:12] = before[32 * f : 32 * f + 32] * keep_before
        e_ref[f, 8:40, 20:28] = after[32 * f : 32 * f + 32] * keep_after
        for ref, keep, deep, rim in ((left, keep_left, 0, 4), (right, keep_right, 40, 40)):
            e_ref[f, deep : deep + 8, 12:20] = ref[8 * f : 8 * f + 8] * keep
            corner = 16 + 4 * f
            e_ref[f, rim : rim + 4, 8:12] = ref[corner : corner + 4, 0:4] * keep
            e_ref[f, rim : rim + 4, 20:24] = ref[corner : corner + 4, 4:8] * keep
    for k, field in ((0, sm), (1, rm), (2, c)):
        m_ref[k, 4:36, 4:12] = field[...]
        m_ref[k, 0:4, 4:12] = left[24 + 4 * k : 28 + 4 * k] * keep_left
        m_ref[k, 36:40, 4:12] = right[24 + 4 * k : 28 + 4 * k] * keep_right
    for ref, keep, rows in ((before, keep_before, slice(0, 4)), (after, keep_after, slice(12, 16))):
        m_ref[0, 4:36, rows] = ref[64:96, 0:4] * keep
        m_ref[1, 4:36, rows] = ref[64:96, 4:8] * keep
        m_ref[2, 4:20, rows] = ref[96:112, 0:4] * keep
        m_ref[2, 20:36, rows] = ref[96:112, 4:8] * keep
    m_ref[3, 4:36, 4:12] = own[0]
    m_ref[3, 4:36, 0:4] = rim_y[:, 0:4]
    m_ref[3, 4:36, 12:16] = rim_y[:, 4:8]
    m_ref[3, 0:4, 4:12] = rim_x[0:4]
    m_ref[3, 36:40, 4:12] = rim_x[4:8]
    near_values = strip_values_tile(values, 0, slice(0, 8))
    near_depth = wide(depth[...])
    v_ref[1, 4:12] = near_values
    d_ref[1, 4:12] = near_depth
    for ref, keep, rows in ((before, keep_before, slice(0, 4)), (after, keep_after, slice(12, 16))):
        v_ref[1, rows] = ref[112, 0:4] * keep
        d_ref[1, rows] = (ref[112, 4:8] * keep).astype(I32)
    for k, ref, keep in ((0, left, keep_left), (2, right, keep_right)):
        v_ref[k] = jnp.zeros((16, 128), F32)
        d_ref[k] = jnp.zeros((16, 128), I32)
        v_ref[k, 4:12] = ref[36] * keep
        d_ref[k, 4:12] = (ref[37] * keep).astype(I32)
    cell = source_cell[0]
    source_x = (cell >> 14) - place[0] * TX
    source_y = ((cell >> 7) & 127) - place[1] * TY
    source_z = cell & 127
    lane, sublane = iota((8, 128), 1), iota((8, 128), 0)

    def first(i, carry):
        part = jnp.where(i >= 4, 1, 0) + jnp.where(i >= 36, 1, 0)
        column = jnp.where(i < 4, i + 28, jnp.where(i < 36, i - 4, i - 36))
        amount = jnp.where(i - 4 == source_x, wavelet[0], 0.0)
        for t in range(2):
            rows = slice(8 * t, 8 * t + 8)
            at_source = (lane == source_z) & (sublane + (8 * t - 4) == source_y)
            courant = m_ref[2, i, rows]
            now, total = curvature(e_ref, 0, i + 4, 8 + 8 * t)
            total = total - jnp.where(at_source, amount, 0.0)
            new = 2.0 * now - m_ref[0, i, rows] + courant * total
            new = overwritten(new, d_ref[part, rows], v_ref[part, rows], column)
            o_ref[0, i, 4 + 8 * t : 12 + 8 * t] = new
            sub_ref[0, t, pl.ds(i, 1)] = new[4 - 4 * t : 5 - 4 * t]
            now, total = curvature(e_ref, 1, i + 4, 8 + 8 * t)
            new = 2.0 * now - m_ref[1, i, rows] + courant * (total + m_ref[3, i, rows])
            o_ref[1, i, 4 + 8 * t : 12 + 8 * t] = new
            sub_ref[2, t, pl.ds(i, 1)] = new[4 - 4 * t : 5 - 4 * t]
        return carry

    lax.fori_loop(0, 40, first, 0)
    late_values = strip_values_tile(values, 1, slice(0, 8))
    at_source = (lane == source_z) & (sublane == source_y)

    def second(x, carry):
        amount = jnp.where(x == source_x, wavelet[1], 0.0)
        now, total = curvature(o_ref, 0, x + 4, 8)
        total = total - jnp.where(at_source, amount, 0.0)
        new = 2.0 * now - s0[x] + c[x] * total
        new = overwritten(new, near_depth, late_values, x)
        s_out[x] = new
        for j in range(2):
            sub_ref[1, j, pl.ds(x + 4, 1)] = new[4 * j : 4 * j + 1]
        now, total = curvature(o_ref, 1, x + 4, 8)
        new = 2.0 * now - r0[x] + c[x] * (total + own[1, x])
        r_out[x] = new
        for j in range(2):
            sub_ref[3, j, pl.ds(x + 4, 1)] = new[4 * j : 4 * j + 1]
        return carry

    lax.fori_loop(0, 32, second, 0)
    z, to = iota((TZ, 128), 0), iota((TZ, 128), 1)
    for k in range(4):
        total = None
        for j in range(2):
            pick = jnp.where((z & 3 == 0) & (to == (z >> 2) + (16 + 64 * j)), 1.0, 0.0)
            part = jnp.dot(
                sub_ref[k, j, 4:36], pick, precision=lax.Precision.HIGHEST, preferred_element_type=F32
            )
            total = part if total is None else total + part
        near_ref[k] = total
        up_ref[k] = total[16:32]
        down_ref[k] = total[0:16]


def angles_kernel(place, near, left, right, out_ref, g_ref):
    keep_left = jnp.where(place[0] > 0, 1.0, 0.0)
    keep_right = jnp.where(place[0] < GX - 1, 1.0, 0.0)
    for k in range(4):
        g_ref[k, 0:16] = left[k] * keep_left
        g_ref[k, 16:48] = near[k]
        g_ref[k, 48:64] = right[k] * keep_right
    sums = [None] * 32
    for lag in range(-16, 17):
        product = None
        for step in range(2):
            source = g_ref[step, pl.ds(16 - lag, 8, stride=4)]
            receiver = g_ref[2 + step, pl.ds(16 + lag, 8, stride=4)]
            part = source * receiver
            product = part if product is None else product + part
        shifted = {}

        def shift(amount):
            if amount not in shifted:
                shifted[amount] = product if amount == 0 else pltpu.roll(product, -amount % 128, 1)
            return shifted[amount]

        for a in range(32):
            move = np.float32(lag) * SLOPES[a] / np.float32(4.0)
            low = np.floor(move)
            frac = float(move - low)
            term = shift(int(low)) * (1.0 - frac)
            if frac != 0.0:
                term = term + shift(int(low) + 1) * frac
            sums[a] = term if sums[a] is None else sums[a] + term
    lane = iota((8, 128), 1)
    for b in range(16):
        first, second = sums[2 * b], sums[2 * b + 1]
        packed = jnp.where(lane < 32, pltpu.roll(first, 112, 1), pltpu.roll(first, 80, 1))
        other = jnp.where(lane < 96, pltpu.roll(second, 48, 1), pltpu.roll(second, 16, 1))
        out_ref[b] = jnp.where(lane < 64, packed, other)


def arrange_kernel(got, out_ref):
    lane = iota((8, 128), 1)
    for t in range(8):
        even, odd = got[2 * t], got[2 * t + 1]
        out_ref[0, :, 128 * t : 128 * t + 128] = jnp.where(lane < 64, even, pltpu.roll(odd, 64, 1))
        out_ref[1, :, 128 * t : 128 * t + 128] = jnp.where(lane < 64, pltpu.roll(even, 64, 1), odd)


def call(kernel, outs, scalars, arrays, out_scalars=0, scratch=(), cost=None):
    smem, vmem = pl.BlockSpec(memory_space=pltpu.SMEM), pl.BlockSpec(memory_space=pltpu.VMEM)
    return pl.pallas_call(
        kernel,
        out_shape=[jax.ShapeDtypeStruct(shape, kind) for shape, kind in outs],
        in_specs=[smem] * len(scalars) + [vmem] * len(arrays),
        out_specs=[vmem] * (len(outs) - out_scalars) + [smem] * out_scalars,
        scratch_shapes=list(scratch),
        compiler_params=pltpu.CompilerParams(vmem_limit_bytes=VMEM_LIMIT),
        cost_estimate=cost,
    )(*scalars, *arrays)


def both_ways(to_next, to_last, axis):
    size = lax.axis_size(axis)
    from_last = lax.ppermute(to_next, axis, [(i, (i + 1) % size) for i in range(size)])
    from_next = lax.ppermute(to_last, axis, [((i + 1) % size, i) for i in range(size)])
    return from_last, from_next


def body(
    source_now,
    source_next,
    receiver_now,
    receiver_next,
    courant,
    source_cell,
    wavelet,
    receiver_cells,
    receiver_traces,
    strip_depth,
    strip_values,
):
    place = jnp.stack([lax.axis_index("gx"), lax.axis_index("gy")]).astype(I32)
    cells = receiver_cells.reshape(1, RECEIVERS)
    tile = (TX, TY, TZ)
    fields = (source_now, receiver_now, source_next, receiver_next, courant, strip_depth, strip_values)
    sent, up_y, down_y = call(
        pack_y_kernel,
        [((DEVICES, 1, 128), F32), ((113, 8, 128), F32), ((113, 8, 128), F32)],
        [], [cells, receiver_traces, *fields],
    )
    before, after = both_ways(up_y, down_y, "gy")
    got = lax.all_to_all(sent, ("gx", "gy"), 0, 0, tiled=True)
    up_x, down_x = call(
        pack_x_kernel, [((38, 8, 128), F32)] * 2, [place], [*fields, before, after]
    )
    left, right = both_ways(up_x, down_x, "gx")
    sums = [((2, *tile), F32), (tile, F32), ((8, 8, 128), F32)]
    own, rim_y, rim_x, rounds = call(
        collect_kernel, [*sums, ((1,), I32)], [], [got], out_scalars=1
    )

    def another(state):
        turn, *partial = state
        (more,) = call(
            route_kernel,
            [((DEVICES, 1, 128), F32)],
            [(turn * SLOTS).reshape(1)], [cells, receiver_traces],
        )
        more = lax.all_to_all(more, ("gx", "gy"), 0, 0, tiled=True)
        return (turn + 1, *call(collect_more_kernel, sums, [], [more, *partial]))

    _, own, rim_y, rim_x = lax.while_loop(
        lambda state: state[0] < rounds[0], another, (jnp.int32(1), own, rim_y, rim_x)
    )
    source_field, receiver_field, near, up, down = call(
        steps_kernel,
        [(tile, F32), (tile, F32), ((4, 32, 128), F32), ((4, 16, 128), F32), ((4, 16, 128), F32)],
        [place, source_cell, wavelet],
        [*fields, before, after, left, right, own, rim_y, rim_x],
        scratch=[
            pltpu.VMEM((2, 48, 32, 128), F32),
            pltpu.VMEM((4, 40, 16, 128), F32),
            pltpu.VMEM((2, 40, 24, 128), F32),
            pltpu.VMEM((3, 16, 128), I32),
            pltpu.VMEM((3, 16, 128), F32),
            pltpu.VMEM((4, 2, 40, 128), F32),
        ],
    )
    near_left, near_right = both_ways(up, down, "gx")
    (angles,) = call(
        angles_kernel, [((16, 8, 128), F32)], [place], [near, near_left, near_right],
        scratch=[pltpu.VMEM((4, 64, 128), F32)],
    )
    angles = lax.all_to_all(angles, "gy", 0, 0, tiled=True)
    (image,) = call(arrange_kernel, [((2, 8, 1024), F32)], [], [angles])
    return source_field, receiver_field, image


def solution(mesh):
    return jax.shard_map(
        body,
        mesh=mesh,
        in_specs=(
            P("gx", "gy", None),
            P("gx", "gy", None),
            P("gx", "gy", None),
            P("gx", "gy", None),
            P("gx", "gy", None),
            P(),
            P(),
            P(("gx", "gy")),
            P(None, ("gx", "gy")),
            P("gy", "gx"),
            P(None, None, "gy", "gx"),
        ),
        out_specs=(P("gx", "gy", None), P("gx", "gy", None), P("gy", "gx", None)),
        check_vma=False,
    )
```

time: 806 us -> 80.5 us (0.10)
  other arithmetic: 371 us -> 0.07 us
  local copies, waits for them, and re-layouts: 289 us -> 7.99 us
  blocking collectives: 70.6 us -> 11.2 us
  starting transfers between devices: 47.6 us -> 19 us
  Pallas kernels: 0 us -> 19.6 us
  matrix products: 12 us -> 0 us
    scatter-add x4 -> x0, other arithmetic: 353 us -> none  [the longest x2 350 us: body(): receiver_new = receiver_new.reshape(-1).at[receiver_local].add(receiver_s...]
    gather x1 -> x0, local copies, waits for them, and re-layouts: 181 us -> none  [body(): receiver_scale = courant_flat[jnp.minimum(receiver_local, total_cells - 1)]]
    all_gather x2 -> x0, blocking collectives: 70.6 us -> none  [the longest x1 37.4 us: body(): lax.all_gather(receiver_cells, ('gx', 'gy'), axis=0, tiled=True)]
    eq x6 -> x0, local copies, waits for them, and re-layouts: 44.3 us -> none  [the longest x4 22.2 us: slant_table(): low_hit = rows == lower_index[:, None, :, :]]
    broadcast_in_dim x4 -> x0, local copies, waits for them, and re-layouts: 44.3 us -> none  [the longest x2 22.1 us: slant_table(): jnp.where(low_hit, (1.0 - frac)[:, None, :, :], zero)]
    ppermute x12 -> x6, starting transfers between devices: 38.8 us -> 7.83 us  [the longest x3 5.27 us: both_ways(): lax.ppermute(to_next, axis, [(i, (i + 1) % size) for i in range(size)])]
    pallas_call x0 -> x6, Pallas kernels: none -> 19.6 us  [call(): pl.pallas_call(kernel, out_shape=[jax.ShapeDtypeStruct(shape, kind) for s...]
    dot_general x1 -> x0, matrix products: 12 us -> none  [body(): jnp.dot(lag_image.reshape(points_x * points_y, 33 * depth_points), table,...]
  transfers between devices with their start and end apart: 13 -> 7, of which waited for: 5 -> 5; matrix products, arithmetic and copies ran while one was open for 37% -> 0% of each run, Pallas kernels for 0% -> 3%
where the time goes in v1:
time: 80.5 us; the launch traced here: 79.2 us
  Pallas kernels  19.6 us (24%)
  waiting for transfers between devices  19.2 us (24%)
  starting transfers between devices  19 us (24%)
  blocking collectives  11.2 us (14%)
  local copies, waits for them, and re-layouts  7.99 us (10%)
  between operations  1.43 us (2%)
    pallas_call x6, Pallas kernels, call(): pl.pallas_call(kernel, out_shape=[jax.ShapeDtypeStruct(shape, kind) for s...  19.6 us
    all_to_all x1, blocking collectives, body(): angles = lax.all_to_all(angles, 'gy', 0, 0, tiled=True)  11.2 us
    all_to_all x1, starting transfers between devices, body(): got = lax.all_to_all(sent, ('gx', 'gy'), 0, 0, tiled=True)  11.2 us
    unnamed x34, local copies, waits for them, and re-layouts  7.99 us
    all_to_all x1, waiting for transfers between devices, body(): got = lax.all_to_all(sent, ('gx', 'gy'), 0, 0, tiled=True)  7.07 us
    ppermute x3, waiting for transfers between devices, both_ways(): lax.ppermute(to_next, axis, [(i, (i + 1) % size) for i in range(size)])  6.69 us
    ppermute x3, waiting for transfers between devices, both_ways(): lax.ppermute(to_last, axis, [((i + 1) % size, i) for i in range(size)])  5.47 us
    ppermute x3, starting transfers between devices, both_ways(): lax.ppermute(to_next, axis, [(i, (i + 1) % size) for i in range(size)])  5.27 us
  transfers between devices with their start and end apart: 7, of which 5 were waited for; matrix products, arithmetic and copies ran while one was open for 0% of the time, Pallas kernels for 3%

profile of v1, /device:TPU:5, one launch (start us, length us, event | category | flops | bytes accessed | tf_op | source)
XLA Modules:
  0.0 79.2 jit_solution(16915276276932667555)
XLA Ops:
  1.3 0.9 %copy-done = f32[32,8,128]{2,1,0:T(8,128)S(1)} copy-done((f32[32,8,128]{2,1,0:T(8,128)S(1)}, f32[32,8,128]{2,1,0:T(8,128)}, u32[]{:S(2)}) %copy-start) | copy-done | bytes 131096
  2.2 0.9 %copy-done.2 = f32[32,8,128]{2,1,0:T(8,128)S(1)} copy-done((f32[32,8,128]{2,1,0:T(8,128)S(1)}, f32[32,8,128]{2,1,0:T(8,128)}, u32[]{:S(2)}) %copy-start.2) | copy-done | bytes 131096
  3.1 0.9 %copy-done.4 = f32[32,8,128]{2,1,0:T(8,128)S(1)} copy-done((f32[32,8,128]{2,1,0:T(8,128)S(1)}, f32[32,8,128]{2,1,0:T(8,128)}, u32[]{:S(2)}) %copy-start.4) | copy-done | bytes 131096
  4.0 0.9 %copy-done.6 = f32[32,8,128]{2,1,0:T(8,128)S(1)} copy-done((f32[32,8,128]{2,1,0:T(8,128)S(1)}, f32[32,8,128]{2,1,0:T(8,128)}, u32[]{:S(2)}) %copy-start.6) | copy-done | bytes 131096
  4.9 0.9 %copy-done.8 = f32[32,8,128]{2,1,0:T(8,128)S(1)} copy-done((f32[32,8,128]{2,1,0:T(8,128)S(1)}, f32[32,8,128]{2,1,0:T(8,128)}, u32[]{:S(2)}) %copy-start.8) | copy-done | bytes 131096
  5.8 0.8 copy-done.10
  6.6 0.7 copy-done.12
  7.3 2.0 %shard_map.130 = (f32[128,1,128]{2,1,0:T(1,128)}, f32[113,8,128]{2,1,0:T(8,128)S(1)}, f32[113,8,128]{2,1,0:T(8,128)S(1)}) custom-call(s32[1,256]{1,0:T(1,128)S(1)} %bitcast.8, f32[2,256]{1,0:T(2,128)} %traces_ref.1, f32[32,8,128]{2,1,0:T(8,128)S(1)} %copy-done, f32[32,8,128]{2,1,0:T(8,128)S(1)} %copy-done.2, f32[32,8,128]{2,1,0:T(8,128)S(1)} %copy-done.4, ...), custom_call_target="tpu_custom_call" | custom-call | tf_op jit(solution)/shard_map/pallas_call | solution.py:350
  9.3 1.9 %collective-permute-start = (f32[113,8,128]{2,1,0:T(8,128)S(1)}, f32[113,8,128]{2,1,0:T(8,128)S(1)}, u32[]{:S(2)}, u32[]{:S(2)}) collective-permute-start(f32[113,8,128]{2,1,0:T(8,128)S(1)} %get-tuple-element.60), channel_id=1, source_target_pairs={{0,1},{1,2},{2,3},{3,4},{4,5},{5,6},{6,7},{7,8},{8,9},{9,10},{10,1... | collective-permute-start | bytes 1388552 | tf_op jit(solution)/shard_map/ppermute | solution.py:363
  11.2 5.4 %collective-permute-done.before = f32[113,8,128]{2,1,0:T(8,128)S(1)} collective-permute-done((f32[113,8,128]{2,1,0:T(8,128)S(1)}, f32[113,8,128]{2,1,0:T(8,128)S(1)}, u32[]{:S(2)}, u32[]{:S(2)}) %collective-permute-start) | collective-permute-done | bytes 462880 | tf_op jit(solution)/shard_map/ppermute | solution.py:363
  16.6 2.8 %collective-permute-done.1.after = f32[113,8,128]{2,1,0:T(8,128)S(1)} collective-permute-done((f32[113,8,128]{2,1,0:T(8,128)S(1)}, f32[113,8,128]{2,1,0:T(8,128)S(1)}, u32[]{:S(2)}, u32[]{:S(2)}) %collective-permute-start.1) | collective-permute-done | bytes 462880 | tf_op jit(solution)/shard_map/ppermute | solution.py:364
  20.1 1.6 %collective-permute-start.2 = (f32[38,8,128]{2,1,0:T(8,128)S(1)}, f32[38,8,128]{2,1,0:T(8,128)S(1)}, u32[]{:S(2)}, u32[]{:S(2)}) collective-permute-start(f32[38,8,128]{2,1,0:T(8,128)S(1)} %get-tuple-element.62), channel_id=1, source_target_pairs={{0,16},{16,32},{32,48},{48,64},{64,80},{80,96},{96,112},{112,0},{1... | collective-permute-start | bytes 466952 | tf_op jit(solution)/shard_map/ppermute | solution.py:363
  21.7 1.4 %collective-permute-start.3 = (f32[38,8,128]{2,1,0:T(8,128)S(1)}, f32[38,8,128]{2,1,0:T(8,128)S(1)}, u32[]{:S(2)}, u32[]{:S(2)}) collective-permute-start(f32[38,8,128]{2,1,0:T(8,128)S(1)} %get-tuple-element.63), channel_id=1, source_target_pairs={{16,0},{32,16},{48,32},{64,48},{80,64},{96,80},{112,96},{0,112},{1... | collective-permute-start | bytes 466952 | tf_op jit(solution)/shard_map/ppermute | solution.py:364
  23.1 11.2 %all-to-all-start.1 = ((f32[128,1,128]{2,1,0:T(1,128)}), f32[128,1,128]{2,1,0:T(1,128)S(1)}, u32[]{:S(2)}, u32[]{:S(2)}) async-start(f32[128,1,128]{2,1,0:T(1,128)} %get-tuple-element.64), calls=%async_computation.1 | async-start | bytes 131072 | tf_op jit(solution)/shard_map/all_to_all | solution.py:391
  34.9 7.1 %all-to-all-done.1.got_ref = f32[128,1,128]{2,1,0:T(1,128)S(1)} async-done(((f32[128,1,128]{2,1,0:T(1,128)}), f32[128,1,128]{2,1,0:T(1,128)S(1)}, u32[]{:S(2)}, u32[]{:S(2)}) %all-to-all-start.1) | async-done | bytes 65568 | tf_op jit(solution)/shard_map/all_to_all | solution.py:391
  42.0 2.7 %shard_map.132 = (f32[2,32,8,128]{3,2,1,0:T(8,128)S(1)}, f32[32,8,128]{2,1,0:T(8,128)S(1)}, f32[8,8,128]{2,1,0:T(8,128)S(1)}, s32[1]{0:T(128)}) custom-call(f32[128,1,128]{2,1,0:T(1,128)S(1)} %all-to-all-done.1.got_ref), custom_call_target="tpu_custom_call" | custom-call | tf_op jit(solution)/shard_map/pallas_call | solution.py:350
  46.7 12.3 %shard_map.133 = (f32[32,8,128]{2,1,0:T(8,128)}, f32[32,8,128]{2,1,0:T(8,128)}, f32[4,32,128]{2,1,0:T(8,128)S(1)}, f32[4,16,128]{2,1,0:T(8,128)S(1)}, f32[4,16,128]{2,1,0:T(8,128)S(1)}) custom-call(s32[2]{0:T(128)S(1)} %pad_add_fusion.place, s32[1]{0:T(128)S(6)} %copy.29.source_cell, f32[2]{0:T(128)S(1)} %copy-done.14, f32[32,8,128]{2,1,0:T(8,128)S(1)} %copy-done.1, ...), custom_call_target="tpu_custom_call" | custom-call | tf_op jit(solution)/shard_map/pallas_call | solution.py:350
  59.0 1.8 %collective-permute-start.4 = (f32[4,16,128]{2,1,0:T(8,128)S(1)}, f32[4,16,128]{2,1,0:T(8,128)S(1)}, u32[]{:S(2)}, u32[]{:S(2)}) collective-permute-start(f32[4,16,128]{2,1,0:T(8,128)S(1)} %get-tuple-element.75), channel_id=1, source_target_pairs={{0,16},{16,32},{32,48},{48,64},{64,80},{80,96},{96,112},{112,0},{1... | collective-permute-start | bytes 98312 | tf_op jit(solution)/shard_map/ppermute | solution.py:363
  60.8 1.2 %collective-permute-start.5 = (f32[4,16,128]{2,1,0:T(8,128)S(1)}, f32[4,16,128]{2,1,0:T(8,128)S(1)}, u32[]{:S(2)}, u32[]{:S(2)}) collective-permute-start(f32[4,16,128]{2,1,0:T(8,128)S(1)} %get-tuple-element.76), channel_id=1, source_target_pairs={{16,0},{32,16},{48,32},{64,48},{80,64},{96,80},{112,96},{0,112},{1... | collective-permute-start | bytes 98312 | tf_op jit(solution)/shard_map/ppermute | solution.py:364
  62.0 1.3 %collective-permute-done.4.left = f32[4,16,128]{2,1,0:T(8,128)S(1)} collective-permute-done((f32[4,16,128]{2,1,0:T(8,128)S(1)}, f32[4,16,128]{2,1,0:T(8,128)S(1)}, u32[]{:S(2)}, u32[]{:S(2)}) %collective-permute-start.4) | collective-permute-done | bytes 32800 | tf_op jit(solution)/shard_map/ppermute | solution.py:363
  63.3 2.7 %collective-permute-done.5.right = f32[4,16,128]{2,1,0:T(8,128)S(1)} collective-permute-done((f32[4,16,128]{2,1,0:T(8,128)S(1)}, f32[4,16,128]{2,1,0:T(8,128)S(1)}, u32[]{:S(2)}, u32[]{:S(2)}) %collective-permute-start.5) | collective-permute-done | bytes 32800 | tf_op jit(solution)/shard_map/ppermute | solution.py:364
  66.0 1.3 %shard_map.134 = f32[16,8,128]{2,1,0:T(8,128)S(1)} custom-call(s32[2]{0:T(128)S(1)} %pad_add_fusion.place, f32[4,32,128]{2,1,0:T(8,128)S(1)} %get-tuple-element.74.near, f32[4,16,128]{2,1,0:T(8,128)S(1)} %collective-permute-done.4.left, f32[4,16,128]{2,1,0:T(8,128)S(1)} %collective-permute-done.5.right), custom_call_target="tpu_custom_call" | custom-call | tf_op jit(solution)/shard_map/pallas_call | solution.py:350
  67.2 11.2 %all_to_all.16.got = f32[16,8,128]{2,1,0:T(8,128)S(1)} all-to-all(f32[16,8,128]{2,1,0:T(8,128)S(1)} %shard_map.134), channel_id=1, replica_groups=mesh['gx'=8,'gy'=16] {'gy'}, dimensions={0} | all-to-all | bytes 131072 | tf_op jit(solution)/shard_map/all_to_all | solution.py:433
  78.5 0.7 shard_map.135
  (33 shorter events, 3.4 us)
Async XLA Ops:
  0.6 0.7 copy-start.16
  1.3 0.9 %copy-start = (f32[32,8,128]{2,1,0:T(8,128)S(1)}, f32[32,8,128]{2,1,0:T(8,128)}, u32[]{:S(2)}) copy-start(f32[32,8,128]{2,1,0:T(8,128)} %s0.5) | copy-start | bytes 393220
  2.2 0.9 %copy-start.2 = (f32[32,8,128]{2,1,0:T(8,128)S(1)}, f32[32,8,128]{2,1,0:T(8,128)}, u32[]{:S(2)}) copy-start(f32[32,8,128]{2,1,0:T(8,128)} %r0.5) | copy-start | bytes 393220
  3.1 0.9 %copy-start.4 = (f32[32,8,128]{2,1,0:T(8,128)S(1)}, f32[32,8,128]{2,1,0:T(8,128)}, u32[]{:S(2)}) copy-start(f32[32,8,128]{2,1,0:T(8,128)} %sm.5) | copy-start | bytes 393220
  4.0 0.9 %copy-start.6 = (f32[32,8,128]{2,1,0:T(8,128)S(1)}, f32[32,8,128]{2,1,0:T(8,128)}, u32[]{:S(2)}) copy-start(f32[32,8,128]{2,1,0:T(8,128)} %rm.5) | copy-start | bytes 393220
  4.9 0.9 %copy-start.8 = (f32[32,8,128]{2,1,0:T(8,128)S(1)}, f32[32,8,128]{2,1,0:T(8,128)}, u32[]{:S(2)}) copy-start(f32[32,8,128]{2,1,0:T(8,128)} %c.5) | copy-start | bytes 393220
  5.8 0.8 copy-start.10
  6.6 0.7 copy-start.12
  7.3 12.1 %copy-start.1 = (f32[32,8,128]{2,1,0:T(8,128)S(1)}, f32[32,8,128]{2,1,0:T(8,128)}, u32[]{:S(2)}) copy-start(f32[32,8,128]{2,1,0:T(8,128)} %s0.5) | copy-start | bytes 393220
  7.3 12.1 %copy-start.3 = (f32[32,8,128]{2,1,0:T(8,128)S(1)}, f32[32,8,128]{2,1,0:T(8,128)}, u32[]{:S(2)}) copy-start(f32[32,8,128]{2,1,0:T(8,128)} %r0.5) | copy-start | bytes 393220
  7.3 12.1 %copy-start.5 = (f32[32,8,128]{2,1,0:T(8,128)S(1)}, f32[32,8,128]{2,1,0:T(8,128)}, u32[]{:S(2)}) copy-start(f32[32,8,128]{2,1,0:T(8,128)} %sm.5) | copy-start | bytes 393220
  7.3 12.1 %copy-start.7 = (f32[32,8,128]{2,1,0:T(8,128)S(1)}, f32[32,8,128]{2,1,0:T(8,128)}, u32[]{:S(2)}) copy-start(f32[32,8,128]{2,1,0:T(8,128)} %rm.5) | copy-start | bytes 393220
  7.3 12.1 %copy-start.9 = (f32[32,8,128]{2,1,0:T(8,128)S(1)}, f32[32,8,128]{2,1,0:T(8,128)}, u32[]{:S(2)}) copy-start(f32[32,8,128]{2,1,0:T(8,128)} %c.5) | copy-start | bytes 393220
  7.3 12.1 %copy-start.11 = (f32[2,4,8,32]{3,2,1,0:T(8,128)S(1)}, f32[2,4,8,32]{3,2,1,0:T(8,128)}, u32[]{:S(2)}) copy-start(f32[2,4,8,32]{3,2,1,0:T(8,128)} %values.5) | copy-start | bytes 24580
  9.3 7.3 %collective-permute-start = (f32[113,8,128]{2,1,0:T(8,128)S(1)}, f32[113,8,128]{2,1,0:T(8,128)S(1)}, u32[]{:S(2)}, u32[]{:S(2)}) collective-permute-start(f32[113,8,128]{2,1,0:T(8,128)S(1)} %get-tuple-element.60), channel_id=1, source_target_pairs={{0,1},{1,2},{2,3},{3,4},{4,5},{5,6},{6,7},{7,8},{8,9},{9,10},{10,1... | collective-permute-start | bytes 1388552 | tf_op jit(solution)/shard_map/ppermute | solution.py:363
  11.2 8.2 %collective-permute-start.1 = (f32[113,8,128]{2,1,0:T(8,128)S(1)}, f32[113,8,128]{2,1,0:T(8,128)S(1)}, u32[]{:S(2)}, u32[]{:S(2)}) collective-permute-start(f32[113,8,128]{2,1,0:T(8,128)S(1)} %get-tuple-element.61), channel_id=1, source_target_pairs={{1,0},{2,1},{3,2},{4,3},{5,4},{6,5},{7,6},{8,7},{9,8},{10,9},{11,1... | collective-permute-start | bytes 1388552 | tf_op jit(solution)/shard_map/ppermute | solution.py:364
  11.2 8.3 %copy-start.13 = (s32[8,32]{1,0:T(8,128)S(1)}, s32[8,32]{1,0:T(8,128)}, u32[]{:S(2)}) copy-start(s32[8,32]{1,0:T(8,128)} %depth.5) | copy-start | bytes 3076
  20.1 25.9 %collective-permute-start.2 = (f32[38,8,128]{2,1,0:T(8,128)S(1)}, f32[38,8,128]{2,1,0:T(8,128)S(1)}, u32[]{:S(2)}, u32[]{:S(2)}) collective-permute-start(f32[38,8,128]{2,1,0:T(8,128)S(1)} %get-tuple-element.62), channel_id=1, source_target_pairs={{0,16},{16,32},{32,48},{48,64},{64,80},{80,96},{96,112},{112,0},{1... | collective-permute-start | bytes 466952 | tf_op jit(solution)/shard_map/ppermute | solution.py:363
  21.7 24.3 %collective-permute-start.3 = (f32[38,8,128]{2,1,0:T(8,128)S(1)}, f32[38,8,128]{2,1,0:T(8,128)S(1)}, u32[]{:S(2)}, u32[]{:S(2)}) collective-permute-start(f32[38,8,128]{2,1,0:T(8,128)S(1)} %get-tuple-element.63), channel_id=1, source_target_pairs={{16,0},{32,16},{48,32},{64,48},{80,64},{96,80},{112,96},{0,112},{1... | collective-permute-start | bytes 466952 | tf_op jit(solution)/shard_map/ppermute | solution.py:364
  23.1 18.9 %all-to-all-start.1 = ((f32[128,1,128]{2,1,0:T(1,128)}), f32[128,1,128]{2,1,0:T(1,128)S(1)}, u32[]{:S(2)}, u32[]{:S(2)}) async-start(f32[128,1,128]{2,1,0:T(1,128)} %get-tuple-element.64), calls=%async_computation.1 | async-start | bytes 131072 | tf_op jit(solution)/shard_map/all_to_all | solution.py:391
  44.6 0.7 copy-start.15
  46.0 0.7 copy-start.14
  59.0 4.3 %collective-permute-start.4 = (f32[4,16,128]{2,1,0:T(8,128)S(1)}, f32[4,16,128]{2,1,0:T(8,128)S(1)}, u32[]{:S(2)}, u32[]{:S(2)}) collective-permute-start(f32[4,16,128]{2,1,0:T(8,128)S(1)} %get-tuple-element.75), channel_id=1, source_target_pairs={{0,16},{16,32},{32,48},{48,64},{64,80},{80,96},{96,112},{112,0},{1... | collective-permute-start | bytes 98312 | tf_op jit(solution)/shard_map/ppermute | solution.py:363
  60.8 5.2 %collective-permute-start.5 = (f32[4,16,128]{2,1,0:T(8,128)S(1)}, f32[4,16,128]{2,1,0:T(8,128)S(1)}, u32[]{:S(2)}, u32[]{:S(2)}) collective-permute-start(f32[4,16,128]{2,1,0:T(8,128)S(1)} %get-tuple-element.76), channel_id=1, source_target_pairs={{16,0},{32,16},{48,32},{64,48},{80,64},{96,80},{112,96},{0,112},{1... | collective-permute-start | bytes 98312 | tf_op jit(solution)/shard_map/ppermute | solution.py:364

commit v2 on v1

--- a/solution.py
+++ b/solution.py
@@ -18,6 +18,7 @@
 DEVICES = GX * GY
 RECEIVERS = 256
 SLOTS = 16
+UNROLL = (10, 16)
 F32, BF16, I32 = jnp.float32, jnp.bfloat16, jnp.int32
 VMEM_LIMIT = 24 * 1024 * 1024
 
@@ -75,8 +76,14 @@
     return jnp.where(iota((DEVICES, 128), 1) >= row, rounds, sent)
 
 
-def route_kernel(first_ref, cells_ref, traces_ref, sent_ref):
-    sent_ref[:, 0, :] = routed(cells_ref[...], traces_ref[...], first_ref[0])
+def route_kernel(cells_ref, traces_ref, sent_ref):
+    sent_ref[:, 0, :] = routed(cells_ref[...], traces_ref[...], jnp.int32(0))
+
+
+def route_more_kernel(first_ref, cells, traces, sent_ref, cells_v, traces_v, sems):
+    for copy in started([(cells, cells_v), (traces, traces_v)], sems):
+        copy.wait()
+    sent_ref[:, 0, :] = routed(cells_v[...], traces_v[...], first_ref[0])
 
 
 def collected(got):
@@ -131,24 +138,44 @@
     return jnp.concatenate([depth, jnp.zeros((depth.shape[0], 96), depth.dtype)], axis=1)
 
 
+def started(copies, sems):
+    copies = [pltpu.make_async_copy(*ends, sems.at[k]) for k, ends in enumerate(copies)]
+    for copy in copies:
+        copy.start()
+    return copies
+
+
 def pack_y_kernel(
-    cells_ref, traces_ref, s0, r0, sm, rm, c, depth, values, sent_ref, up_ref, down_ref
+    cells, traces, s0, r0, sm, rm, c, depth, values,
+    up_ref, down_ref, cells_ref, traces_ref, sm_v, rm_v, c_v, depth_v, values_v, sems,
 ):
+    copies = started(
+        [
+            (sm, sm_v), (rm, rm_v), (c, c_v), (depth, depth_v), (values, values_v),
+            (s0, up_ref.at[0:32]), (r0, up_ref.at[32:64]), (s0, down_ref.at[0:32]), (r0, down_ref.at[32:64]),
+            (cells, cells_ref), (traces, traces_ref),
+        ],
+        sems,
+    )
+    for copy in copies[:5]:
+        copy.wait()
     for ref, rows in ((up_ref, slice(4, 8)), (down_ref, slice(0, 4))):
-        ref[0:32] = s0[...]
-        ref[32:64] = r0[...]
-        ref[64:96, 0:4] = sm[:, rows]
-        ref[64:96, 4:8] = rm[:, rows]
-        ref[96:112, 0:4] = c[0:16, rows]
-        ref[96:112, 4:8] = c[16:32, rows]
-        ref[112, 0:4] = strip_values_tile(values, 0, rows)
-        ref[112, 4:8] = wide(depth[rows].astype(F32))
-    sent_ref[:, 0, :] = routed(cells_ref[...], traces_ref[...], jnp.int32(0))
-
-
-def pack_x_kernel(
-    place, s0, r0, sm, rm, c, depth, values, before, after, up_ref, down_ref
-):
+        ref[64:96, 0:4] = sm_v[:, rows]
+        ref[64:96, 4:8] = rm_v[:, rows]
+        ref[96:112, 0:4] = c_v[0:16, rows]
+        ref[96:112, 4:8] = c_v[16:32, rows]
+        ref[112, 0:4] = strip_values_tile(values_v, 0, rows)
+        ref[112, 4:8] = wide(depth_v[rows].astype(F32))
+    for copy in copies[5:]:
+        copy.wait()
+
+
+def own_place():
+    return lax.axis_index("gx"), lax.axis_index("gy")
+
+
+def pack_x_kernel(s0, r0, sm, rm, c, depth, values, before, after, got, up_ref, down_ref):
+    place = own_place()
     keep_before = jnp.where(place[1] > 0, 1.0, 0.0)
     keep_after = jnp.where(place[1] < GY - 1, 1.0, 0.0)
     near = strip_values_tile(values, 0, slice(0, 8))
@@ -166,21 +193,28 @@
         ref[37] = depths
 
 
-def depth_pairs(tile, reach):
-    lane = iota((8, 128), 1)
-    below = jnp.where(lane < 128 - reach, pltpu.roll(tile, 128 - reach, 1), 0.0)
-    above = jnp.where(lane >= reach, pltpu.roll(tile, reach, 1), 0.0)
-    return below + above
-
-
-def curvature(ref, f, x, row):
+def depth_matrix():
+    apart = jnp.abs(iota((TZ, TZ), 0) - iota((TZ, TZ), 1))
+    weights = jnp.zeros((TZ, TZ), F32)
+    for reach in range(1, 5):
+        weights = jnp.where(apart == reach, COEFS[reach], weights)
+    high, low = halves(weights)
+    top = jnp.concatenate([high, low], axis=1)
+    return jnp.concatenate([top, jnp.concatenate([high, jnp.zeros_like(low)], axis=1)], axis=0)
+
+
+def depth_sums(rows, matrix):
+    both = jnp.dot(jnp.concatenate(halves(rows), axis=1), matrix, preferred_element_type=F32)
+    return both[:, :128] + both[:, 128:]
+
+
+def curvature(ref, f, x, row, depth_sum):
     tile = ref[f, x, row : row + 8]
-    total = (3.0 * COEFS[0]) * tile
+    total = (3.0 * COEFS[0]) * tile + depth_sum
     for reach in range(1, 5):
         pairs = ref[f, x + reach, row : row + 8] + ref[f, x - reach, row : row + 8]
         pairs = pairs + ref[f, x, row + reach : row + reach + 8]
         pairs = pairs + ref[f, x, row - reach : row - reach + 8]
-        pairs = pairs + depth_pairs(tile, reach)
         total = total + COEFS[reach] * pairs
     return tile, total
 
@@ -194,11 +228,13 @@
 
 
 def steps_kernel(
-    place, source_cell, wavelet,
+    source_cell, wavelet,
     s0, r0, sm, rm, c, depth, values, before, after, left, right, own, rim_y, rim_x,
     s_out, r_out, near_ref, up_ref, down_ref,
-    e_ref, m_ref, o_ref, d_ref, v_ref, sub_ref,
+    e_ref, m_ref, o_ref, z_ref, d_ref, v_ref, sub_ref, cell_s, wavelet_s, sems,
 ):
+    place = own_place()
+    copies = started([(source_cell, cell_s), (wavelet, wavelet_s)], sems)
     keep_before = jnp.where(place[1] > 0, 1.0, 0.0)
     keep_after = jnp.where(place[1] < GY - 1, 1.0, 0.0)
     keep_left = jnp.where(place[0] > 0, 1.0, 0.0)
@@ -238,53 +274,63 @@
         d_ref[k] = jnp.zeros((16, 128), I32)
         v_ref[k, 4:12] = ref[36] * keep
         d_ref[k, 4:12] = (ref[37] * keep).astype(I32)
-    cell = source_cell[0]
+    for copy in copies:
+        copy.wait()
+    cell = cell_s[0]
     source_x = (cell >> 14) - place[0] * TX
     source_y = ((cell >> 7) & 127) - place[1] * TY
     source_z = cell & 127
     lane, sublane = iota((8, 128), 1), iota((8, 128), 0)
 
+    matrix = depth_matrix()
+    for f in range(2):
+        rows = e_ref[f, 4:44, 8:24].reshape(640, 128)
+        z_ref[f] = depth_sums(rows, matrix).reshape(40, 16, 128)
+
     def first(i, carry):
         part = jnp.where(i >= 4, 1, 0) + jnp.where(i >= 36, 1, 0)
         column = jnp.where(i < 4, i + 28, jnp.where(i < 36, i - 4, i - 36))
-        amount = jnp.where(i - 4 == source_x, wavelet[0], 0.0)
+        amount = jnp.where(i - 4 == source_x, wavelet_s[0], 0.0)
         for t in range(2):
             rows = slice(8 * t, 8 * t + 8)
             at_source = (lane == source_z) & (sublane + (8 * t - 4) == source_y)
             courant = m_ref[2, i, rows]
-            now, total = curvature(e_ref, 0, i + 4, 8 + 8 * t)
+            now, total = curvature(e_ref, 0, i + 4, 8 + 8 * t, z_ref[0, i, rows])
             total = total - jnp.where(at_source, amount, 0.0)
             new = 2.0 * now - m_ref[0, i, rows] + courant * total
             new = overwritten(new, d_ref[part, rows], v_ref[part, rows], column)
             o_ref[0, i, 4 + 8 * t : 12 + 8 * t] = new
             sub_ref[0, t, pl.ds(i, 1)] = new[4 - 4 * t : 5 - 4 * t]
-            now, total = curvature(e_ref, 1, i + 4, 8 + 8 * t)
+            now, total = curvature(e_ref, 1, i + 4, 8 + 8 * t, z_ref[1, i, rows])
             new = 2.0 * now - m_ref[1, i, rows] + courant * (total + m_ref[3, i, rows])
             o_ref[1, i, 4 + 8 * t : 12 + 8 * t] = new
             sub_ref[2, t, pl.ds(i, 1)] = new[4 - 4 * t : 5 - 4 * t]
         return carry
 
-    lax.fori_loop(0, 40, first, 0)
+    lax.fori_loop(0, 40, first, 0, unroll=UNROLL[0])
+    for f in range(2):
+        rows = o_ref[f, 4:36, 8:16].reshape(256, 128)
+        z_ref[f, 0:32, 0:8] = depth_sums(rows, matrix).reshape(32, 8, 128)
     late_values = strip_values_tile(values, 1, slice(0, 8))
     at_source = (lane == source_z) & (sublane == source_y)
 
     def second(x, carry):
-        amount = jnp.where(x == source_x, wavelet[1], 0.0)
-        now, total = curvature(o_ref, 0, x + 4, 8)
+        amount = jnp.where(x == source_x, wavelet_s[1], 0.0)
+        now, total = curvature(o_ref, 0, x + 4, 8, z_ref[0, x, 0:8])
         total = total - jnp.where(at_source, amount, 0.0)
         new = 2.0 * now - s0[x] + c[x] * total
         new = overwritten(new, near_depth, late_values, x)
         s_out[x] = new
         for j in range(2):
             sub_ref[1, j, pl.ds(x + 4, 1)] = new[4 * j : 4 * j + 1]
-        now, total = curvature(o_ref, 1, x + 4, 8)
+        now, total = curvature(o_ref, 1, x + 4, 8, z_ref[1, x, 0:8])
         new = 2.0 * now - r0[x] + c[x] * (total + own[1, x])
         r_out[x] = new
         for j in range(2):
             sub_ref[3, j, pl.ds(x + 4, 1)] = new[4 * j : 4 * j + 1]
         return carry
 
-    lax.fori_loop(0, 32, second, 0)
+    lax.fori_loop(0, 32, second, 0, unroll=UNROLL[1])
     z, to = iota((TZ, 128), 0), iota((TZ, 128), 1)
     for k in range(4):
         total = None
@@ -299,7 +345,8 @@
         down_ref[k] = total[0:16]
 
 
-def angles_kernel(place, near, left, right, out_ref, g_ref):
+def angles_kernel(near, left, right, out_ref, g_ref):
+    place = own_place()
     keep_left = jnp.where(place[0] > 0, 1.0, 0.0)
     keep_right = jnp.where(place[0] < GX - 1, 1.0, 0.0)
     for k in range(4):
@@ -345,17 +392,21 @@
         out_ref[1, :, 128 * t : 128 * t + 128] = jnp.where(lane < 64, pltpu.roll(even, 64, 1), odd)
 
 
-def call(kernel, outs, scalars, arrays, out_scalars=0, scratch=(), cost=None):
+def call(kernel, outs, arrays, scalars=(), hbm=(), out_scalars=0, scratch=(), weight=0):
     smem, vmem = pl.BlockSpec(memory_space=pltpu.SMEM), pl.BlockSpec(memory_space=pltpu.VMEM)
+    far = pl.BlockSpec(memory_space=pltpu.HBM)
+    hbm = [
+        pltpu.with_memory_space_constraint(array, pltpu.HBM) if array.size > 2 else array for array in hbm
+    ]
     return pl.pallas_call(
         kernel,
         out_shape=[jax.ShapeDtypeStruct(shape, kind) for shape, kind in outs],
-        in_specs=[smem] * len(scalars) + [vmem] * len(arrays),
+        in_specs=[smem] * len(scalars) + [far] * len(hbm) + [vmem] * len(arrays),
         out_specs=[vmem] * (len(outs) - out_scalars) + [smem] * out_scalars,
         scratch_shapes=list(scratch),
         compiler_params=pltpu.CompilerParams(vmem_limit_bytes=VMEM_LIMIT),
-        cost_estimate=cost,
-    )(*scalars, *arrays)
+        cost_estimate=pl.CostEstimate(flops=0, bytes_accessed=weight, transcendentals=0) if weight else None,
+    )(*scalars, *hbm, *arrays)
 
 
 def both_ways(to_next, to_last, axis):
@@ -378,35 +429,38 @@
     strip_depth,
     strip_values,
 ):
-    place = jnp.stack([lax.axis_index("gx"), lax.axis_index("gy")]).astype(I32)
     cells = receiver_cells.reshape(1, RECEIVERS)
-    tile = (TX, TY, TZ)
+    tile, sent_shape = (TX, TY, TZ), ((DEVICES, 1, 128), F32)
+    listed = [((1, RECEIVERS), I32), ((2, RECEIVERS), F32)]
     fields = (source_now, receiver_now, source_next, receiver_next, courant, strip_depth, strip_values)
-    sent, up_y, down_y = call(
+    up_y, down_y, near_cells, near_traces = call(
         pack_y_kernel,
-        [((DEVICES, 1, 128), F32), ((113, 8, 128), F32), ((113, 8, 128), F32)],
-        [], [cells, receiver_traces, *fields],
+        [((113, 8, 128), F32), ((113, 8, 128), F32), *listed],
+        [],
+        hbm=[cells, receiver_traces, *fields],
+        scratch=[pltpu.VMEM(tile, F32)] * 3
+        + [pltpu.VMEM((8, 32), I32), pltpu.VMEM((2, 4, 8, 32), F32), pltpu.SemaphoreType.DMA((11,))],
     )
     before, after = both_ways(up_y, down_y, "gy")
+    (sent,) = call(route_kernel, [sent_shape], [near_cells, near_traces], weight=20_000_000)
     got = lax.all_to_all(sent, ("gx", "gy"), 0, 0, tiled=True)
-    up_x, down_x = call(
-        pack_x_kernel, [((38, 8, 128), F32)] * 2, [place], [*fields, before, after]
-    )
+    up_x, down_x = call(pack_x_kernel, [((38, 8, 128), F32)] * 2, [*fields, before, after, got])
     left, right = both_ways(up_x, down_x, "gx")
     sums = [((2, *tile), F32), (tile, F32), ((8, 8, 128), F32)]
-    own, rim_y, rim_x, rounds = call(
-        collect_kernel, [*sums, ((1,), I32)], [], [got], out_scalars=1
-    )
+    own, rim_y, rim_x, rounds = call(collect_kernel, [*sums, ((1,), I32)], [got], out_scalars=1, weight=40_000_000)
 
     def another(state):
         turn, *partial = state
         (more,) = call(
-            route_kernel,
-            [((DEVICES, 1, 128), F32)],
-            [(turn * SLOTS).reshape(1)], [cells, receiver_traces],
+            route_more_kernel,
+            [sent_shape],
+            [],
+            scalars=[(turn * SLOTS).reshape(1)],
+            hbm=[cells, receiver_traces],
+            scratch=[pltpu.VMEM(*shape) for shape in listed] + [pltpu.SemaphoreType.DMA((2,))],
         )
         more = lax.all_to_all(more, ("gx", "gy"), 0, 0, tiled=True)
-        return (turn + 1, *call(collect_more_kernel, sums, [], [more, *partial]))
+        return (turn + 1, *call(collect_more_kernel, sums, [more, *partial]))
 
     _, own, rim_y, rim_x = lax.while_loop(
         lambda state: state[0] < rounds[0], another, (jnp.int32(1), own, rim_y, rim_x)
@@ -414,24 +468,28 @@
     source_field, receiver_field, near, up, down = call(
         steps_kernel,
         [(tile, F32), (tile, F32), ((4, 32, 128), F32), ((4, 16, 128), F32), ((4, 16, 128), F32)],
-        [place, source_cell, wavelet],
         [*fields, before, after, left, right, own, rim_y, rim_x],
+        hbm=[source_cell, wavelet],
         scratch=[
             pltpu.VMEM((2, 48, 32, 128), F32),
             pltpu.VMEM((4, 40, 16, 128), F32),
             pltpu.VMEM((2, 40, 24, 128), F32),
+            pltpu.VMEM((2, 40, 16, 128), F32),
             pltpu.VMEM((3, 16, 128), I32),
             pltpu.VMEM((3, 16, 128), F32),
             pltpu.VMEM((4, 2, 40, 128), F32),
+            pltpu.SMEM((1,), I32),
+            pltpu.SMEM((2,), F32),
+            pltpu.SemaphoreType.DMA((2,)),
         ],
     )
     near_left, near_right = both_ways(up, down, "gx")
     (angles,) = call(
-        angles_kernel, [((16, 8, 128), F32)], [place], [near, near_left, near_right],
+        angles_kernel, [((16, 8, 128), F32)], [near, near_left, near_right],
         scratch=[pltpu.VMEM((4, 64, 128), F32)],
     )
     angles = lax.all_to_all(angles, "gy", 0, 0, tiled=True)
-    (image,) = call(arrange_kernel, [((2, 8, 1024), F32)], [], [angles])
+    (image,) = call(arrange_kernel, [((2, 8, 1024), F32)], [angles])
     return source_field, receiver_field, image
 
 

time: 80.5 us -> 58.9 us (0.73)
  blocking collectives: 11.2 us -> 30.1 us
  waiting for transfers between devices: 19.2 us -> 7.27 us
  starting transfers between devices: 19 us -> 7.97 us
  Pallas kernels: 19.6 us -> 9.68 us
  local copies, waits for them, and re-layouts: 7.99 us -> 0.69 us
    all_to_all x0 -> x1, blocking collectives: none -> 18.3 us  [body(): got = lax.all_to_all(sent, ('gx', 'gy'), 0, 0, tiled=True)]
    all_to_all x1 -> x0, starting transfers between devices: 11.2 us -> none  [body(): got = lax.all_to_all(sent, ('gx', 'gy'), 0, 0, tiled=True)]
    pallas_call x6 -> x7, Pallas kernels: 19.6 us -> 9.68 us  [call(): pl.pallas_call(kernel, out_shape=[jax.ShapeDtypeStruct(shape, kind) for s...]
    unnamed x34 -> x16, local copies, waits for them, and re-layouts: 7.99 us -> 0.69 us
    all_to_all x1 -> x0, waiting for transfers between devices: 7.07 us -> none  [body(): got = lax.all_to_all(sent, ('gx', 'gy'), 0, 0, tiled=True)]
    ppermute x3, waiting for transfers between devices: 6.69 us -> 1.3 us  [both_ways(): lax.ppermute(to_next, axis, [(i, (i + 1) % size) for i in range(size)])]
  transfers between devices with their start and end apart: 7 -> 6, of which waited for: 5 -> 3; matrix products, arithmetic and copies ran while one was open for 0% -> 0% of each run, Pallas kernels for 3% -> 6%
where the time goes in v2:
time: 58.9 us; the launch traced here: 57.8 us
  blocking collectives  30.1 us (51%)
  Pallas kernels  9.68 us (16%)
  starting transfers between devices  7.97 us (14%)
  waiting for transfers between devices  7.27 us (12%)
  between operations  1.45 us (2%)
  local copies, waits for them, and re-layouts  0.69 us (1%)
  loops' own time  0.65 us (1%)
    all_to_all x1, blocking collectives, body(): got = lax.all_to_all(sent, ('gx', 'gy'), 0, 0, tiled=True)  18.3 us
    all_to_all x1, blocking collectives, body(): angles = lax.all_to_all(angles, 'gy', 0, 0, tiled=True)  11.8 us
    pallas_call x7, Pallas kernels, call(): pl.pallas_call(kernel, out_shape=[jax.ShapeDtypeStruct(shape, kind) for s...  9.68 us
    ppermute x3, waiting for transfers between devices, both_ways(): lax.ppermute(to_last, axis, [((i + 1) % size, i) for i in range(size)])  5.96 us
    ppermute x3, starting transfers between devices, both_ways(): lax.ppermute(to_next, axis, [(i, (i + 1) % size) for i in range(size)])  5.74 us
    ppermute x3, starting transfers between devices, both_ways(): lax.ppermute(to_last, axis, [((i + 1) % size, i) for i in range(size)])  2.23 us
    ppermute x3, waiting for transfers between devices, both_ways(): lax.ppermute(to_next, axis, [(i, (i + 1) % size) for i in range(size)])  1.3 us
  transfers between devices with their start and end apart: 6, of which 3 were waited for; matrix products, arithmetic and copies ran while one was open for 0% of the time, Pallas kernels for 6%

profile of v2, /device:TPU:5, one launch (start us, length us, event | category | flops | bytes accessed | tf_op | source)
XLA Modules:
  0.0 57.8 jit_solution(12576860237361747606)
XLA Ops:
  0.7 1.4 %shard_map.130 = (f32[113,8,128]{2,1,0:T(8,128)S(1)}, f32[113,8,128]{2,1,0:T(8,128)S(1)}, s32[1,256]{1,0:T(1,128)S(1)}, f32[2,256]{1,0:T(2,128)S(1)}) custom-call(s32[1,256]{1,0:T(1,128)} %bitcast.6, f32[2,256]{1,0:T(2,128)} %traces.1, f32[32,8,128]{2,1,0:T(8,128)} %s0.5, f32[32,8,128]{2,1,0:T(8,128)} %r0.5, f32[32,8,128]{2,1,0:T(8,128)} %sm.5, ...), custom_call_target="tpu_custom_call" | custom-call | tf_op jit(solution)/shard_map/pallas_call | solution.py:401
  2.1 0.0 copy-start
  2.1 1.9 %collective-permute-start = (f32[113,8,128]{2,1,0:T(8,128)S(1)}, f32[113,8,128]{2,1,0:T(8,128)S(1)}, u32[]{:S(2)}, u32[]{:S(2)}) collective-permute-start(f32[113,8,128]{2,1,0:T(8,128)S(1)} %get-tuple-element.61), channel_id=1, source_target_pairs={{0,1},{1,2},{2,3},{3,4},{4,5},{5,6},{6,7},{7,8},{8,9},{9,10},{10,1... | collective-permute-start | bytes 1388552 | tf_op jit(solution)/shard_map/ppermute | solution.py:414
  4.0 0.0 collective-permute-start.1
  4.0 0.5 shard_map.131
  4.6 0.0 copy-start.5
  4.6 0.0 copy-start.6
  4.6 18.3 %all_to_all.16.got.got_ref = f32[128,1,128]{2,1,0:T(1,128)S(1)} all-to-all(f32[128,1,128]{2,1,0:T(1,128)S(1)} %shard_map.131), channel_id=1, replica_groups=mesh['gx'=8,'gy'=16] {'gx','gy'}, dimensions={0} | all-to-all | bytes 131072 | tf_op jit(solution)/shard_map/all_to_all | solution.py:446
  22.9 0.0 collective-permute-done.before
  23.0 0.1 shard_map.132
  23.1 1.8 %collective-permute-start.2 = (f32[38,8,128]{2,1,0:T(8,128)S(1)}, f32[38,8,128]{2,1,0:T(8,128)S(1)}, u32[]{:S(2)}, u32[]{:S(2)}) collective-permute-start(f32[38,8,128]{2,1,0:T(8,128)S(1)} %get-tuple-element.65), channel_id=1, source_target_pairs={{0,16},{16,32},{32,48},{48,64},{64,80},{80,96},{96,112},{112,0},{1... | collective-permute-start | bytes 466952 | tf_op jit(solution)/shard_map/ppermute | solution.py:414
  24.9 1.2 %collective-permute-start.3 = (f32[38,8,128]{2,1,0:T(8,128)S(1)}, f32[38,8,128]{2,1,0:T(8,128)S(1)}, u32[]{:S(2)}, u32[]{:S(2)}) collective-permute-start(f32[38,8,128]{2,1,0:T(8,128)S(1)} %get-tuple-element.66), channel_id=1, source_target_pairs={{16,0},{32,16},{48,32},{64,48},{80,64},{96,80},{112,96},{0,112},{1... | collective-permute-start | bytes 466952 | tf_op jit(solution)/shard_map/ppermute | solution.py:415
  26.7 2.7 %shard_map.133 = (f32[2,32,8,128]{3,2,1,0:T(8,128)S(1)}, f32[32,8,128]{2,1,0:T(8,128)S(1)}, f32[8,8,128]{2,1,0:T(8,128)S(1)}, s32[1]{0:T(128)}) custom-call(f32[128,1,128]{2,1,0:T(1,128)S(1)} %all_to_all.16.got.got_ref), custom_call_target="tpu_custom_call" | custom-call | bytes 40000000 | tf_op jit(solution)/shard_map/pallas_call | solution.py:401
  29.4 0.7 %while.14 = (s32[]{:T(128)}, f32[2,32,8,128]{3,2,1,0:T(8,128)S(1)}, f32[32,8,128]{2,1,0:T(8,128)S(1)}, f32[8,8,128]{2,1,0:T(8,128)S(1)}, s32[1]{0:T(128)}, /*ind...) while((s32[]{:T(128)}, f32[2,32,8,128]{3,2,1,0:T(8,128)S(1)}, f32[32,8,128]{2,1,0:T(8,128)S(1)}, ...), condition=%wide.region_1.0_spmd, body=%wide.region_0.0_spmd.sunk | while | flops 3 | bytes 1048713 | solution.py:465
  30.1 3.1 %collective-permute-done.3.right = f32[38,8,128]{2,1,0:T(8,128)S(1)} collective-permute-done((f32[38,8,128]{2,1,0:T(8,128)S(1)}, f32[38,8,128]{2,1,0:T(8,128)S(1)}, u32[]{:S(2)}, u32[]{:S(2)}) %collective-permute-start.3) | collective-permute-done | bytes 155680 | tf_op jit(solution)/shard_map/ppermute | solution.py:415
  33.2 0.7 %copy-done.7 = f32[2]{0:T(128)S(1)} copy-done((f32[2]{0:T(128)S(1)}, f32[2]{0:T(128)}, u32[]{:S(2)}) %copy-start.7) | copy-done | bytes 32
  33.9 3.5 %shard_map.134 = (f32[32,8,128]{2,1,0:T(8,128)}, f32[32,8,128]{2,1,0:T(8,128)}, f32[4,32,128]{2,1,0:T(8,128)S(1)}, f32[4,16,128]{2,1,0:T(8,128)S(1)}, f32[4,16,128]{2,1,0:T(8,128)S(1)}) custom-call(s32[1]{0:T(128)S(6)} %copy.29.source_cell, f32[2]{0:T(128)S(1)} %copy-done.7, f32[32,8,128]{2,1,0:T(8,128)S(1)} %copy-done, f32[32,8,128]{2,1,0:T(8,128)S(1)} %copy-done.1, ...), custom_call_target="tpu_custom_call" | custom-call | tf_op jit(solution)/shard_map/pallas_call | solution.py:401
  37.4 2.0 %collective-permute-start.4 = (f32[4,16,128]{2,1,0:T(8,128)S(1)}, f32[4,16,128]{2,1,0:T(8,128)S(1)}, u32[]{:S(2)}, u32[]{:S(2)}) collective-permute-start(f32[4,16,128]{2,1,0:T(8,128)S(1)} %get-tuple-element.77), channel_id=1, source_target_pairs={{0,16},{16,32},{32,48},{48,64},{64,80},{80,96},{96,112},{112,0},{1... | collective-permute-start | bytes 98312 | tf_op jit(solution)/shard_map/ppermute | solution.py:414
  39.4 1.1 %collective-permute-start.5 = (f32[4,16,128]{2,1,0:T(8,128)S(1)}, f32[4,16,128]{2,1,0:T(8,128)S(1)}, u32[]{:S(2)}, u32[]{:S(2)}) collective-permute-start(f32[4,16,128]{2,1,0:T(8,128)S(1)} %get-tuple-element.78), channel_id=1, source_target_pairs={{16,0},{32,16},{48,32},{64,48},{80,64},{96,80},{112,96},{0,112},{1... | collective-permute-start | bytes 98312 | tf_op jit(solution)/shard_map/ppermute | solution.py:415
  40.5 1.3 %collective-permute-done.4.left = f32[4,16,128]{2,1,0:T(8,128)S(1)} collective-permute-done((f32[4,16,128]{2,1,0:T(8,128)S(1)}, f32[4,16,128]{2,1,0:T(8,128)S(1)}, u32[]{:S(2)}, u32[]{:S(2)}) %collective-permute-start.4) | collective-permute-done | bytes 32800 | tf_op jit(solution)/shard_map/ppermute | solution.py:414
  41.8 2.8 %collective-permute-done.5.right = f32[4,16,128]{2,1,0:T(8,128)S(1)} collective-permute-done((f32[4,16,128]{2,1,0:T(8,128)S(1)}, f32[4,16,128]{2,1,0:T(8,128)S(1)}, u32[]{:S(2)}, u32[]{:S(2)}) %collective-permute-start.5) | collective-permute-done | bytes 32800 | tf_op jit(solution)/shard_map/ppermute | solution.py:415
  44.6 0.7 %shard_map.135 = f32[16,8,128]{2,1,0:T(8,128)S(1)} custom-call(f32[4,32,128]{2,1,0:T(8,128)S(1)} %get-tuple-element.76.near, f32[4,16,128]{2,1,0:T(8,128)S(1)} %collective-permute-done.4.left, f32[4,16,128]{2,1,0:T(8,128)S(1)} %collective-permute-done.5.right), custom_call_target="tpu_custom_call" | custom-call | tf_op jit(solution)/shard_map/pallas_call | solution.py:401
  45.3 11.8 %all_to_all.17.got = f32[16,8,128]{2,1,0:T(8,128)S(1)} all-to-all(f32[16,8,128]{2,1,0:T(8,128)S(1)} %shard_map.135), channel_id=1, replica_groups=mesh['gx'=8,'gy'=16] {'gy'}, dimensions={0} | all-to-all | bytes 131072 | tf_op jit(solution)/shard_map/all_to_all | solution.py:491
  57.1 0.7 %shard_map.136 = f32[2,8,1024]{2,1,0:T(8,128)} custom-call(f32[16,8,128]{2,1,0:T(8,128)S(1)} %all_to_all.17.got), custom_call_target="tpu_custom_call" | custom-call | tf_op jit(solution)/shard_map/pallas_call | solution.py:401
  (14 shorter events, 0.0 us)
Async XLA Ops:
  0.6 22.3 %copy-start.1 = (f32[32,8,128]{2,1,0:T(8,128)S(1)}, f32[32,8,128]{2,1,0:T(8,128)}, u32[]{:S(2)}) copy-start(f32[32,8,128]{2,1,0:T(8,128)} %r0.5) | copy-start | bytes 393220
  0.6 22.3 %copy-start.2 = (f32[32,8,128]{2,1,0:T(8,128)S(1)}, f32[32,8,128]{2,1,0:T(8,128)}, u32[]{:S(2)}) copy-start(f32[32,8,128]{2,1,0:T(8,128)} %sm.5) | copy-start | bytes 393220
  0.7 22.3 %copy-start.3 = (f32[32,8,128]{2,1,0:T(8,128)S(1)}, f32[32,8,128]{2,1,0:T(8,128)}, u32[]{:S(2)}) copy-start(f32[32,8,128]{2,1,0:T(8,128)} %rm.5) | copy-start | bytes 393220
  0.7 22.3 %copy-start.4 = (f32[32,8,128]{2,1,0:T(8,128)S(1)}, f32[32,8,128]{2,1,0:T(8,128)}, u32[]{:S(2)}) copy-start(f32[32,8,128]{2,1,0:T(8,128)} %c.5) | copy-start | bytes 393220
  2.1 20.9 %copy-start = (f32[32,8,128]{2,1,0:T(8,128)S(1)}, f32[32,8,128]{2,1,0:T(8,128)}, u32[]{:S(2)}) copy-start(f32[32,8,128]{2,1,0:T(8,128)} %s0.5) | copy-start | bytes 393220
  2.1 20.8 %collective-permute-start = (f32[113,8,128]{2,1,0:T(8,128)S(1)}, f32[113,8,128]{2,1,0:T(8,128)S(1)}, u32[]{:S(2)}, u32[]{:S(2)}) collective-permute-start(f32[113,8,128]{2,1,0:T(8,128)S(1)} %get-tuple-element.61), channel_id=1, source_target_pairs={{0,1},{1,2},{2,3},{3,4},{4,5},{5,6},{6,7},{7,8},{8,9},{9,10},{10,1... | collective-permute-start | bytes 1388552 | tf_op jit(solution)/shard_map/ppermute | solution.py:414
  4.0 18.9 %collective-permute-start.1 = (f32[113,8,128]{2,1,0:T(8,128)S(1)}, f32[113,8,128]{2,1,0:T(8,128)S(1)}, u32[]{:S(2)}, u32[]{:S(2)}) collective-permute-start(f32[113,8,128]{2,1,0:T(8,128)S(1)} %get-tuple-element.62), channel_id=1, source_target_pairs={{1,0},{2,1},{3,2},{4,3},{5,4},{6,5},{7,6},{8,7},{9,8},{10,9},{11,1... | collective-permute-start | bytes 1388552 | tf_op jit(solution)/shard_map/ppermute | solution.py:415
  4.6 18.4 %copy-start.5 = (f32[2,4,8,32]{3,2,1,0:T(8,128)S(1)}, f32[2,4,8,32]{3,2,1,0:T(8,128)}, u32[]{:S(2)}) copy-start(f32[2,4,8,32]{3,2,1,0:T(8,128)} %values.5) | copy-start | bytes 24580
  4.6 18.4 %copy-start.6 = (s32[8,32]{1,0:T(8,128)S(1)}, s32[8,32]{1,0:T(8,128)}, u32[]{:S(2)}) copy-start(s32[8,32]{1,0:T(8,128)} %depth.5) | copy-start | bytes 3076
  23.1 7.0 %collective-permute-start.2 = (f32[38,8,128]{2,1,0:T(8,128)S(1)}, f32[38,8,128]{2,1,0:T(8,128)S(1)}, u32[]{:S(2)}, u32[]{:S(2)}) collective-permute-start(f32[38,8,128]{2,1,0:T(8,128)S(1)} %get-tuple-element.65), channel_id=1, source_target_pairs={{0,16},{16,32},{32,48},{48,64},{64,80},{80,96},{96,112},{112,0},{1... | collective-permute-start | bytes 466952 | tf_op jit(solution)/shard_map/ppermute | solution.py:414
  24.9 8.3 %collective-permute-start.3 = (f32[38,8,128]{2,1,0:T(8,128)S(1)}, f32[38,8,128]{2,1,0:T(8,128)S(1)}, u32[]{:S(2)}, u32[]{:S(2)}) collective-permute-start(f32[38,8,128]{2,1,0:T(8,128)S(1)} %get-tuple-element.66), channel_id=1, source_target_pairs={{16,0},{32,16},{48,32},{64,48},{80,64},{96,80},{112,96},{0,112},{1... | collective-permute-start | bytes 466952 | tf_op jit(solution)/shard_map/ppermute | solution.py:415
  33.2 0.7 %copy-start.7 = (f32[2]{0:T(128)S(1)}, f32[2]{0:T(128)}, u32[]{:S(2)}) copy-start(f32[2]{0:T(128)} %wavelet.1) | copy-start | bytes 28
  37.4 4.3 %collective-permute-start.4 = (f32[4,16,128]{2,1,0:T(8,128)S(1)}, f32[4,16,128]{2,1,0:T(8,128)S(1)}, u32[]{:S(2)}, u32[]{:S(2)}) collective-permute-start(f32[4,16,128]{2,1,0:T(8,128)S(1)} %get-tuple-element.77), channel_id=1, source_target_pairs={{0,16},{16,32},{32,48},{48,64},{64,80},{80,96},{96,112},{112,0},{1... | collective-permute-start | bytes 98312 | tf_op jit(solution)/shard_map/ppermute | solution.py:414
  39.4 5.2 %collective-permute-start.5 = (f32[4,16,128]{2,1,0:T(8,128)S(1)}, f32[4,16,128]{2,1,0:T(8,128)S(1)}, u32[]{:S(2)}, u32[]{:S(2)}) collective-permute-start(f32[4,16,128]{2,1,0:T(8,128)S(1)} %get-tuple-element.78), channel_id=1, source_target_pairs={{16,0},{32,16},{48,32},{64,48},{80,64},{96,80},{112,96},{0,112},{1... | collective-permute-start | bytes 98312 | tf_op jit(solution)/shard_map/ppermute | solution.py:415

commit v3 on v2

--- a/solution.py
+++ b/solution.py
@@ -18,7 +18,6 @@
 DEVICES = GX * GY
 RECEIVERS = 256
 SLOTS = 16
-UNROLL = (10, 16)
 F32, BF16, I32 = jnp.float32, jnp.bfloat16, jnp.int32
 VMEM_LIMIT = 24 * 1024 * 1024
 
@@ -113,7 +112,7 @@
 
 
 def collect_kernel(got_ref, own_ref, rim_y_ref, rim_x_ref, rounds_ref):
-    got = got_ref[:, 0, :]
+    got = got_ref[...]
     own_0, own_1, rim_y, rim_x = collected(got)
     own_ref[0] = own_0.reshape(TX, 8, 128)
     own_ref[1] = own_1.reshape(TX, 8, 128)
@@ -145,21 +144,21 @@
     return copies
 
 
-def pack_y_kernel(
-    cells, traces, s0, r0, sm, rm, c, depth, values,
-    up_ref, down_ref, cells_ref, traces_ref, sm_v, rm_v, c_v, depth_v, values_v, sems,
+def pack_kernel(
+    cells, traces, wavelet, s0, r0, sm, rm, c, depth, values,
+    up_y, down_y, cells_ref, traces_ref, wavelet_ref, sm_v, rm_v, c_v, depth_v, values_v, sems,
 ):
     copies = started(
         [
             (sm, sm_v), (rm, rm_v), (c, c_v), (depth, depth_v), (values, values_v),
-            (s0, up_ref.at[0:32]), (r0, up_ref.at[32:64]), (s0, down_ref.at[0:32]), (r0, down_ref.at[32:64]),
-            (cells, cells_ref), (traces, traces_ref),
+            (s0, up_y.at[0:32]), (r0, up_y.at[32:64]), (s0, down_y.at[0:32]), (r0, down_y.at[32:64]),
+            (cells, cells_ref), (traces, traces_ref), (wavelet, wavelet_ref),
         ],
         sems,
     )
     for copy in copies[:5]:
         copy.wait()
-    for ref, rows in ((up_ref, slice(4, 8)), (down_ref, slice(0, 4))):
+    for ref, rows in ((up_y, slice(4, 8)), (down_y, slice(0, 4))):
         ref[64:96, 0:4] = sm_v[:, rows]
         ref[64:96, 4:8] = rm_v[:, rows]
         ref[96:112, 0:4] = c_v[0:16, rows]
@@ -170,14 +169,8 @@
         copy.wait()
 
 
-def own_place():
-    return lax.axis_index("gx"), lax.axis_index("gy")
-
-
-def pack_x_kernel(s0, r0, sm, rm, c, depth, values, before, after, got, up_ref, down_ref):
-    place = own_place()
-    keep_before = jnp.where(place[1] > 0, 1.0, 0.0)
-    keep_after = jnp.where(place[1] < GY - 1, 1.0, 0.0)
+def pack_x_kernel(s0, r0, sm, rm, c, depth, values, before, after, up_ref, down_ref):
+    keep_before, keep_after = keeps("gy", GY)
     near = strip_values_tile(values, 0, slice(0, 8))
     depths = wide(depth[...].astype(F32))
     for ref, deep, rim in ((up_ref, 24, 28), (down_ref, 0, 0)):
@@ -227,117 +220,191 @@
     return jnp.where((relative >= 0) & (relative < 4), fill, tile)
 
 
+def keeps(axis, size):
+    at = lax.axis_index(axis)
+    return jnp.where(at > 0, 1.0, 0.0), jnp.where(at < size - 1, 1.0, 0.0)
+
+
+def pulse(source_cell, wavelet, step, row):
+    cell = source_cell[0]
+    lane, sublane = iota((8, 128), 1), iota((8, 128), 0)
+    at_row = sublane + (row + lax.axis_index("gy") * TY) == (cell >> 7) & 127
+    return jnp.where((lane == cell & 127) & at_row, wavelet[0:1, step : step + 1], 0.0)
+
+
+def source_layer(source_cell):
+    return (source_cell[0] >> 14) - lax.axis_index("gx") * TX
+
+
+def near_strips(depth, values, before, after, keep_before, keep_after, d_ref, v_ref):
+    v_ref[4:12] = strip_values_tile(values, 0, slice(0, 8))
+    d_ref[4:12] = wide(depth[...])
+    for ref, keep, rows in ((before, keep_before, slice(0, 4)), (after, keep_after, slice(12, 16))):
+        v_ref[rows] = ref[112, 0:4] * keep
+        d_ref[rows] = (ref[112, 4:8] * keep).astype(I32)
+
+
+def beside_rows(ref, before, after, keep_before, keep_after, to, first, last):
+    size = last - first
+    for part, keep, rows in ((before, keep_before, slice(0, 4)), (after, keep_after, slice(12, 16))):
+        ref[0, to : to + size, rows] = part[64 + first : 64 + last, 0:4] * keep
+        ref[1, to : to + size, rows] = part[64 + first : 64 + last, 4:8] * keep
+        for half in range(2):
+            low, high = max(first, 16 * half), min(last, 16 * half + 16)
+            if low < high:
+                at = to + low - first
+                start = 96 + low - 16 * half
+                ref[2, at : at + high - low, rows] = (
+                    part[start : start + high - low, 4 * half : 4 * half + 4] * keep
+                )
+
+
+def inner_kernel(
+    source_cell,
+    wavelet, s0, r0, sm, rm, c, depth, values, before, after,
+    new_ref, courant_ref,
+    e_ref, m_ref, z_ref, d_ref, v_ref,
+):
+    keep_before, keep_after = keeps("gy", GY)
+    for f, field in ((0, s0), (1, r0)):
+        e_ref[f, :, 12:20] = field[...]
+        e_ref[f, :, 4:12] = before[32 * f : 32 * f + 32] * keep_before
+        e_ref[f, :, 20:28] = after[32 * f : 32 * f + 32] * keep_after
+    for k, field in ((0, sm), (1, rm), (2, c)):
+        m_ref[k, :, 4:12] = field[4:28]
+    beside_rows(m_ref, before, after, keep_before, keep_after, 0, 4, 28)
+    near_strips(depth, values, before, after, keep_before, keep_after, d_ref, v_ref)
+    pulses = [pulse(source_cell, wavelet, 0, 8 * t - 4) for t in range(2)]
+    source_x = source_layer(source_cell)
+    matrix = depth_matrix()
+    for f in range(2):
+        rows = e_ref[f, 4:28, 8:24].reshape(384, 128)
+        z_ref[f] = depth_sums(rows, matrix).reshape(24, 16, 128)
+
+    def layer(i, carry):
+        for t in range(2):
+            rows = slice(8 * t, 8 * t + 8)
+            courant = m_ref[2, i, rows]
+            courant_ref[i, rows] = courant
+            now, total = curvature(e_ref, 0, i + 4, 8 + 8 * t, z_ref[0, i, rows])
+            total = total - jnp.where(i + 4 == source_x, pulses[t], 0.0)
+            new = 2.0 * now - m_ref[0, i, rows] + courant * total
+            new_ref[0, i, rows] = overwritten(new, d_ref[rows], v_ref[rows], i + 4)
+            now, total = curvature(e_ref, 1, i + 4, 8 + 8 * t, z_ref[1, i, rows])
+            new_ref[1, i, rows] = 2.0 * now - m_ref[1, i, rows] + courant * total
+        return carry
+
+    lax.fori_loop(0, 24, layer, 0, unroll=8)
+
+
 def steps_kernel(
-    source_cell, wavelet,
-    s0, r0, sm, rm, c, depth, values, before, after, left, right, own, rim_y, rim_x,
+    source_cell,
+    wavelet, s0, r0, sm, rm, c, depth, values, before, after, left, right, inner, inner_courant,
+    own, rim_y, rim_x,
     s_out, r_out, near_ref, up_ref, down_ref,
-    e_ref, m_ref, o_ref, z_ref, d_ref, v_ref, sub_ref, cell_s, wavelet_s, sems,
+    e_ref, m_ref, o_ref, z_ref, d_ref, v_ref, sub_ref,
 ):
-    place = own_place()
-    copies = started([(source_cell, cell_s), (wavelet, wavelet_s)], sems)
-    keep_before = jnp.where(place[1] > 0, 1.0, 0.0)
-    keep_after = jnp.where(place[1] < GY - 1, 1.0, 0.0)
-    keep_left = jnp.where(place[0] > 0, 1.0, 0.0)
-    keep_right = jnp.where(place[0] < GX - 1, 1.0, 0.0)
+    keep_before, keep_after = keeps("gy", GY)
+    keep_left, keep_right = keeps("gx", GX)
+    sides = ((0, left, keep_left), (1, right, keep_right))
     for f, field in ((0, s0), (1, r0)):
-        e_ref[f, 8:40, 12:20] = field[...]
-        e_ref[f, 8:40, 4:12] = before[32 * f : 32 * f + 32] * keep_before
-        e_ref[f, 8:40, 20:28] = after[32 * f : 32 * f + 32] * keep_after
-        for ref, keep, deep, rim in ((left, keep_left, 0, 4), (right, keep_right, 40, 40)):
-            e_ref[f, deep : deep + 8, 12:20] = ref[8 * f : 8 * f + 8] * keep
+        for side, ref, keep in sides:
+            near, far, rim, first = ((8, 0, 4, 0), (16, 24, 24, 24))[side]
+            e_ref[f, near : near + 8, 12:20] = field[first : first + 8]
+            start = 32 * f + first
+            e_ref[f, near : near + 8, 4:12] = before[start : start + 8] * keep_before
+            e_ref[f, near : near + 8, 20:28] = after[start : start + 8] * keep_after
+            e_ref[f, far : far + 8, 12:20] = ref[8 * f : 8 * f + 8] * keep
             corner = 16 + 4 * f
             e_ref[f, rim : rim + 4, 8:12] = ref[corner : corner + 4, 0:4] * keep
             e_ref[f, rim : rim + 4, 20:24] = ref[corner : corner + 4, 4:8] * keep
     for k, field in ((0, sm), (1, rm), (2, c)):
-        m_ref[k, 4:36, 4:12] = field[...]
         m_ref[k, 0:4, 4:12] = left[24 + 4 * k : 28 + 4 * k] * keep_left
-        m_ref[k, 36:40, 4:12] = right[24 + 4 * k : 28 + 4 * k] * keep_right
-    for ref, keep, rows in ((before, keep_before, slice(0, 4)), (after, keep_after, slice(12, 16))):
-        m_ref[0, 4:36, rows] = ref[64:96, 0:4] * keep
-        m_ref[1, 4:36, rows] = ref[64:96, 4:8] * keep
-        m_ref[2, 4:20, rows] = ref[96:112, 0:4] * keep
-        m_ref[2, 20:36, rows] = ref[96:112, 4:8] * keep
-    m_ref[3, 4:36, 4:12] = own[0]
-    m_ref[3, 4:36, 0:4] = rim_y[:, 0:4]
-    m_ref[3, 4:36, 12:16] = rim_y[:, 4:8]
+        m_ref[k, 4:8, 4:12] = field[0:4]
+        m_ref[k, 8:12, 4:12] = field[28:32]
+        m_ref[k, 12:16, 4:12] = right[24 + 4 * k : 28 + 4 * k] * keep_right
+    beside_rows(m_ref, before, after, keep_before, keep_after, 4, 0, 4)
+    beside_rows(m_ref, before, after, keep_before, keep_after, 8, 28, 32)
     m_ref[3, 0:4, 4:12] = rim_x[0:4]
-    m_ref[3, 36:40, 4:12] = rim_x[4:8]
-    near_values = strip_values_tile(values, 0, slice(0, 8))
-    near_depth = wide(depth[...])
-    v_ref[1, 4:12] = near_values
-    d_ref[1, 4:12] = near_depth
-    for ref, keep, rows in ((before, keep_before, slice(0, 4)), (after, keep_after, slice(12, 16))):
-        v_ref[1, rows] = ref[112, 0:4] * keep
-        d_ref[1, rows] = (ref[112, 4:8] * keep).astype(I32)
-    for k, ref, keep in ((0, left, keep_left), (2, right, keep_right)):
-        v_ref[k] = jnp.zeros((16, 128), F32)
-        d_ref[k] = jnp.zeros((16, 128), I32)
-        v_ref[k, 4:12] = ref[36] * keep
-        d_ref[k, 4:12] = (ref[37] * keep).astype(I32)
-    for copy in copies:
-        copy.wait()
-    cell = cell_s[0]
-    source_x = (cell >> 14) - place[0] * TX
-    source_y = ((cell >> 7) & 127) - place[1] * TY
-    source_z = cell & 127
-    lane, sublane = iota((8, 128), 1), iota((8, 128), 0)
-
+    m_ref[3, 12:16, 4:12] = rim_x[4:8]
+    for to, first in ((4, 0), (8, 28)):
+        m_ref[3, to : to + 4, 4:12] = own[0, first : first + 4]
+        m_ref[3, to : to + 4, 0:4] = rim_y[first : first + 4, 0:4]
+        m_ref[3, to : to + 4, 12:16] = rim_y[first : first + 4, 4:8]
+    near_strips(depth, values, before, after, keep_before, keep_after, d_ref.at[1], v_ref.at[1])
+    for side, ref, keep in sides:
+        v_ref[2 * side] = jnp.zeros((16, 128), F32)
+        d_ref[2 * side] = jnp.zeros((16, 128), I32)
+        v_ref[2 * side, 4:12] = ref[36] * keep
+        d_ref[2 * side, 4:12] = (ref[37] * keep).astype(I32)
+    o_ref[0, 8:32, 4:20] = inner[0]
+    o_ref[1, 8:32, 8:16] = inner[1, :, 4:12] + inner_courant[:, 4:12] * own[0, 4:28]
+    o_ref[1, 8:32, 4:8] = inner[1, :, 0:4] + inner_courant[:, 0:4] * rim_y[4:28, 0:4]
+    o_ref[1, 8:32, 16:20] = inner[1, :, 12:16] + inner_courant[:, 12:16] * rim_y[4:28, 4:8]
+    pulses = [pulse(source_cell, wavelet, 0, 8 * t - 4) for t in range(2)]
+    source_x = source_layer(source_cell)
     matrix = depth_matrix()
     for f in range(2):
-        rows = e_ref[f, 4:44, 8:24].reshape(640, 128)
-        z_ref[f] = depth_sums(rows, matrix).reshape(40, 16, 128)
-
-    def first(i, carry):
-        part = jnp.where(i >= 4, 1, 0) + jnp.where(i >= 36, 1, 0)
-        column = jnp.where(i < 4, i + 28, jnp.where(i < 36, i - 4, i - 36))
-        amount = jnp.where(i - 4 == source_x, wavelet_s[0], 0.0)
+        for side in range(2):
+            rows = e_ref[f, 4 + 16 * side : 12 + 16 * side, 8:24].reshape(128, 128)
+            z_ref[f, 8 * side : 8 * side + 8] = depth_sums(rows, matrix).reshape(8, 16, 128)
+
+    def first(j, carry):
+        part = jnp.where(j >= 4, 1, 0) + jnp.where(j >= 12, 1, 0)
+        low = j < 8
+        column = jnp.where(j < 4, j + 28, jnp.where(low, j - 4, jnp.where(j < 12, j + 20, j - 12)))
+        at = jnp.where(low, j + 4, j + 12)
+        i = jnp.where(low, j, j + 24)
         for t in range(2):
             rows = slice(8 * t, 8 * t + 8)
-            at_source = (lane == source_z) & (sublane + (8 * t - 4) == source_y)
-            courant = m_ref[2, i, rows]
-            now, total = curvature(e_ref, 0, i + 4, 8 + 8 * t, z_ref[0, i, rows])
-            total = total - jnp.where(at_source, amount, 0.0)
-            new = 2.0 * now - m_ref[0, i, rows] + courant * total
+            courant = m_ref[2, j, rows]
+            now, total = curvature(e_ref, 0, at, 8 + 8 * t, z_ref[0, j, rows])
+            total = total - jnp.where(i - 4 == source_x, pulses[t], 0.0)
+            new = 2.0 * now - m_ref[0, j, rows] + courant * total
             new = overwritten(new, d_ref[part, rows], v_ref[part, rows], column)
             o_ref[0, i, 4 + 8 * t : 12 + 8 * t] = new
-            sub_ref[0, t, pl.ds(i, 1)] = new[4 - 4 * t : 5 - 4 * t]
-            now, total = curvature(e_ref, 1, i + 4, 8 + 8 * t, z_ref[1, i, rows])
-            new = 2.0 * now - m_ref[1, i, rows] + courant * (total + m_ref[3, i, rows])
+            now, total = curvature(e_ref, 1, at, 8 + 8 * t, z_ref[1, j, rows])
+            new = 2.0 * now - m_ref[1, j, rows] + courant * (total + m_ref[3, j, rows])
             o_ref[1, i, 4 + 8 * t : 12 + 8 * t] = new
-            sub_ref[2, t, pl.ds(i, 1)] = new[4 - 4 * t : 5 - 4 * t]
         return carry
 
-    lax.fori_loop(0, 40, first, 0, unroll=UNROLL[0])
+    lax.fori_loop(0, 16, first, 0, unroll=8)
     for f in range(2):
-        rows = o_ref[f, 4:36, 8:16].reshape(256, 128)
-        z_ref[f, 0:32, 0:8] = depth_sums(rows, matrix).reshape(32, 8, 128)
+        for half in range(2):
+            rows = o_ref[f, 4 + 16 * half : 20 + 16 * half, 8:16].reshape(128, 128)
+            z_ref[f, :, 8 * half : 8 * half + 8] = depth_sums(rows, matrix).reshape(16, 8, 128)
     late_values = strip_values_tile(values, 1, slice(0, 8))
-    at_source = (lane == source_z) & (sublane == source_y)
-
-    def second(x, carry):
-        amount = jnp.where(x == source_x, wavelet_s[1], 0.0)
-        now, total = curvature(o_ref, 0, x + 4, 8, z_ref[0, x, 0:8])
-        total = total - jnp.where(at_source, amount, 0.0)
+    near_depth = wide(depth[...])
+    late_pulse = pulse(source_cell, wavelet, 1, 0)
+
+    def second(x, half):
+        rows = slice(8 * half, 8 * half + 8)
+        now, total = curvature(o_ref, 0, x + 4, 8, z_ref[0, x - 16 * half, rows])
+        total = total - jnp.where(x == source_x, late_pulse, 0.0)
         new = 2.0 * now - s0[x] + c[x] * total
         new = overwritten(new, near_depth, late_values, x)
         s_out[x] = new
         for j in range(2):
-            sub_ref[1, j, pl.ds(x + 4, 1)] = new[4 * j : 4 * j + 1]
-        now, total = curvature(o_ref, 1, x + 4, 8, z_ref[1, x, 0:8])
+            sub_ref[0, j, pl.ds(x, 1)] = now[4 * j : 4 * j + 1]
+            sub_ref[1, j, pl.ds(x, 1)] = new[4 * j : 4 * j + 1]
+        now, total = curvature(o_ref, 1, x + 4, 8, z_ref[1, x - 16 * half, rows])
         new = 2.0 * now - r0[x] + c[x] * (total + own[1, x])
         r_out[x] = new
         for j in range(2):
-            sub_ref[3, j, pl.ds(x + 4, 1)] = new[4 * j : 4 * j + 1]
-        return carry
-
-    lax.fori_loop(0, 32, second, 0, unroll=UNROLL[1])
+            sub_ref[2, j, pl.ds(x, 1)] = now[4 * j : 4 * j + 1]
+            sub_ref[3, j, pl.ds(x, 1)] = new[4 * j : 4 * j + 1]
+
+    for half in range(2):
+        lax.fori_loop(
+            16 * half, 16 * half + 16, lambda x, carry, half=half: (second(x, half), carry)[1], 0, unroll=16
+        )
     z, to = iota((TZ, 128), 0), iota((TZ, 128), 1)
     for k in range(4):
         total = None
         for j in range(2):
             pick = jnp.where((z & 3 == 0) & (to == (z >> 2) + (16 + 64 * j)), 1.0, 0.0)
             part = jnp.dot(
-                sub_ref[k, j, 4:36], pick, precision=lax.Precision.HIGHEST, preferred_element_type=F32
+                sub_ref[k, j], pick, precision=lax.Precision.HIGHEST, preferred_element_type=F32
             )
             total = part if total is None else total + part
         near_ref[k] = total
@@ -346,9 +413,7 @@
 
 
 def angles_kernel(near, left, right, out_ref, g_ref):
-    place = own_place()
-    keep_left = jnp.where(place[0] > 0, 1.0, 0.0)
-    keep_right = jnp.where(place[0] < GX - 1, 1.0, 0.0)
+    keep_left, keep_right = keeps("gx", GX)
     for k in range(4):
         g_ref[k, 0:16] = left[k] * keep_left
         g_ref[k, 16:48] = near[k]
@@ -396,7 +461,7 @@
     smem, vmem = pl.BlockSpec(memory_space=pltpu.SMEM), pl.BlockSpec(memory_space=pltpu.VMEM)
     far = pl.BlockSpec(memory_space=pltpu.HBM)
     hbm = [
-        pltpu.with_memory_space_constraint(array, pltpu.HBM) if array.size > 2 else array for array in hbm
+        pltpu.with_memory_space_constraint(array, pltpu.HBM) for array in hbm
     ]
     return pl.pallas_call(
         kernel,
@@ -433,21 +498,35 @@
     tile, sent_shape = (TX, TY, TZ), ((DEVICES, 1, 128), F32)
     listed = [((1, RECEIVERS), I32), ((2, RECEIVERS), F32)]
     fields = (source_now, receiver_now, source_next, receiver_next, courant, strip_depth, strip_values)
-    up_y, down_y, near_cells, near_traces = call(
-        pack_y_kernel,
-        [((113, 8, 128), F32), ((113, 8, 128), F32), *listed],
+    up_y, down_y, near_cells, near_traces, near_wavelet = call(
+        pack_kernel,
+        [((113, 8, 128), F32)] * 2 + [*listed, ((1, 2), F32)],
         [],
-        hbm=[cells, receiver_traces, *fields],
+        hbm=[cells, receiver_traces, wavelet.reshape(1, 2), *fields],
         scratch=[pltpu.VMEM(tile, F32)] * 3
-        + [pltpu.VMEM((8, 32), I32), pltpu.VMEM((2, 4, 8, 32), F32), pltpu.SemaphoreType.DMA((11,))],
+        + [pltpu.VMEM((8, 32), I32), pltpu.VMEM((2, 4, 8, 32), F32), pltpu.SemaphoreType.DMA((12,))],
     )
     before, after = both_ways(up_y, down_y, "gy")
     (sent,) = call(route_kernel, [sent_shape], [near_cells, near_traces], weight=20_000_000)
     got = lax.all_to_all(sent, ("gx", "gy"), 0, 0, tiled=True)
-    up_x, down_x = call(pack_x_kernel, [((38, 8, 128), F32)] * 2, [*fields, before, after, got])
+    got = jnp.maximum(got.reshape(DEVICES, 128), -jnp.finfo(F32).max)
+    up_x, down_x = call(pack_x_kernel, [((38, 8, 128), F32)] * 2, [*fields, before, after])
     left, right = both_ways(up_x, down_x, "gx")
+    inner, inner_courant = call(
+        inner_kernel,
+        [((2, 24, 16, 128), F32), ((24, 16, 128), F32)],
+        [near_wavelet, *fields, before, after],
+        scalars=[source_cell],
+        scratch=[
+            pltpu.VMEM((2, 32, 32, 128), F32),
+            pltpu.VMEM((3, 24, 16, 128), F32),
+            pltpu.VMEM((2, 24, 16, 128), F32),
+            pltpu.VMEM((16, 128), I32),
+            pltpu.VMEM((16, 128), F32),
+        ],
+    )
     sums = [((2, *tile), F32), (tile, F32), ((8, 8, 128), F32)]
-    own, rim_y, rim_x, rounds = call(collect_kernel, [*sums, ((1,), I32)], [got], out_scalars=1, weight=40_000_000)
+    own, rim_y, rim_x, rounds = call(collect_kernel, [*sums, ((1,), I32)], [got], out_scalars=1, weight=1000)
 
     def another(state):
         turn, *partial = state
@@ -468,19 +547,16 @@
     source_field, receiver_field, near, up, down = call(
         steps_kernel,
         [(tile, F32), (tile, F32), ((4, 32, 128), F32), ((4, 16, 128), F32), ((4, 16, 128), F32)],
-        [*fields, before, after, left, right, own, rim_y, rim_x],
-        hbm=[source_cell, wavelet],
+        [near_wavelet, *fields, before, after, left, right, inner, inner_courant, own, rim_y, rim_x],
+        scalars=[source_cell],
         scratch=[
-            pltpu.VMEM((2, 48, 32, 128), F32),
-            pltpu.VMEM((4, 40, 16, 128), F32),
+            pltpu.VMEM((2, 32, 32, 128), F32),
+            pltpu.VMEM((4, 16, 16, 128), F32),
             pltpu.VMEM((2, 40, 24, 128), F32),
-            pltpu.VMEM((2, 40, 16, 128), F32),
+            pltpu.VMEM((2, 16, 16, 128), F32),
             pltpu.VMEM((3, 16, 128), I32),
             pltpu.VMEM((3, 16, 128), F32),
-            pltpu.VMEM((4, 2, 40, 128), F32),
-            pltpu.SMEM((1,), I32),
-            pltpu.SMEM((2,), F32),
-            pltpu.SemaphoreType.DMA((2,)),
+            pltpu.VMEM((4, 2, 32, 128), F32),
         ],
     )
     near_left, near_right = both_ways(up, down, "gx")

time: 58.9 us -> 53.6 us (0.910); the launches traced: 57.8 us -> 53.3 us
  blocking collectives: 30.1 us -> 13.3 us
  starting transfers between devices: 7.97 us -> 18.6 us
  Pallas kernels: 9.68 us -> 11.2 us
  waiting for transfers between devices: 7.27 us -> 8.07 us
  local copies, waits for them, and re-layouts: 0.69 us -> 0.03 us
    all_to_all x1 -> x0, blocking collectives: 18.3 us -> none  [body(): got = lax.all_to_all(sent, ('gx', 'gy'), 0, 0, tiled=True)]
    all_to_all x0 -> x1, starting transfers between devices: none -> 10.7 us  [body(): got = lax.all_to_all(sent, ('gx', 'gy'), 0, 0, tiled=True)]
    all_to_all x0 -> x1, waiting for transfers between devices: none -> 3.9 us  [body(): got = lax.all_to_all(sent, ('gx', 'gy'), 0, 0, tiled=True)]
    ppermute x3, waiting for transfers between devices: 5.96 us -> 2.87 us  [both_ways(): lax.ppermute(to_last, axis, [((i + 1) % size, i) for i in range(size)])]
    pallas_call x7 -> x8, Pallas kernels: 9.68 us -> 11.2 us  [call(): pl.pallas_call(kernel, out_shape=[jax.ShapeDtypeStruct(shape, kind) for s...]
    all_to_all x1, blocking collectives: 11.8 us -> 13.3 us  [body(): angles = lax.all_to_all(angles, 'gy', 0, 0, tiled=True)]
    ppermute x3, starting transfers between devices: 5.74 us -> 5.05 us  [both_ways(): lax.ppermute(to_next, axis, [(i, (i + 1) % size) for i in range(size)])]
    unnamed x16 -> x14, local copies, waits for them, and re-layouts: 0.69 us -> 0.03 us
  transfers between devices with their start and end apart: 6 -> 7, of which waited for: 3 -> 3; matrix products, arithmetic and copies ran while one was open for 0% -> 0% of each run, Pallas kernels for 6% -> 10%
where the time goes in v3:
time: 53.6 us; the launch traced here: 53.3 us
  starting transfers between devices  18.6 us (35%)
  blocking collectives  13.3 us (25%)
  Pallas kernels  11.2 us (21%)
  waiting for transfers between devices  8.07 us (15%)
  between operations  1.46 us (3%)
  loops' own time  0.65 us (1%)
    all_to_all x1, blocking collectives, body(): angles = lax.all_to_all(angles, 'gy', 0, 0, tiled=True)  13.3 us
    pallas_call x8, Pallas kernels, call(): pl.pallas_call(kernel, out_shape=[jax.ShapeDtypeStruct(shape, kind) for s...  11.2 us
    all_to_all x1, starting transfers between devices, body(): got = lax.all_to_all(sent, ('gx', 'gy'), 0, 0, tiled=True)  10.7 us
    ppermute x3, starting transfers between devices, both_ways(): lax.ppermute(to_next, axis, [(i, (i + 1) % size) for i in range(size)])  5.05 us
    all_to_all x1, waiting for transfers between devices, body(): got = lax.all_to_all(sent, ('gx', 'gy'), 0, 0, tiled=True)  3.9 us
    ppermute x3, waiting for transfers between devices, both_ways(): lax.ppermute(to_last, axis, [((i + 1) % size, i) for i in range(size)])  2.87 us
    ppermute x3, starting transfers between devices, both_ways(): lax.ppermute(to_last, axis, [((i + 1) % size, i) for i in range(size)])  2.85 us
    ppermute x3, waiting for transfers between devices, both_ways(): lax.ppermute(to_next, axis, [(i, (i + 1) % size) for i in range(size)])  1.3 us
  transfers between devices with their start and end apart: 7, of which 3 were waited for; matrix products, arithmetic and copies ran while one was open for 0% of the time, Pallas kernels for 10%

profile of v3, /device:TPU:5, one launch (start us, length us, event | category | flops | bytes accessed | tf_op | source)
XLA Modules:
  0.0 53.3 jit_solution(12059334673189122447)
XLA Ops:
  0.7 1.4 %shard_map.130 = (f32[113,8,128]{2,1,0:T(8,128)S(1)}, f32[113,8,128]{2,1,0:T(8,128)S(1)}, s32[1,256]{1,0:T(1,128)S(1)}, f32[2,256]{1,0:T(2,128)S(1)}, f32[1,2]{1,0:T(1,128)S(1)}) custom-call(s32[1,256]{1,0:T(1,128)} %bitcast.11, f32[2,256]{1,0:T(2,128)} %traces.1, f32[1,2]{1,0:T(1,128)} %bitcast.13, f32[32,8,128]{2,1,0:T(8,128)} %s0.7, f32[32,8,128]{2,1,0:T(8,128)} %r0.7, ...), custom_call_target="tpu_custom_call" | custom-call | tf_op jit(solution)/shard_map/pallas_call | solution.py:466
  2.1 0.0 copy-start
  2.1 1.9 %collective-permute-start = (f32[113,8,128]{2,1,0:T(8,128)S(1)}, f32[113,8,128]{2,1,0:T(8,128)S(1)}, u32[]{:S(2)}, u32[]{:S(2)}) collective-permute-start(f32[113,8,128]{2,1,0:T(8,128)S(1)} %get-tuple-element.65), channel_id=1, source_target_pairs={{0,1},{1,2},{2,3},{3,4},{4,5},{5,6},{6,7},{7,8},{8,9},{9,10},{10,1... | collective-permute-start | bytes 1388552 | tf_op jit(solution)/shard_map/ppermute | solution.py:479
  4.1 0.0 collective-permute-start.1
  4.1 1.2 %shard_map.133 = f32[128,1,128]{2,1,0:T(1,128)} custom-call(s32[1,256]{1,0:T(1,128)S(1)} %get-tuple-element.71.cells_ref, f32[2,256]{1,0:T(2,128)S(1)} %get-tuple-element.72.traces_ref), custom_call_target="tpu_custom_call" | custom-call | bytes 20000000 | tf_op jit(solution)/shard_map/pallas_call | solution.py:466
  5.2 10.7 %all-to-all-start.1 = ((f32[128,1,128]{2,1,0:T(1,128)}), f32[128,1,128]{2,1,0:T(1,128)S(1)}, u32[]{:S(2)}, u32[]{:S(2)}) async-start(f32[128,1,128]{2,1,0:T(1,128)} %shard_map.133), calls=%async_computation.1 | async-start | bytes 131072 | tf_op jit(solution)/shard_map/all_to_all | solution.py:511
  16.6 0.0 collective-permute-done.before
  16.6 0.0 collective-permute-done.1.after
  16.7 0.1 shard_map.131
  16.8 1.3 %collective-permute-start.2 = (f32[38,8,128]{2,1,0:T(8,128)S(1)}, f32[38,8,128]{2,1,0:T(8,128)S(1)}, u32[]{:S(2)}, u32[]{:S(2)}) collective-permute-start(f32[38,8,128]{2,1,0:T(8,128)S(1)} %get-tuple-element.67), channel_id=1, source_target_pairs={{0,16},{16,32},{32,48},{48,64},{64,80},{80,96},{96,112},{112,0},{1... | collective-permute-start | bytes 466952 | tf_op jit(solution)/shard_map/ppermute | solution.py:479
  18.1 1.7 %collective-permute-start.3 = (f32[38,8,128]{2,1,0:T(8,128)S(1)}, f32[38,8,128]{2,1,0:T(8,128)S(1)}, u32[]{:S(2)}, u32[]{:S(2)}) collective-permute-start(f32[38,8,128]{2,1,0:T(8,128)S(1)} %get-tuple-element.68), channel_id=1, source_target_pairs={{16,0},{32,16},{48,32},{64,48},{80,64},{96,80},{112,96},{0,112},{1... | collective-permute-start | bytes 466952 | tf_op jit(solution)/shard_map/ppermute | solution.py:480
  19.8 3.9 %all-to-all-done.1 = f32[128,1,128]{2,1,0:T(1,128)S(1)} async-done(((f32[128,1,128]{2,1,0:T(1,128)}), f32[128,1,128]{2,1,0:T(1,128)S(1)}, u32[]{:S(2)}, u32[]{:S(2)}) %all-to-all-start.1) | async-done | bytes 65568 | tf_op jit(solution)/shard_map/all_to_all | solution.py:511
  23.7 2.7 %shard_map.134 = (f32[2,32,8,128]{3,2,1,0:T(8,128)}, f32[32,8,128]{2,1,0:T(8,128)S(1)}, f32[8,8,128]{2,1,0:T(8,128)S(1)}, s32[1]{0:T(128)}) custom-call(f32[128,128]{1,0:T(8,128)S(1)} %maximum_bitcast_fusion.got_ref), custom_call_target="tpu_custom_call" | custom-call | bytes 1000 | tf_op jit(solution)/shard_map/pallas_call | solution.py:466
  26.4 1.1 %shard_map.132 = (f32[2,24,16,128]{3,2,1,0:T(8,128)S(1)}, f32[24,16,128]{2,1,0:T(8,128)S(1)}) custom-call(s32[1]{0:T(128)S(6)} %copy.31.source_cell, f32[1,2]{1,0:T(1,128)S(1)} %get-tuple-element.64.wavelet, f32[32,8,128]{2,1,0:T(8,128)S(1)} %copy-done, f32[32,8,128]{2,1,0:T(8,128)S(1)} %copy-done.1, f32[32,8,128]{2,1,0:T(8,128)S(1)} %copy-done.2, ...), custom_call_target="tpu_custom_call" | custom-call | tf_op jit(solution)/shard_map/pallas_call | solution.py:466
  27.5 0.7 %while.14 = (s32[]{:T(128)}, f32[2,32,8,128]{3,2,1,0:T(8,128)}, f32[32,8,128]{2,1,0:T(8,128)S(1)}, f32[8,8,128]{2,1,0:T(8,128)S(1)}, s32[1]{0:T(128)}, /*index=5...) while((s32[]{:T(128)}, f32[2,32,8,128]{3,2,1,0:T(8,128)}, f32[32,8,128]{2,1,0:T(8,128)S(1)}, ...), condition=%wide.region_1.0_spmd, body=%wide.region_0.0_spmd.sunk | while | flops 3 | bytes 1048713 | solution.py:544
  28.2 0.0 collective-permute-done.3.right
  28.2 3.2 %shard_map.135 = (f32[32,8,128]{2,1,0:T(8,128)}, f32[32,8,128]{2,1,0:T(8,128)}, f32[4,32,128]{2,1,0:T(8,128)S(1)}, f32[4,16,128]{2,1,0:T(8,128)S(1)}, f32[4,16,128]{2,1,0:T(8,128)S(1)}) custom-call(s32[1]{0:T(128)S(6)} %copy.31.source_cell, f32[1,2]{1,0:T(1,128)S(1)} %get-tuple-element.64.wavelet, f32[32,8,128]{2,1,0:T(8,128)S(1)} %copy-done, ...), custom_call_target="tpu_custom_call" | custom-call | tf_op jit(solution)/shard_map/pallas_call | solution.py:466
  31.4 1.8 %collective-permute-start.4 = (f32[4,16,128]{2,1,0:T(8,128)S(1)}, f32[4,16,128]{2,1,0:T(8,128)S(1)}, u32[]{:S(2)}, u32[]{:S(2)}) collective-permute-start(f32[4,16,128]{2,1,0:T(8,128)S(1)} %get-tuple-element.83), channel_id=1, source_target_pairs={{0,16},{16,32},{32,48},{48,64},{64,80},{80,96},{96,112},{112,0},{1... | collective-permute-start | bytes 98312 | tf_op jit(solution)/shard_map/ppermute | solution.py:479
  33.2 1.2 %collective-permute-start.5 = (f32[4,16,128]{2,1,0:T(8,128)S(1)}, f32[4,16,128]{2,1,0:T(8,128)S(1)}, u32[]{:S(2)}, u32[]{:S(2)}) collective-permute-start(f32[4,16,128]{2,1,0:T(8,128)S(1)} %get-tuple-element.84), channel_id=1, source_target_pairs={{16,0},{32,16},{48,32},{64,48},{80,64},{96,80},{112,96},{0,112},{1... | collective-permute-start | bytes 98312 | tf_op jit(solution)/shard_map/ppermute | solution.py:480
  34.4 1.3 %collective-permute-done.4.left = f32[4,16,128]{2,1,0:T(8,128)S(1)} collective-permute-done((f32[4,16,128]{2,1,0:T(8,128)S(1)}, f32[4,16,128]{2,1,0:T(8,128)S(1)}, u32[]{:S(2)}, u32[]{:S(2)}) %collective-permute-start.4) | collective-permute-done | bytes 32800 | tf_op jit(solution)/shard_map/ppermute | solution.py:479
  35.7 2.9 %collective-permute-done.5.right = f32[4,16,128]{2,1,0:T(8,128)S(1)} collective-permute-done((f32[4,16,128]{2,1,0:T(8,128)S(1)}, f32[4,16,128]{2,1,0:T(8,128)S(1)}, u32[]{:S(2)}, u32[]{:S(2)}) %collective-permute-start.5) | collective-permute-done | bytes 32800 | tf_op jit(solution)/shard_map/ppermute | solution.py:480
  38.5 0.7 %shard_map.136 = f32[16,8,128]{2,1,0:T(8,128)S(1)} custom-call(f32[4,32,128]{2,1,0:T(8,128)S(1)} %get-tuple-element.82.near, f32[4,16,128]{2,1,0:T(8,128)S(1)} %collective-permute-done.4.left, f32[4,16,128]{2,1,0:T(8,128)S(1)} %collective-permute-done.5.right), custom_call_target="tpu_custom_call" | custom-call | tf_op jit(solution)/shard_map/pallas_call | solution.py:466
  39.3 13.3 %all_to_all.16.got = f32[16,8,128]{2,1,0:T(8,128)S(1)} all-to-all(f32[16,8,128]{2,1,0:T(8,128)S(1)} %shard_map.136), channel_id=1, replica_groups=mesh['gx'=8,'gy'=16] {'gy'}, dimensions={0} | all-to-all | bytes 131072 | tf_op jit(solution)/shard_map/all_to_all | solution.py:567
  52.6 0.7 %shard_map.137 = f32[2,8,1024]{2,1,0:T(8,128)} custom-call(f32[16,8,128]{2,1,0:T(8,128)S(1)} %all_to_all.16.got), custom_call_target="tpu_custom_call" | custom-call | tf_op jit(solution)/shard_map/pallas_call | solution.py:466
  (15 shorter events, 0.0 us)
Async XLA Ops:
  0.6 16.0 %copy-start.1 = (f32[32,8,128]{2,1,0:T(8,128)S(1)}, f32[32,8,128]{2,1,0:T(8,128)}, u32[]{:S(2)}) copy-start(f32[32,8,128]{2,1,0:T(8,128)} %r0.7) | copy-start | bytes 393220
  0.6 16.0 %copy-start.2 = (f32[32,8,128]{2,1,0:T(8,128)S(1)}, f32[32,8,128]{2,1,0:T(8,128)}, u32[]{:S(2)}) copy-start(f32[32,8,128]{2,1,0:T(8,128)} %sm.7) | copy-start | bytes 393220
  0.7 16.0 %copy-start.3 = (f32[32,8,128]{2,1,0:T(8,128)S(1)}, f32[32,8,128]{2,1,0:T(8,128)}, u32[]{:S(2)}) copy-start(f32[32,8,128]{2,1,0:T(8,128)} %rm.7) | copy-start | bytes 393220
  0.7 16.0 %copy-start.4 = (f32[32,8,128]{2,1,0:T(8,128)S(1)}, f32[32,8,128]{2,1,0:T(8,128)}, u32[]{:S(2)}) copy-start(f32[32,8,128]{2,1,0:T(8,128)} %c.7) | copy-start | bytes 393220
  2.1 14.5 %copy-start = (f32[32,8,128]{2,1,0:T(8,128)S(1)}, f32[32,8,128]{2,1,0:T(8,128)}, u32[]{:S(2)}) copy-start(f32[32,8,128]{2,1,0:T(8,128)} %s0.7) | copy-start | bytes 393220
  2.1 14.5 %collective-permute-start = (f32[113,8,128]{2,1,0:T(8,128)S(1)}, f32[113,8,128]{2,1,0:T(8,128)S(1)}, u32[]{:S(2)}, u32[]{:S(2)}) collective-permute-start(f32[113,8,128]{2,1,0:T(8,128)S(1)} %get-tuple-element.65), channel_id=1, source_target_pairs={{0,1},{1,2},{2,3},{3,4},{4,5},{5,6},{6,7},{7,8},{8,9},{9,10},{10,1... | collective-permute-start | bytes 1388552 | tf_op jit(solution)/shard_map/ppermute | solution.py:479
  4.1 12.5 %collective-permute-start.1 = (f32[113,8,128]{2,1,0:T(8,128)S(1)}, f32[113,8,128]{2,1,0:T(8,128)S(1)}, u32[]{:S(2)}, u32[]{:S(2)}) collective-permute-start(f32[113,8,128]{2,1,0:T(8,128)S(1)} %get-tuple-element.66), channel_id=1, source_target_pairs={{1,0},{2,1},{3,2},{4,3},{5,4},{6,5},{7,6},{8,7},{9,8},{10,9},{11,1... | collective-permute-start | bytes 1388552 | tf_op jit(solution)/shard_map/ppermute | solution.py:480
  5.2 11.4 %copy-start.5 = (f32[2,4,8,32]{3,2,1,0:T(8,128)S(1)}, f32[2,4,8,32]{3,2,1,0:T(8,128)}, u32[]{:S(2)}) copy-start(f32[2,4,8,32]{3,2,1,0:T(8,128)} %values.7) | copy-start | bytes 24580
  5.2 11.4 %copy-start.6 = (s32[8,32]{1,0:T(8,128)S(1)}, s32[8,32]{1,0:T(8,128)}, u32[]{:S(2)}) copy-start(s32[8,32]{1,0:T(8,128)} %depth.7) | copy-start | bytes 3076
  5.2 18.4 %all-to-all-start.1 = ((f32[128,1,128]{2,1,0:T(1,128)}), f32[128,1,128]{2,1,0:T(1,128)S(1)}, u32[]{:S(2)}, u32[]{:S(2)}) async-start(f32[128,1,128]{2,1,0:T(1,128)} %shard_map.133), calls=%async_computation.1 | async-start | bytes 131072 | tf_op jit(solution)/shard_map/all_to_all | solution.py:511
  16.8 11.4 %collective-permute-start.2 = (f32[38,8,128]{2,1,0:T(8,128)S(1)}, f32[38,8,128]{2,1,0:T(8,128)S(1)}, u32[]{:S(2)}, u32[]{:S(2)}) collective-permute-start(f32[38,8,128]{2,1,0:T(8,128)S(1)} %get-tuple-element.67), channel_id=1, source_target_pairs={{0,16},{16,32},{32,48},{48,64},{64,80},{80,96},{96,112},{112,0},{1... | collective-permute-start | bytes 466952 | tf_op jit(solution)/shard_map/ppermute | solution.py:479
  18.1 10.1 %collective-permute-start.3 = (f32[38,8,128]{2,1,0:T(8,128)S(1)}, f32[38,8,128]{2,1,0:T(8,128)S(1)}, u32[]{:S(2)}, u32[]{:S(2)}) collective-permute-start(f32[38,8,128]{2,1,0:T(8,128)S(1)} %get-tuple-element.68), channel_id=1, source_target_pairs={{16,0},{32,16},{48,32},{64,48},{80,64},{96,80},{112,96},{0,112},{1... | collective-permute-start | bytes 466952 | tf_op jit(solution)/shard_map/ppermute | solution.py:480
  31.4 4.3 %collective-permute-start.4 = (f32[4,16,128]{2,1,0:T(8,128)S(1)}, f32[4,16,128]{2,1,0:T(8,128)S(1)}, u32[]{:S(2)}, u32[]{:S(2)}) collective-permute-start(f32[4,16,128]{2,1,0:T(8,128)S(1)} %get-tuple-element.83), channel_id=1, source_target_pairs={{0,16},{16,32},{32,48},{48,64},{64,80},{80,96},{96,112},{112,0},{1... | collective-permute-start | bytes 98312 | tf_op jit(solution)/shard_map/ppermute | solution.py:479
  33.2 5.4 %collective-permute-start.5 = (f32[4,16,128]{2,1,0:T(8,128)S(1)}, f32[4,16,128]{2,1,0:T(8,128)S(1)}, u32[]{:S(2)}, u32[]{:S(2)}) collective-permute-start(f32[4,16,128]{2,1,0:T(8,128)S(1)} %get-tuple-element.84), channel_id=1, source_target_pairs={{16,0},{32,16},{48,32},{64,48},{80,64},{96,80},{112,96},{0,112},{1... | collective-permute-start | bytes 98312 | tf_op jit(solution)/shard_map/ppermute | solution.py:480

commit v4 on v3

v4 whole, which is shorter than its diff:
```python
import math

import jax
import jax.numpy as jnp
import numpy as np
from jax import lax
from jax.experimental import pallas as pl
from jax.experimental.pallas import tpu as pltpu
from jax.sharding import PartitionSpec as P

COEFS = (-205.0 / 72.0, 8.0 / 5.0, -1.0 / 5.0, 8.0 / 315.0, -1.0 / 560.0)
SLOPES = np.array(
    [math.tan(math.pi * (-60.0 + 120.0 * (angle + 0.5) / 32.0) / 180.0) for angle in range(32)],
    dtype=np.float32,
)
GX, GY = 8, 16
TX, TY, TZ = 32, 8, 128
DEVICES = GX * GY
RECEIVERS = 256
SLOTS = 16
F32, BF16, I32 = jnp.float32, jnp.bfloat16, jnp.int32
VMEM_LIMIT = 24 * 1024 * 1024


def iota(shape, dim):
    return lax.broadcasted_iota(I32, shape, dim)


def halves(value):
    high = value.astype(BF16)
    return high, (value - high.astype(F32)).astype(BF16)


def dot_nt(left, right):
    return lax.dot_general(left, right, (((1,), (1,)), ((), ())), preferred_element_type=F32)


def routed(cells, traces, first_slot):
    x, y, z = cells >> 14, (cells >> 7) & 127, cells & 127
    tile_x, tile_y, in_x, in_y = x >> 5, y >> 3, x & 31, y & 7
    beside_y = jnp.where(in_y < 4, tile_y - 1, tile_y + 1)
    beside_x = jnp.where(in_x < 4, tile_x - 1, jnp.where(in_x >= 28, tile_x + 1, -1))
    to_y = jnp.where((beside_y >= 0) & (beside_y < GY), tile_x * GY + beside_y, -1)
    to_x = jnp.where((beside_x >= 0) & (beside_x < GX), beside_x * GY + tile_y, -1)
    rim_x = jnp.where(in_x < 4, in_x + 4, in_x - 28)
    classes = (
        (tile_x * GY + tile_y, (in_x * 8 + in_y) * 128 + z, 2),
        (to_y, (in_x * 8 + (in_y ^ 4)) * 128 + z, 1),
        (to_x, (rim_x * 8 + in_y) * 128 + z, 1),
    )
    earlier = jnp.where(
        iota((RECEIVERS, RECEIVERS), 0) < iota((RECEIVERS, RECEIVERS), 1), 1.0, 0.0
    ).astype(BF16)
    device = iota((DEVICES, RECEIVERS), 0)
    slot = iota((SLOTS, RECEIVERS), 0).astype(F32) + first_slot.astype(F32)
    hits, kept, last_rank, row = [], [], None, 0
    for target, place, steps in classes:
        hit = jnp.where(device == target, 1.0, 0.0)
        before = jnp.dot(hit.astype(BF16), earlier, preferred_element_type=F32)
        rank = jnp.sum(hit * before, axis=0, keepdims=True)
        last_rank = rank if last_rank is None else jnp.maximum(last_rank, rank)
        mine = slot == rank
        rows = [jnp.where(mine, place.astype(F32), 0.0)]
        rows += [jnp.where(mine, traces[s : s + 1], 0.0) for s in range(steps)]
        size = SLOTS * len(rows)
        above = [jnp.zeros((row, RECEIVERS), F32)] if row else []
        below = [jnp.zeros((128 - row - size, RECEIVERS), F32)]
        kept.append(jnp.concatenate(above + rows + below, axis=0))
        hits.append(hit.astype(BF16))
        row += size
    hits = jnp.concatenate(hits, axis=1)
    high, low = halves(jnp.concatenate(kept, axis=1))
    sent = dot_nt(hits, high) + dot_nt(hits, low)
    rounds = (jnp.max(last_rank, axis=1, keepdims=True).astype(I32) // SLOTS + 1).astype(F32)
    return jnp.where(iota((DEVICES, 128), 1) >= row, rounds, sent)


def route_more_kernel(first_ref, cells, traces, sent_ref, cells_v, traces_v, sems):
    for copy in started([(cells, cells_v), (traces, traces_v)], sems):
        copy.wait()
    sent_ref[:, 0, :] = routed(cells_v[...], traces_v[...], first_ref[0])


def collected(got):
    rows = got.T
    sums, row = [], 0
    down = iota((TZ, DEVICES), 0).astype(F32).astype(BF16)
    unit, zero = jnp.ones((), BF16), jnp.zeros((), BF16)
    for columns, steps in ((TX * 8, 2), (TX * 8, 1), (64, 1)):
        cell = rows[row : row + SLOTS].astype(I32)
        column, depth = (cell >> 7).astype(F32), (cell & 127).astype(F32)
        at = iota((columns, DEVICES), 0).astype(F32).astype(BF16)
        one, parts = [], [[] for _ in range(2 * steps)]
        for k in range(SLOTS):
            one.append(jnp.where(at == column[k : k + 1].astype(BF16), unit, zero))
            same = down == depth[k : k + 1].astype(BF16)
            for s in range(steps):
                value = rows[row + (s + 1) * SLOTS + k : row + (s + 1) * SLOTS + k + 1]
                high, low = halves(value)
                parts[2 * s].append(jnp.where(same, high, zero))
                parts[2 * s + 1].append(jnp.where(same, low, zero))
        one = jnp.concatenate(one, axis=1)
        both = dot_nt(one, jnp.concatenate([jnp.concatenate(part, axis=1) for part in parts], axis=0))
        for s in range(steps):
            sums.append(both[:, 256 * s : 256 * s + 128] + both[:, 256 * s + 128 : 256 * s + 256])
        row += SLOTS * (steps + 1)
    return sums


def collect_kernel(got_ref, inner_courant, own_ref, rim_y_ref, rim_x_ref, rounds_ref):
    got = got_ref[...]
    own_0, own_1, rim_y, rim_x = collected(got)
    own_ref[0] = own_0.reshape(TX, 8, 128)
    own_ref[1] = own_1.reshape(TX, 8, 128)
    rim_y_ref[...] = rim_y.reshape(TX, 8, 128)
    rim_x_ref[...] = rim_x.reshape(8, 8, 128)
    rounds_ref[0] = jnp.max(got[:, 112:128]).astype(I32)


def collect_more_kernel(got_ref, own_in, rim_y_in, rim_x_in, own_ref, rim_y_ref, rim_x_ref):
    own_0, own_1, rim_y, rim_x = collected(got_ref[:, 0, :])
    own_ref[0] = own_in[0] + own_0.reshape(TX, 8, 128)
    own_ref[1] = own_in[1] + own_1.reshape(TX, 8, 128)
    rim_y_ref[...] = rim_y_in[...] + rim_y.reshape(TX, 8, 128)
    rim_x_ref[...] = rim_x_in[...] + rim_x.reshape(8, 8, 128)


def strip_values_tile(values, step, rows):
    return jnp.concatenate([values[step, layer][rows] for layer in range(4)], axis=1)


def wide(depth):
    return jnp.concatenate([depth, jnp.zeros((depth.shape[0], 96), depth.dtype)], axis=1)


def started(copies, sems):
    copies = [pltpu.make_async_copy(*ends, sems.at[k]) for k, ends in enumerate(copies)]
    for copy in copies:
        copy.start()
    return copies


def pack_kernel(
    cells, traces, wavelet, s0, r0, sm, rm, c, depth, values,
    up_y, down_y, wavelet_ref, sm_v, rm_v, c_v, depth_v, values_v, sent_ref,
    sent_v, cells_v, traces_v, sems,
):
    copies = started(
        [
            (cells, cells_v), (traces, traces_v), (depth, depth_v), (values, values_v), (wavelet, wavelet_ref),
            (sm, sm_v), (rm, rm_v), (c, c_v),
            (s0, up_y.at[0:32]), (r0, up_y.at[32:64]), (s0, down_y.at[0:32]), (r0, down_y.at[32:64]),
        ],
        sems,
    )
    for copy in copies[:2]:
        copy.wait()
    sent_v[:, 0, :] = routed(cells_v[...], traces_v[...], jnp.int32(0))
    out = pltpu.make_async_copy(sent_v, sent_ref, sems.at[12])
    out.start()
    for copy in copies[2:8]:
        copy.wait()
    for ref, rows in ((up_y, slice(4, 8)), (down_y, slice(0, 4))):
        ref[64:96, 0:4] = sm_v[:, rows]
        ref[64:96, 4:8] = rm_v[:, rows]
        ref[96:112, 0:4] = c_v[0:16, rows]
        ref[96:112, 4:8] = c_v[16:32, rows]
        ref[112, 0:4] = strip_values_tile(values_v, 0, rows)
        ref[112, 4:8] = wide(depth_v[rows].astype(F32))
    for copy in copies[8:]:
        copy.wait()
    out.wait()


def depth_matrix():
    apart = jnp.abs(iota((TZ, TZ), 0) - iota((TZ, TZ), 1))
    weights = jnp.zeros((TZ, TZ), F32)
    for reach in range(1, 5):
        weights = jnp.where(apart == reach, COEFS[reach], weights)
    high, low = halves(weights)
    top = jnp.concatenate([high, low], axis=1)
    return jnp.concatenate([top, jnp.concatenate([high, jnp.zeros_like(low)], axis=1)], axis=0)


def depth_sums(rows, matrix):
    both = jnp.dot(jnp.concatenate(halves(rows), axis=1), matrix, preferred_element_type=F32)
    return both[:, :128] + both[:, 128:]


def curvature(ref, f, x, row, depth_sum):
    tile = ref[f, x, row : row + 8]
    total = (3.0 * COEFS[0]) * tile + depth_sum
    for reach in range(1, 5):
        pairs = ref[f, x + reach, row : row + 8] + ref[f, x - reach, row : row + 8]
        pairs = pairs + ref[f, x, row + reach : row + reach + 8]
        pairs = pairs + ref[f, x, row - reach : row - reach + 8]
        total = total + COEFS[reach] * pairs
    return tile, total


def overwritten(tile, depths, values, lane_start):
    lane = iota((8, 128), 1)
    column = jnp.full((8, 128), lane_start, I32)
    relative = lane - jnp.take_along_axis(depths, column, axis=1)
    fill = jnp.take_along_axis(values, (relative & 3) * 32 + column, axis=1)
    return jnp.where((relative >= 0) & (relative < 4), fill, tile)


def keeps(axis, size):
    at = lax.axis_index(axis)
    return jnp.where(at > 0, 1.0, 0.0), jnp.where(at < size - 1, 1.0, 0.0)


def pulse(source_cell, wavelet, step, row):
    cell = source_cell[0]
    lane, sublane = iota((8, 128), 1), iota((8, 128), 0)
    at_row = sublane + (row + lax.axis_index("gy") * TY) == (cell >> 7) & 127
    return jnp.where((lane == cell & 127) & at_row, wavelet[0:1, step : step + 1], 0.0)


def source_layer(source_cell):
    return (source_cell[0] >> 14) - lax.axis_index("gx") * TX


def advanced(i, at, x, e_ref, z_ref, m_ref, courant_ref, depth_ref, v_ref, pulses, source_x, new_ref):
    for t in range(2):
        rows = slice(8 * t, 8 * t + 8)
        courant = courant_ref[i, rows]
        now, total = curvature(e_ref, 0, at, 8 + 8 * t, z_ref[0, i, rows])
        if pulses is not None:
            total = total - jnp.where(x == source_x, pulses[t], 0.0)
        new = 2.0 * now - m_ref[0, i, rows] + courant * total
        new_ref[0, i, rows] = overwritten(new, depth_ref[rows], v_ref[rows], x)
        now, total = curvature(e_ref, 1, at, 8 + 8 * t, z_ref[1, i, rows])
        new_ref[1, i, rows] = 2.0 * now - m_ref[1, i, rows] + courant * total


def edge_kernel(
    own_y, sm, rm, c, depth, values, before, after,
    new_ref, courant_ref, depth_ref, v_ref, up_ref, down_ref,
    e_ref, m_ref, z_ref,
):
    keep_before, keep_after = keeps("gy", GY)
    for f in range(2):
        e_ref[f, 0:4, 8:24] = jnp.zeros((4, 16, 128), F32)
        e_ref[f, 20:24, 8:24] = jnp.zeros((4, 16, 128), F32)
        for to, first in ((4, 0), (12, 24)):
            start = 32 * f + first
            e_ref[f, to : to + 8, 12:20] = own_y[start : start + 8]
            e_ref[f, to : to + 8, 4:12] = before[start : start + 8] * keep_before
            e_ref[f, to : to + 8, 20:28] = after[start : start + 8] * keep_after
    v_ref[4:12] = strip_values_tile(values, 0, slice(0, 8))
    depth_ref[4:12] = wide(depth[...])
    for to, first in ((0, 0), (4, 28)):
        layers = slice(to, to + 4)
        m_ref[0, layers, 4:12] = sm[first : first + 4]
        m_ref[1, layers, 4:12] = rm[first : first + 4]
        courant_ref[layers, 4:12] = c[first : first + 4]
    for ref, keep, rows in ((before, keep_before, slice(0, 4)), (after, keep_after, slice(12, 16))):
        for to, first in ((0, 0), (4, 28)):
            layers, half = slice(to, to + 4), first // 16
            m_ref[0, layers, rows] = ref[64 + first : 68 + first, 0:4] * keep
            m_ref[1, layers, rows] = ref[64 + first : 68 + first, 4:8] * keep
            start = 96 + first - 16 * half
            courant_ref[layers, rows] = ref[start : start + 4, 4 * half : 4 * half + 4] * keep
        v_ref[rows] = ref[112, 0:4] * keep
        depth_ref[rows] = (ref[112, 4:8] * keep).astype(I32)
    matrix = depth_matrix()
    for f in range(2):
        for half in range(2):
            rows = e_ref[f, 4 + 12 * half : 8 + 12 * half, 8:24].reshape(64, 128)
            z_ref[f, 4 * half : 4 * half + 4] = depth_sums(rows, matrix).reshape(4, 16, 128)
    for i in range(8):
        at, x = (i + 4, i) if i < 4 else (i + 12, i + 24)
        advanced(
            i, at, x, e_ref, z_ref, m_ref, courant_ref, depth_ref, v_ref, None, None, new_ref
        )
    for ref, to, rim, at in ((up_ref, 4, 28, 16), (down_ref, 0, 0, 4)):
        for f in range(2):
            ref[4 * f : 4 * f + 4] = new_ref[f, to : to + 4, 4:12]
            ref[12 + 4 * f : 16 + 4 * f] = own_y[32 * f + rim : 32 * f + rim + 4]
            ref[20 + 4 * f : 24 + 4 * f, 0:4] = e_ref[f, at : at + 4, 8:12]
            ref[20 + 4 * f : 24 + 4 * f, 4:8] = e_ref[f, at : at + 4, 20:24]
        ref[8:12] = c[rim : rim + 4]
        ref[28] = depth_ref[4:12].astype(F32)


def inner_kernel(
    source_cell,
    wavelet, own_y, sm, rm, c, before, after, depths, values,
    new_ref, courant_ref,
    e_ref, m_ref, z_ref,
):
    keep_before, keep_after = keeps("gy", GY)
    for f in range(2):
        fields = slice(32 * f, 32 * f + 32)
        e_ref[f, :, 12:20] = own_y[fields]
        e_ref[f, :, 4:12] = before[fields] * keep_before
        e_ref[f, :, 20:28] = after[fields] * keep_after
    m_ref[0, :, 4:12] = sm[4:28]
    m_ref[1, :, 4:12] = rm[4:28]
    courant_ref[:, 4:12] = c[4:28]
    for ref, keep, rows in ((before, keep_before, slice(0, 4)), (after, keep_after, slice(12, 16))):
        m_ref[0, :, rows] = ref[68:92, 0:4] * keep
        m_ref[1, :, rows] = ref[68:92, 4:8] * keep
        courant_ref[0:12, rows] = ref[100:112, 0:4] * keep
        courant_ref[12:24, rows] = ref[96:108, 4:8] * keep
    pulses = [pulse(source_cell, wavelet, 0, 8 * t - 4) for t in range(2)]
    source_x = source_layer(source_cell)
    matrix = depth_matrix()
    for f in range(2):
        rows = e_ref[f, 4:28, 8:24].reshape(384, 128)
        z_ref[f] = depth_sums(rows, matrix).reshape(24, 16, 128)

    def layer(i, carry):
        advanced(
            i, i + 4, i + 4, e_ref, z_ref, m_ref, courant_ref, depths, values, pulses, source_x, new_ref
        )
        return carry

    lax.fori_loop(0, 24, layer, 0, unroll=8)


def unless_strip(depths, column, amount):
    relative = iota((8, 128), 1) - depths[:, column : column + 1]
    return jnp.where((relative >= 0) & (relative < 4), 0.0, amount)


def steps_kernel(
    source_cell,
    wavelet, own_y, c, depth, values, left, right, edge, edge_courant, inner, inner_courant, depths,
    own, rim_y, rim_x,
    s_out, r_out, near_ref, up_ref, down_ref,
    o_ref, h_ref, z_ref, sub_ref, s_v, r_v, sems,
):
    keep_left, keep_right = keeps("gx", GX)
    s0, r0 = own_y.at[0:32], own_y.at[32:64]
    for new1, courant, start, first, size in (
        (edge, edge_courant, 0, 0, 4), (inner, inner_courant, 0, 4, 24), (edge, edge_courant, 4, 28, 4)
    ):
        to, part, x = slice(first + 4, first + 4 + size), slice(start, start + size), slice(first, first + size)
        o_ref[0, to, 4:20] = new1[0, part]
        o_ref[1, to, 8:16] = new1[1, part, 4:12] + courant[part, 4:12] * own[0, x]
        o_ref[1, to, 4:8] = new1[1, part, 0:4] + courant[part, 0:4] * rim_y[x, 0:4]
        o_ref[1, to, 16:20] = new1[1, part, 12:16] + courant[part, 12:16] * rim_y[x, 4:8]
    source_x = source_layer(source_cell)
    pulses = [pulse(source_cell, wavelet, 0, row) for row in (-4, 4, 0)]
    for side, ref, keep in ((0, left, keep_left), (1, right, keep_right)):
        beyond_depths = (ref[28] * keep).astype(I32)
        for f in range(2):
            h_ref[f, side, :, 4:12] = ref[12 + 4 * f : 16 + 4 * f] * keep
            h_ref[f, side, :, 0:4] = ref[20 + 4 * f : 24 + 4 * f, 0:4] * keep
            h_ref[f, side, :, 12:16] = ref[20 + 4 * f : 24 + 4 * f, 4:8] * keep
        for n in range(4):
            x = 31 - n if side else n
            for f in range(2):
                for t in range(2):
                    rows = slice(8 * t, 8 * t + 8)
                    amount = None
                    for reach in range(n + 1, 5):
                        away = reach - n
                        term = COEFS[reach] * h_ref[f, side, away - 1 if side else 4 - away, rows]
                        amount = term if amount is None else amount + term
                    if f == 0:
                        amount = amount - jnp.where(x == source_x, pulses[t], 0.0)
                    amount = edge_courant[x - 24 if side else x, rows] * amount
                    if f == 0:
                        amount = unless_strip(depths[rows], x, amount)
                    at = slice(4 + 8 * t, 12 + 8 * t)
                    o_ref[f, x + 4, at] = o_ref[f, x + 4, at] + amount
            k = n if side else 3 - n
            for f, field in ((0, s0), (1, r0)):
                amount = None
                for reach in range(n + 1, 5):
                    inward = reach - n - 1
                    term = COEFS[reach] * field[31 - inward if side else inward]
                    amount = term if amount is None else amount + term
                if f == 0:
                    beyond = 32 + n if side else -1 - n
                    amount = amount - jnp.where(beyond == source_x, pulses[2], 0.0)
                else:
                    amount = amount + rim_x[4 * side + k]
                amount = ref[8 + k] * amount
                if f == 0:
                    amount = unless_strip(beyond_depths, k if side else 28 + k, amount)
                o_ref[f, 36 + n if side else 3 - n, 8:16] = (ref[4 * f + k] + amount) * keep
    matrix = depth_matrix()
    for f in range(2):
        rows = o_ref[f, 4:36, 8:16].reshape(256, 128)
        z_ref[f] = depth_sums(rows, matrix).reshape(32, 8, 128)
    late_values = strip_values_tile(values, 1, slice(0, 8))
    near_depth = wide(depth[...])
    late_pulse = pulse(source_cell, wavelet, 1, 0)

    def second(x, carry):
        now, total = curvature(o_ref, 0, x + 4, 8, z_ref[0, x])
        total = total - jnp.where(x == source_x, late_pulse, 0.0)
        new = 2.0 * now - s0[x] + c[x] * total
        new = overwritten(new, near_depth, late_values, x)
        s_v[x] = new
        for j in range(2):
            sub_ref[0, j, pl.ds(x, 1)] = now[4 * j : 4 * j + 1]
            sub_ref[1, j, pl.ds(x, 1)] = new[4 * j : 4 * j + 1]
        now, total = curvature(o_ref, 1, x + 4, 8, z_ref[1, x])
        new = 2.0 * now - r0[x] + c[x] * (total + own[1, x])
        r_v[x] = new
        for j in range(2):
            sub_ref[2, j, pl.ds(x, 1)] = now[4 * j : 4 * j + 1]
            sub_ref[3, j, pl.ds(x, 1)] = new[4 * j : 4 * j + 1]
        return carry

    lax.fori_loop(0, 32, second, 0, unroll=16)
    copies = started([(s_v, s_out), (r_v, r_out)], sems)
    z, to = iota((TZ, 128), 0), iota((TZ, 128), 1)
    totals = []
    for k in range(4):
        total = None
        for j in range(2):
            pick = jnp.where((z & 3 == 0) & (to == (z >> 2) + (16 + 64 * j)), 1.0, 0.0)
            part = jnp.dot(
                sub_ref[k, j], pick, precision=lax.Precision.HIGHEST, preferred_element_type=F32
            )
            total = part if total is None else total + part
        near_ref[k] = total
        totals.append(total)
    for f in range(2):
        packed = totals[2 * f] + pltpu.roll(totals[2 * f + 1], 32, 1)
        up_ref[f] = packed[16:32]
        down_ref[f] = packed[0:16]
    for copy in copies:
        copy.wait()


def angles_kernel(near, left, right, out_ref, g_ref):
    keep_left, keep_right = keeps("gx", GX)
    lane = iota((16, 128), 1)
    held = ((lane >= 16) & (lane < 48)) | ((lane >= 80) & (lane < 112))
    for f in range(2):
        for ref, keep, rows in ((left, keep_left, slice(0, 16)), (right, keep_right, slice(48, 64))):
            packed = ref[f] * keep
            g_ref[2 * f, rows] = jnp.where(held, packed, 0.0)
            g_ref[2 * f + 1, rows] = jnp.where(held, pltpu.roll(packed, 96, 1), 0.0)
    for k in range(4):
        g_ref[k, 16:48] = near[k]
    sums = [None] * 32
    for lag in range(-16, 17):
        product = None
        for step in range(2):
            source = g_ref[step, pl.ds(16 - lag, 8, stride=4)]
            receiver = g_ref[2 + step, pl.ds(16 + lag, 8, stride=4)]
            part = source * receiver
            product = part if product is None else product + part
        shifted = {}

        def shift(amount):
            if amount not in shifted:
                shifted[amount] = product if amount == 0 else pltpu.roll(product, -amount % 128, 1)
            return shifted[amount]

        for a in range(32):
            move = np.float32(lag) * SLOPES[a] / np.float32(4.0)
            low = np.floor(move)
            frac = float(move - low)
            term = shift(int(low)) * (1.0 - frac)
            if frac != 0.0:
                term = term + shift(int(low) + 1) * frac
            sums[a] = term if sums[a] is None else sums[a] + term
    lane = iota((8, 128), 1)
    for b in range(16):
        first, second = sums[2 * b], sums[2 * b + 1]
        packed = jnp.where(lane < 32, pltpu.roll(first, 112, 1), pltpu.roll(first, 80, 1))
        other = jnp.where(lane < 96, pltpu.roll(second, 48, 1), pltpu.roll(second, 16, 1))
        out_ref[b] = jnp.where(lane < 64, packed, other)


def arrange_kernel(got, out_ref):
    lane = iota((8, 128), 1)
    for t in range(8):
        even, odd = got[2 * t], got[2 * t + 1]
        out_ref[0, :, 128 * t : 128 * t + 128] = jnp.where(lane < 64, even, pltpu.roll(odd, 64, 1))
        out_ref[1, :, 128 * t : 128 * t + 128] = jnp.where(lane < 64, pltpu.roll(even, 64, 1), odd)


def call(kernel, outs, arrays, scalars=(), hbm=(), out_scalars=0, out_hbm=(), scratch=(), weight=0):
    smem, vmem = pl.BlockSpec(memory_space=pltpu.SMEM), pl.BlockSpec(memory_space=pltpu.VMEM)
    far = pl.BlockSpec(memory_space=pltpu.HBM)
    hbm = [
        pltpu.with_memory_space_constraint(array, pltpu.HBM) for array in hbm
    ]
    return pl.pallas_call(
        kernel,
        out_shape=[jax.ShapeDtypeStruct(shape, kind) for shape, kind in outs],
        in_specs=[smem] * len(scalars) + [far] * len(hbm) + [vmem] * len(arrays),
        out_specs=[
            smem if k >= len(outs) - out_scalars else far if k in out_hbm else vmem for k in range(len(outs))
        ],
        scratch_shapes=list(scratch),
        compiler_params=pltpu.CompilerParams(vmem_limit_bytes=VMEM_LIMIT),
        cost_estimate=pl.CostEstimate(flops=0, bytes_accessed=weight, transcendentals=0) if weight else None,
    )(*scalars, *hbm, *arrays)


def both_ways(to_next, to_last, axis):
    size = lax.axis_size(axis)
    from_last = lax.ppermute(to_next, axis, [(i, (i + 1) % size) for i in range(size)])
    from_next = lax.ppermute(to_last, axis, [((i + 1) % size, i) for i in range(size)])
    return from_last, from_next


def body(
    source_now,
    source_next,
    receiver_now,
    receiver_next,
    courant,
    source_cell,
    wavelet,
    receiver_cells,
    receiver_traces,
    strip_depth,
    strip_values,
):
    cells = receiver_cells.reshape(1, RECEIVERS)
    tile, sent_shape = (TX, TY, TZ), ((DEVICES, 1, 128), F32)
    listed = [((1, RECEIVERS), I32), ((2, RECEIVERS), F32)]
    fields = (source_now, receiver_now, source_next, receiver_next, courant, strip_depth, strip_values)
    up_y, down_y, near_wavelet, near_sm, near_rm, near_c, near_depth, near_values, sent = call(
        pack_kernel,
        [((113, 8, 128), F32)] * 2
        + [((1, 2), F32), *[(tile, F32)] * 3, ((8, 32), I32), ((2, 4, 8, 32), F32), sent_shape],
        [],
        hbm=[cells, receiver_traces, wavelet.reshape(1, 2), *fields],
        out_hbm=(8,),
        scratch=[pltpu.VMEM(*shape) for shape in (sent_shape, *listed)] + [pltpu.SemaphoreType.DMA((13,))],
    )
    before, after = both_ways(up_y, down_y, "gy")
    got = lax.all_to_all(sent, ("gx", "gy"), 0, 0, tiled=True)
    got = jnp.maximum(got.reshape(DEVICES, 128), -jnp.finfo(F32).max)
    edge, edge_courant, depths, strips, up_x, down_x = call(
        edge_kernel,
        [((2, 8, 16, 128), F32), ((8, 16, 128), F32), ((16, 128), I32), ((16, 128), F32)]
        + [((29, 8, 128), F32)] * 2,
        [up_y, near_sm, near_rm, near_c, near_depth, near_values, before, after],
        scratch=[
            pltpu.VMEM((2, 24, 32, 128), F32),
            pltpu.VMEM((2, 8, 16, 128), F32),
            pltpu.VMEM((2, 8, 16, 128), F32),
        ],
    )
    left, right = both_ways(up_x, down_x, "gx")
    inner, inner_courant = call(
        inner_kernel,
        [((2, 24, 16, 128), F32), ((24, 16, 128), F32)],
        [near_wavelet, up_y, near_sm, near_rm, near_c, before, after, depths, strips],
        scalars=[source_cell],
        scratch=[
            pltpu.VMEM((2, 32, 32, 128), F32),
            pltpu.VMEM((2, 24, 16, 128), F32),
            pltpu.VMEM((2, 24, 16, 128), F32),
        ],
    )
    sums = [((2, *tile), F32), (tile, F32), ((8, 8, 128), F32)]
    own, rim_y, rim_x, rounds = call(collect_kernel, [*sums, ((1,), I32)], [got, inner_courant], out_scalars=1, weight=1000)

    def another(state):
        turn, *partial = state
        (more,) = call(
            route_more_kernel,
            [sent_shape],
            [],
            scalars=[(turn * SLOTS).reshape(1)],
            hbm=[cells, receiver_traces],
            scratch=[pltpu.VMEM(*shape) for shape in listed] + [pltpu.SemaphoreType.DMA((2,))],
        )
        more = lax.all_to_all(more, ("gx", "gy"), 0, 0, tiled=True)
        return (turn + 1, *call(collect_more_kernel, sums, [more, *partial]))

    _, own, rim_y, rim_x = lax.while_loop(
        lambda state: state[0] < rounds[0], another, (jnp.int32(1), own, rim_y, rim_x)
    )
    source_field, receiver_field, near, up, down = call(
        steps_kernel,
        [(tile, F32), (tile, F32), ((4, 32, 128), F32), ((2, 16, 128), F32), ((2, 16, 128), F32)],
        [
            near_wavelet, up_y, near_c, near_depth, near_values,
            left, right, edge, edge_courant, inner, inner_courant, depths, own, rim_y, rim_x,
        ],
        out_hbm=(0, 1),
        scalars=[source_cell],
        scratch=[
            pltpu.VMEM((2, 40, 24, 128), F32),
            pltpu.VMEM((2, 2, 4, 16, 128), F32),
            pltpu.VMEM((2, 32, 8, 128), F32),
            pltpu.VMEM((4, 2, 32, 128), F32),
            pltpu.VMEM(tile, F32),
            pltpu.VMEM(tile, F32),
            pltpu.SemaphoreType.DMA((2,)),
        ],
    )
    near_left, near_right = both_ways(up, down, "gx")
    (angles,) = call(
        angles_kernel, [((16, 8, 128), F32)], [near, near_left, near_right],
        scratch=[pltpu.VMEM((4, 64, 128), F32)],
    )
    angles = lax.all_to_all(angles, "gy", 0, 0, tiled=True)
    (image,) = call(arrange_kernel, [((2, 8, 1024), F32)], [angles])
    return source_field, receiver_field, image


def solution(mesh):
    return jax.shard_map(
        body,
        mesh=mesh,
        in_specs=(
            P("gx", "gy", None),
            P("gx", "gy", None),
            P("gx", "gy", None),
            P("gx", "gy", None),
            P("gx", "gy", None),
            P(),
            P(),
            P(("gx", "gy")),
            P(None, ("gx", "gy")),
            P("gy", "gx"),
            P(None, None, "gy", "gx"),
        ),
        out_specs=(P("gx", "gy", None), P("gx", "gy", None), P("gy", "gx", None)),
        check_vma=False,
    )
```

time: 53.6 us -> 49.8 us (0.929)
  Pallas kernels: 11.2 us -> 8.36 us
  waiting for transfers between devices: 8.07 us -> 7.46 us
    pallas_call x8 -> x7, Pallas kernels: 11.2 us -> 8.36 us  [call(): pl.pallas_call(kernel, out_shape=[jax.ShapeDtypeStruct(shape, kind) for s...]
  transfers between devices with their start and end apart: 7 -> 7, of which waited for: 3 -> 3; matrix products, arithmetic and copies ran while one was open for 0% -> 0% of each run, Pallas kernels for 10% -> 7%
where the time goes in v4:
time: 49.8 us; the launch traced here: 49.6 us
  starting transfers between devices  18.7 us (38%)
  blocking collectives  13.1 us (26%)
  Pallas kernels  8.36 us (17%)
  waiting for transfers between devices  7.46 us (15%)
  between operations  1.38 us (3%)
  loops' own time  0.65 us (1%)
    all_to_all x1, blocking collectives, body(): angles = lax.all_to_all(angles, 'gy', 0, 0, tiled=True)  13.1 us
    all_to_all x1, starting transfers between devices, body(): got = lax.all_to_all(sent, ('gx', 'gy'), 0, 0, tiled=True)  10.7 us
    pallas_call x7, Pallas kernels, call(): pl.pallas_call(kernel, out_shape=[jax.ShapeDtypeStruct(shape, kind) for s...  8.36 us
    ppermute x3, starting transfers between devices, both_ways(): lax.ppermute(to_next, axis, [(i, (i + 1) % size) for i in range(size)])  5.16 us
    all_to_all x1, waiting for transfers between devices, body(): got = lax.all_to_all(sent, ('gx', 'gy'), 0, 0, tiled=True)  3.63 us
    ppermute x3, starting transfers between devices, both_ways(): lax.ppermute(to_last, axis, [((i + 1) % size, i) for i in range(size)])  2.85 us
    ppermute x3, waiting for transfers between devices, both_ways(): lax.ppermute(to_last, axis, [((i + 1) % size, i) for i in range(size)])  2.7 us
    ppermute x3, waiting for transfers between devices, both_ways(): lax.ppermute(to_next, axis, [(i, (i + 1) % size) for i in range(size)])  1.13 us
  transfers between devices with their start and end apart: 7, of which 3 were waited for; matrix products, arithmetic and copies ran while one was open for 0% of the time, Pallas kernels for 7%

profile of v4, /device:TPU:5, one launch (start us, length us, event | category | flops | bytes accessed | tf_op | source)
XLA Modules:
  0.0 49.6 jit_solution(5693892817839546918)
XLA Ops:
  0.6 2.0 %shard_map.130 = (f32[113,8,128]{2,1,0:T(8,128)S(1)}, f32[113,8,128]{2,1,0:T(8,128)S(1)}, f32[1,2]{1,0:T(1,128)S(1)}, f32[32,8,128]{2,1,0:T(8,128)S(1)}, f32[32,...) custom-call(s32[1,256]{1,0:T(1,128)} %bitcast.11, ...), custom_call_target="tpu_custom_call" | custom-call | tf_op jit(solution)/shard_map/pallas_call | solution.py:490
  2.6 1.9 %collective-permute-start = (f32[113,8,128]{2,1,0:T(8,128)S(1)}, f32[113,8,128]{2,1,0:T(8,128)S(1)}, u32[]{:S(2)}, u32[]{:S(2)}) collective-permute-start(f32[113,8,128]{2,1,0:T(8,128)S(1)} %get-tuple-element.73.own_y), channel_id=1, source_target_pairs={{0,1},{1,2},{2,3},{3,4},{4,5},{5,6},{6,7},{7,8},{8,9},{9,10},{10,1... | collective-permute-start | bytes 1388552 | tf_op jit(solution)/shard_map/ppermute | solution.py:505
  4.6 0.0 collective-permute-start.1
  4.6 10.7 %all-to-all-start.1 = ((f32[128,1,128]{2,1,0:T(1,128)}), f32[128,1,128]{2,1,0:T(1,128)S(1)}, u32[]{:S(2)}, u32[]{:S(2)}) async-start(f32[128,1,128]{2,1,0:T(1,128)} %get-tuple-element.88), calls=%async_computation.1 | async-start | bytes 131072 | tf_op jit(solution)/shard_map/all_to_all | solution.py:537
  15.9 0.0 collective-permute-done.before
  15.9 0.0 collective-permute-done.1.after
  15.9 0.4 shard_map.131
  16.3 1.4 %collective-permute-start.2 = (f32[29,8,128]{2,1,0:T(8,128)S(1)}, f32[29,8,128]{2,1,0:T(8,128)S(1)}, u32[]{:S(2)}, u32[]{:S(2)}) collective-permute-start(f32[29,8,128]{2,1,0:T(8,128)S(1)} %get-tuple-element.80), channel_id=1, source_target_pairs={{0,16},{16,32},{32,48},{48,64},{64,80},{80,96},{96,112},{112,0},{1... | collective-permute-start | bytes 356360 | tf_op jit(solution)/shard_map/ppermute | solution.py:505
  17.7 1.7 %collective-permute-start.3 = (f32[29,8,128]{2,1,0:T(8,128)S(1)}, f32[29,8,128]{2,1,0:T(8,128)S(1)}, u32[]{:S(2)}, u32[]{:S(2)}) collective-permute-start(f32[29,8,128]{2,1,0:T(8,128)S(1)} %get-tuple-element.81), channel_id=1, source_target_pairs={{16,0},{32,16},{48,32},{64,48},{80,64},{96,80},{112,96},{0,112},{1... | collective-permute-start | bytes 356360 | tf_op jit(solution)/shard_map/ppermute | solution.py:506
  19.4 3.6 %all-to-all-done.1 = f32[128,1,128]{2,1,0:T(1,128)S(1)} async-done(((f32[128,1,128]{2,1,0:T(1,128)}), f32[128,1,128]{2,1,0:T(1,128)S(1)}, u32[]{:S(2)}, u32[]{:S(2)}) %all-to-all-start.1) | async-done | bytes 65568 | tf_op jit(solution)/shard_map/all_to_all | solution.py:537
  23.0 1.1 %shard_map.132 = (f32[2,24,16,128]{3,2,1,0:T(8,128)S(1)}, f32[24,16,128]{2,1,0:T(8,128)S(1)}) custom-call(s32[1]{0:T(128)S(6)} %copy.31.source_cell, f32[1,2]{1,0:T(1,128)S(1)} %get-tuple-element.72.wavelet, f32[113,8,128]{2,1,0:T(8,128)S(1)} %get-tuple-element.73.own_y, f32[32,8,128]{2,1,0:T(8,128)S(1)} %get-tuple-element.77.sm, ...), custom_call_target="tpu_custom_call" | custom-call | tf_op jit(solution)/shard_map/pallas_call | solution.py:490
  24.1 1.9 %shard_map.133 = (f32[2,32,8,128]{3,2,1,0:T(8,128)S(1)}, f32[32,8,128]{2,1,0:T(8,128)S(1)}, f32[8,8,128]{2,1,0:T(8,128)S(1)}, s32[1]{0:T(128)}) custom-call(f32[128,128]{1,0:T(8,128)S(1)} %maximum_bitcast_fusion.got_ref, f32[24,16,128]{2,1,0:T(8,128)S(1)} %get-tuple-element.87.inner_courant), custom_call_target="tpu_custom_call" | custom-call | bytes 1000 | tf_op jit(solution)/shard_map/pallas_call | solution.py:490
  26.0 0.7 %while.14 = (s32[]{:T(128)}, f32[2,32,8,128]{3,2,1,0:T(8,128)S(1)}, f32[32,8,128]{2,1,0:T(8,128)S(1)}, f32[8,8,128]{2,1,0:T(8,128)S(1)}, s32[1]{0:T(128)}, /*ind...) while((s32[]{:T(128)}, f32[2,32,8,128]{3,2,1,0:T(8,128)S(1)}, f32[32,8,128]{2,1,0:T(8,128)S(1)}, ...), condition=%wide.region_1.0_spmd, body=%wide.region_0.0_spmd.sunk | while | flops 3 | bytes 1048713 | solution.py:578
  26.6 0.0 collective-permute-done.2.left
  26.6 0.0 collective-permute-done.3.right
  26.7 1.5 %shard_map.134 = (f32[32,8,128]{2,1,0:T(8,128)}, f32[32,8,128]{2,1,0:T(8,128)}, f32[4,32,128]{2,1,0:T(8,128)S(1)}, f32[2,16,128]{2,1,0:T(8,128)S(1)}, f32[2,16,128]{2,1,0:T(8,128)S(1)}) custom-call(s32[1]{0:T(128)S(6)} %copy.31.source_cell, f32[1,2]{1,0:T(1,128)S(1)} %get-tuple-element.72.wavelet, f32[113,8,128]{2,1,0:T(8,128)S(1)} %get-tuple-element.73.own_y, ...), custom_call_target="tpu_custom_call" | custom-call | tf_op jit(solution)/shard_map/pallas_call | solution.py:490
  28.2 1.9 %collective-permute-start.4 = (f32[2,16,128]{2,1,0:T(8,128)S(1)}, f32[2,16,128]{2,1,0:T(8,128)S(1)}, u32[]{:S(2)}, u32[]{:S(2)}) collective-permute-start(f32[2,16,128]{2,1,0:T(8,128)S(1)} %get-tuple-element.99), channel_id=1, source_target_pairs={{0,16},{16,32},{32,48},{48,64},{64,80},{80,96},{96,112},{112,0},{1... | collective-permute-start | bytes 49160 | tf_op jit(solution)/shard_map/ppermute | solution.py:505
  30.0 1.2 %collective-permute-start.5 = (f32[2,16,128]{2,1,0:T(8,128)S(1)}, f32[2,16,128]{2,1,0:T(8,128)S(1)}, u32[]{:S(2)}, u32[]{:S(2)}) collective-permute-start(f32[2,16,128]{2,1,0:T(8,128)S(1)} %get-tuple-element.100), channel_id=1, source_target_pairs={{16,0},{32,16},{48,32},{64,48},{80,64},{96,80},{112,96},{0,112},{1... | collective-permute-start | bytes 49160 | tf_op jit(solution)/shard_map/ppermute | solution.py:506
  31.2 1.1 %collective-permute-done.4.left = f32[2,16,128]{2,1,0:T(8,128)S(1)} collective-permute-done((f32[2,16,128]{2,1,0:T(8,128)S(1)}, f32[2,16,128]{2,1,0:T(8,128)S(1)}, u32[]{:S(2)}, u32[]{:S(2)}) %collective-permute-start.4) | collective-permute-done | bytes 16416 | tf_op jit(solution)/shard_map/ppermute | solution.py:505
  32.3 2.7 %collective-permute-done.5.right = f32[2,16,128]{2,1,0:T(8,128)S(1)} collective-permute-done((f32[2,16,128]{2,1,0:T(8,128)S(1)}, f32[2,16,128]{2,1,0:T(8,128)S(1)}, u32[]{:S(2)}, u32[]{:S(2)}) %collective-permute-start.5) | collective-permute-done | bytes 16416 | tf_op jit(solution)/shard_map/ppermute | solution.py:506
  35.0 0.8 %shard_map.135 = f32[16,8,128]{2,1,0:T(8,128)S(1)} custom-call(f32[4,32,128]{2,1,0:T(8,128)S(1)} %get-tuple-element.98.near, f32[2,16,128]{2,1,0:T(8,128)S(1)} %collective-permute-done.4.left, f32[2,16,128]{2,1,0:T(8,128)S(1)} %collective-permute-done.5.right), custom_call_target="tpu_custom_call" | custom-call | tf_op jit(solution)/shard_map/pallas_call | solution.py:490
  35.8 13.1 %all_to_all.16.got = f32[16,8,128]{2,1,0:T(8,128)S(1)} all-to-all(f32[16,8,128]{2,1,0:T(8,128)S(1)} %shard_map.135), channel_id=1, replica_groups=mesh['gx'=8,'gy'=16] {'gy'}, dimensions={0} | all-to-all | bytes 131072 | tf_op jit(solution)/shard_map/all_to_all | solution.py:605
  48.9 0.7 %shard_map.136 = f32[2,8,1024]{2,1,0:T(8,128)} custom-call(f32[16,8,128]{2,1,0:T(8,128)S(1)} %all_to_all.16.got), custom_call_target="tpu_custom_call" | custom-call | tf_op jit(solution)/shard_map/pallas_call | solution.py:490
  (1 shorter events, 0.0 us)
Async XLA Ops:
  2.6 13.3 %collective-permute-start = (f32[113,8,128]{2,1,0:T(8,128)S(1)}, f32[113,8,128]{2,1,0:T(8,128)S(1)}, u32[]{:S(2)}, u32[]{:S(2)}) collective-permute-start(f32[113,8,128]{2,1,0:T(8,128)S(1)} %get-tuple-element.73.own_y), channel_id=1, source_target_pairs={{0,1},{1,2},{2,3},{3,4},{4,5},{5,6},{6,7},{7,8},{8,9},{9,10},{10,1... | collective-permute-start | bytes 1388552 | tf_op jit(solution)/shard_map/ppermute | solution.py:505
  4.6 11.4 %collective-permute-start.1 = (f32[113,8,128]{2,1,0:T(8,128)S(1)}, f32[113,8,128]{2,1,0:T(8,128)S(1)}, u32[]{:S(2)}, u32[]{:S(2)}) collective-permute-start(f32[113,8,128]{2,1,0:T(8,128)S(1)} %get-tuple-element.79), channel_id=1, source_target_pairs={{1,0},{2,1},{3,2},{4,3},{5,4},{6,5},{7,6},{8,7},{9,8},{10,9},{11,1... | collective-permute-start | bytes 1388552 | tf_op jit(solution)/shard_map/ppermute | solution.py:506
  4.6 18.4 %all-to-all-start.1 = ((f32[128,1,128]{2,1,0:T(1,128)}), f32[128,1,128]{2,1,0:T(1,128)S(1)}, u32[]{:S(2)}, u32[]{:S(2)}) async-start(f32[128,1,128]{2,1,0:T(1,128)} %get-tuple-element.88), calls=%async_computation.1 | async-start | bytes 131072 | tf_op jit(solution)/shard_map/all_to_all | solution.py:537
  16.3 10.3 %collective-permute-start.2 = (f32[29,8,128]{2,1,0:T(8,128)S(1)}, f32[29,8,128]{2,1,0:T(8,128)S(1)}, u32[]{:S(2)}, u32[]{:S(2)}) collective-permute-start(f32[29,8,128]{2,1,0:T(8,128)S(1)} %get-tuple-element.80), channel_id=1, source_target_pairs={{0,16},{16,32},{32,48},{48,64},{64,80},{80,96},{96,112},{112,0},{1... | collective-permute-start | bytes 356360 | tf_op jit(solution)/shard_map/ppermute | solution.py:505
  17.7 9.0 %collective-permute-start.3 = (f32[29,8,128]{2,1,0:T(8,128)S(1)}, f32[29,8,128]{2,1,0:T(8,128)S(1)}, u32[]{:S(2)}, u32[]{:S(2)}) collective-permute-start(f32[29,8,128]{2,1,0:T(8,128)S(1)} %get-tuple-element.81), channel_id=1, source_target_pairs={{16,0},{32,16},{48,32},{64,48},{80,64},{96,80},{112,96},{0,112},{1... | collective-permute-start | bytes 356360 | tf_op jit(solution)/shard_map/ppermute | solution.py:506
  28.2 4.2 %collective-permute-start.4 = (f32[2,16,128]{2,1,0:T(8,128)S(1)}, f32[2,16,128]{2,1,0:T(8,128)S(1)}, u32[]{:S(2)}, u32[]{:S(2)}) collective-permute-start(f32[2,16,128]{2,1,0:T(8,128)S(1)} %get-tuple-element.99), channel_id=1, source_target_pairs={{0,16},{16,32},{32,48},{48,64},{64,80},{80,96},{96,112},{112,0},{1... | collective-permute-start | bytes 49160 | tf_op jit(solution)/shard_map/ppermute | solution.py:505
  30.0 5.0 %collective-permute-start.5 = (f32[2,16,128]{2,1,0:T(8,128)S(1)}, f32[2,16,128]{2,1,0:T(8,128)S(1)}, u32[]{:S(2)}, u32[]{:S(2)}) collective-permute-start(f32[2,16,128]{2,1,0:T(8,128)S(1)} %get-tuple-element.100), channel_id=1, source_target_pairs={{16,0},{32,16},{48,32},{64,48},{80,64},{96,80},{112,96},{0,112},{1... | collective-permute-start | bytes 49160 | tf_op jit(solution)/shard_map/ppermute | solution.py:506

commit v5 on v4

--- a/solution.py
+++ b/solution.py
@@ -142,14 +142,14 @@
 
 def pack_kernel(
     cells, traces, wavelet, s0, r0, sm, rm, c, depth, values,
-    up_y, down_y, wavelet_ref, sm_v, rm_v, c_v, depth_v, values_v, sent_ref,
+    first_y, second_y, wavelet_ref, sm_v, rm_v, c_v, depth_v, values_v, sent_ref,
     sent_v, cells_v, traces_v, sems,
 ):
     copies = started(
         [
             (cells, cells_v), (traces, traces_v), (depth, depth_v), (values, values_v), (wavelet, wavelet_ref),
             (sm, sm_v), (rm, rm_v), (c, c_v),
-            (s0, up_y.at[0:32]), (r0, up_y.at[32:64]), (s0, down_y.at[0:32]), (r0, down_y.at[32:64]),
+            (s0, first_y.at[0:32]), (r0, first_y.at[32:64]), (s0, second_y.at[0:32]), (r0, second_y.at[32:64]),
         ],
         sems,
     )
@@ -160,13 +160,19 @@
     out.start()
     for copy in copies[2:8]:
         copy.wait()
-    for ref, rows in ((up_y, slice(4, 8)), (down_y, slice(0, 4))):
-        ref[64:96, 0:4] = sm_v[:, rows]
-        ref[64:96, 4:8] = rm_v[:, rows]
-        ref[96:112, 0:4] = c_v[0:16, rows]
-        ref[96:112, 4:8] = c_v[16:32, rows]
-        ref[112, 0:4] = strip_values_tile(values_v, 0, rows)
-        ref[112, 4:8] = wide(depth_v[rows].astype(F32))
+    even = lax.axis_index("gy") % 2 == 0
+    strips, depths = strip_values_tile(values_v, 0, slice(0, 8)), wide(depth_v[...].astype(F32))
+    for ref, high in ((first_y, even), (second_y, ~even)):
+
+        def four(rows):
+            return jnp.where(high, rows[..., 4:8, :], rows[..., 0:4, :])
+
+        ref[64:96, 0:4] = four(sm_v[...])
+        ref[64:96, 4:8] = four(rm_v[...])
+        ref[96:112, 0:4] = four(c_v[0:16])
+        ref[96:112, 4:8] = four(c_v[16:32])
+        ref[112, 0:4] = four(strips)
+        ref[112, 4:8] = four(depths)
     for copy in copies[8:]:
         copy.wait()
     out.wait()
@@ -235,36 +241,55 @@
         new_ref[1, i, rows] = 2.0 * now - m_ref[1, i, rows] + courant * total
 
 
+def in_order(beside, first, second):
+    even = lax.axis_index("gy") % 2 == 0
+
+    @pl.when(even)
+    def _():
+        beside(second, first)
+
+    @pl.when(~even)
+    def _():
+        beside(first, second)
+
+
 def edge_kernel(
-    own_y, sm, rm, c, depth, values, before, after,
+    own_y, sm, rm, c, depth, values, first, second,
     new_ref, courant_ref, depth_ref, v_ref, up_ref, down_ref,
     e_ref, m_ref, z_ref,
 ):
     keep_before, keep_after = keeps("gy", GY)
+    spans = ((4, 0), (12, 24))
     for f in range(2):
         e_ref[f, 0:4, 8:24] = jnp.zeros((4, 16, 128), F32)
         e_ref[f, 20:24, 8:24] = jnp.zeros((4, 16, 128), F32)
-        for to, first in ((4, 0), (12, 24)):
-            start = 32 * f + first
-            e_ref[f, to : to + 8, 12:20] = own_y[start : start + 8]
-            e_ref[f, to : to + 8, 4:12] = before[start : start + 8] * keep_before
-            e_ref[f, to : to + 8, 20:28] = after[start : start + 8] * keep_after
+        for to, start in spans:
+            e_ref[f, to : to + 8, 12:20] = own_y[32 * f + start : 32 * f + start + 8]
     v_ref[4:12] = strip_values_tile(values, 0, slice(0, 8))
     depth_ref[4:12] = wide(depth[...])
-    for to, first in ((0, 0), (4, 28)):
+    for to, start in ((0, 0), (4, 28)):
         layers = slice(to, to + 4)
-        m_ref[0, layers, 4:12] = sm[first : first + 4]
-        m_ref[1, layers, 4:12] = rm[first : first + 4]
-        courant_ref[layers, 4:12] = c[first : first + 4]
-    for ref, keep, rows in ((before, keep_before, slice(0, 4)), (after, keep_after, slice(12, 16))):
-        for to, first in ((0, 0), (4, 28)):
-            layers, half = slice(to, to + 4), first // 16
-            m_ref[0, layers, rows] = ref[64 + first : 68 + first, 0:4] * keep
-            m_ref[1, layers, rows] = ref[64 + first : 68 + first, 4:8] * keep
-            start = 96 + first - 16 * half
-            courant_ref[layers, rows] = ref[start : start + 4, 4 * half : 4 * half + 4] * keep
-        v_ref[rows] = ref[112, 0:4] * keep
-        depth_ref[rows] = (ref[112, 4:8] * keep).astype(I32)
+        m_ref[0, layers, 4:12] = sm[start : start + 4]
+        m_ref[1, layers, 4:12] = rm[start : start + 4]
+        courant_ref[layers, 4:12] = c[start : start + 4]
+
+    def beside(before, after):
+        for f in range(2):
+            for to, start in spans:
+                layers = slice(32 * f + start, 32 * f + start + 8)
+                e_ref[f, to : to + 8, 4:12] = before[layers] * keep_before
+                e_ref[f, to : to + 8, 20:28] = after[layers] * keep_after
+        for ref, keep, rows in ((before, keep_before, slice(0, 4)), (after, keep_after, slice(12, 16))):
+            for to, start in ((0, 0), (4, 28)):
+                layers, half = slice(to, to + 4), start // 16
+                m_ref[0, layers, rows] = ref[64 + start : 68 + start, 0:4] * keep
+                m_ref[1, layers, rows] = ref[64 + start : 68 + start, 4:8] * keep
+                at = 96 + start - 16 * half
+                courant_ref[layers, rows] = ref[at : at + 4, 4 * half : 4 * half + 4] * keep
+            v_ref[rows] = ref[112, 0:4] * keep
+            depth_ref[rows] = (ref[112, 4:8] * keep).astype(I32)
+
+    in_order(beside, first, second)
     matrix = depth_matrix()
     for f in range(2):
         for half in range(2):
@@ -287,24 +312,28 @@
 
 def inner_kernel(
     source_cell,
-    wavelet, own_y, sm, rm, c, before, after, depths, values,
+    wavelet, own_y, sm, rm, c, first, second, depths, values,
     new_ref, courant_ref,
     e_ref, m_ref, z_ref,
 ):
     keep_before, keep_after = keeps("gy", GY)
     for f in range(2):
-        fields = slice(32 * f, 32 * f + 32)
-        e_ref[f, :, 12:20] = own_y[fields]
-        e_ref[f, :, 4:12] = before[fields] * keep_before
-        e_ref[f, :, 20:28] = after[fields] * keep_after
+        e_ref[f, :, 12:20] = own_y[32 * f : 32 * f + 32]
     m_ref[0, :, 4:12] = sm[4:28]
     m_ref[1, :, 4:12] = rm[4:28]
     courant_ref[:, 4:12] = c[4:28]
-    for ref, keep, rows in ((before, keep_before, slice(0, 4)), (after, keep_after, slice(12, 16))):
-        m_ref[0, :, rows] = ref[68:92, 0:4] * keep
-        m_ref[1, :, rows] = ref[68:92, 4:8] * keep
-        courant_ref[0:12, rows] = ref[100:112, 0:4] * keep
-        courant_ref[12:24, rows] = ref[96:108, 4:8] * keep
+
+    def beside(before, after):
+        for f in range(2):
+            e_ref[f, :, 4:12] = before[32 * f : 32 * f + 32] * keep_before
+            e_ref[f, :, 20:28] = after[32 * f : 32 * f + 32] * keep_after
+        for ref, keep, rows in ((before, keep_before, slice(0, 4)), (after, keep_after, slice(12, 16))):
+            m_ref[0, :, rows] = ref[68:92, 0:4] * keep
+            m_ref[1, :, rows] = ref[68:92, 4:8] * keep
+            courant_ref[0:12, rows] = ref[100:112, 0:4] * keep
+            courant_ref[12:24, rows] = ref[96:108, 4:8] * keep
+
+    in_order(beside, first, second)
     pulses = [pulse(source_cell, wavelet, 0, 8 * t - 4) for t in range(2)]
     source_x = source_layer(source_cell)
     matrix = depth_matrix()
@@ -524,7 +553,7 @@
     tile, sent_shape = (TX, TY, TZ), ((DEVICES, 1, 128), F32)
     listed = [((1, RECEIVERS), I32), ((2, RECEIVERS), F32)]
     fields = (source_now, receiver_now, source_next, receiver_next, courant, strip_depth, strip_values)
-    up_y, down_y, near_wavelet, near_sm, near_rm, near_c, near_depth, near_values, sent = call(
+    first_y, second_y, near_wavelet, near_sm, near_rm, near_c, near_depth, near_values, sent = call(
         pack_kernel,
         [((113, 8, 128), F32)] * 2
         + [((1, 2), F32), *[(tile, F32)] * 3, ((8, 32), I32), ((2, 4, 8, 32), F32), sent_shape],
@@ -533,14 +562,16 @@
         out_hbm=(8,),
         scratch=[pltpu.VMEM(*shape) for shape in (sent_shape, *listed)] + [pltpu.SemaphoreType.DMA((13,))],
     )
-    before, after = both_ways(up_y, down_y, "gy")
+    pairs = [(i, i ^ 1) for i in range(GY)]
+    first = lax.ppermute(first_y, "gy", pairs)
+    second = lax.ppermute(second_y, "gy", [(i, (i + 1 if i % 2 else i - 1) % GY) for i in range(GY)])
     got = lax.all_to_all(sent, ("gx", "gy"), 0, 0, tiled=True)
     got = jnp.maximum(got.reshape(DEVICES, 128), -jnp.finfo(F32).max)
     edge, edge_courant, depths, strips, up_x, down_x = call(
         edge_kernel,
         [((2, 8, 16, 128), F32), ((8, 16, 128), F32), ((16, 128), I32), ((16, 128), F32)]
         + [((29, 8, 128), F32)] * 2,
-        [up_y, near_sm, near_rm, near_c, near_depth, near_values, before, after],
+        [first_y, near_sm, near_rm, near_c, near_depth, near_values, first, second],
         scratch=[
             pltpu.VMEM((2, 24, 32, 128), F32),
             pltpu.VMEM((2, 8, 16, 128), F32),
@@ -551,7 +582,7 @@
     inner, inner_courant = call(
         inner_kernel,
         [((2, 24, 16, 128), F32), ((24, 16, 128), F32)],
-        [near_wavelet, up_y, near_sm, near_rm, near_c, before, after, depths, strips],
+        [near_wavelet, first_y, near_sm, near_rm, near_c, first, second, depths, strips],
         scalars=[source_cell],
         scratch=[
             pltpu.VMEM((2, 32, 32, 128), F32),
@@ -582,7 +613,7 @@
         steps_kernel,
         [(tile, F32), (tile, F32), ((4, 32, 128), F32), ((2, 16, 128), F32), ((2, 16, 128), F32)],
         [
-            near_wavelet, up_y, near_c, near_depth, near_values,
+            near_wavelet, first_y, near_c, near_depth, near_values,
             left, right, edge, edge_courant, inner, inner_courant, depths, own, rim_y, rim_x,
         ],
         out_hbm=(0, 1),

time: 49.8 us -> 49.4 us (level)
  starting transfers between devices: 18.7 us -> 18.1 us
    ppermute x0 -> x2, starting transfers between devices: none -> 2.03 us  [the longest x1 1.27 us: body(): lax.ppermute(second_y, 'gy', [(i, (i + 1 if i % 2 else i - 1) % GY) for i...]
    ppermute x3 -> x2, starting transfers between devices: 5.16 us -> 3.23 us  [both_ways(): lax.ppermute(to_next, axis, [(i, (i + 1) % size) for i in range(size)])]
    all_to_all x1, starting transfers between devices: 10.7 us -> 10 us  [body(): got = lax.all_to_all(sent, ('gx', 'gy'), 0, 0, tiled=True)]
    ppermute x3 -> x2, waiting for transfers between devices: 1.13 us -> 1.13 us  [both_ways(): lax.ppermute(to_next, axis, [(i, (i + 1) % size) for i in range(size)])]
    ppermute x3 -> x2, waiting for transfers between devices: 2.7 us -> 2.69 us  [both_ways(): lax.ppermute(to_last, axis, [((i + 1) % size, i) for i in range(size)])]
    ppermute x3 -> x2, starting transfers between devices: 2.85 us -> 2.84 us  [both_ways(): lax.ppermute(to_last, axis, [((i + 1) % size, i) for i in range(size)])]
where the time goes in v5:
time: 49.4 us; the launch traced here: 49.1 us
  starting transfers between devices  18.1 us (37%)
  blocking collectives  13.1 us (27%)
  Pallas kernels  8.6 us (17%)
  waiting for transfers between devices  7.33 us (15%)
  between operations  1.38 us (3%)
  loops' own time  0.65 us (1%)
    all_to_all x1, blocking collectives, body(): angles = lax.all_to_all(angles, 'gy', 0, 0, tiled=True)  13.1 us
    all_to_all x1, starting transfers between devices, body(): got = lax.all_to_all(sent, ('gx', 'gy'), 0, 0, tiled=True)  10 us
    pallas_call x7, Pallas kernels, call(): pl.pallas_call(kernel, out_shape=[jax.ShapeDtypeStruct(shape, kind) for s...  8.6 us
    all_to_all x1, waiting for transfers between devices, body(): got = lax.all_to_all(sent, ('gx', 'gy'), 0, 0, tiled=True)  3.51 us
    ppermute x2, starting transfers between devices, both_ways(): lax.ppermute(to_next, axis, [(i, (i + 1) % size) for i in range(size)])  3.23 us
    ppermute x2, starting transfers between devices, both_ways(): lax.ppermute(to_last, axis, [((i + 1) % size, i) for i in range(size)])  2.84 us
    ppermute x2, waiting for transfers between devices, both_ways(): lax.ppermute(to_last, axis, [((i + 1) % size, i) for i in range(size)])  2.69 us
    ppermute x1, starting transfers between devices, body(): lax.ppermute(second_y, 'gy', [(i, (i + 1 if i % 2 else i - 1) % GY) for i...  1.27 us
  transfers between devices with their start and end apart: 7, of which 3 were waited for; matrix products, arithmetic and copies ran while one was open for 0% of the time, Pallas kernels for 7%

profile of v5, /device:TPU:5, one launch (start us, length us, event | category | flops | bytes accessed | tf_op | source)
XLA Modules:
  0.0 49.1 jit_solution(2977336250960711014)
XLA Ops:
  0.6 2.0 %shard_map.130 = (f32[113,8,128]{2,1,0:T(8,128)S(1)}, f32[113,8,128]{2,1,0:T(8,128)S(1)}, f32[1,2]{1,0:T(1,128)S(1)}, f32[32,8,128]{2,1,0:T(8,128)S(1)}, f32[32,...) custom-call(s32[1,256]{1,0:T(1,128)} %bitcast.11, ...), custom_call_target="tpu_custom_call" | custom-call | tf_op jit(solution)/shard_map/pallas_call | solution.py:519
  2.6 0.8 %collective-permute-start = (f32[113,8,128]{2,1,0:T(8,128)S(1)}, f32[113,8,128]{2,1,0:T(8,128)S(1)}, u32[]{:S(2)}, u32[]{:S(2)}) collective-permute-start(f32[113,8,128]{2,1,0:T(8,128)S(1)} %get-tuple-element.73.own_y), channel_id=1, source_target_pairs={{0,1},{1,0},{2,3},{3,2},{4,5},{5,4},{6,7},{7,6},{8,9},{9,8},{10,11... | collective-permute-start | bytes 1388552 | tf_op jit(solution)/shard_map/ppermute | solution.py:566
  3.4 1.3 %collective-permute-start.1 = (f32[113,8,128]{2,1,0:T(8,128)S(1)}, f32[113,8,128]{2,1,0:T(8,128)S(1)}, u32[]{:S(2)}, u32[]{:S(2)}) collective-permute-start(f32[113,8,128]{2,1,0:T(8,128)S(1)} %get-tuple-element.79), channel_id=1, source_target_pairs={{0,15},{1,2},{2,1},{3,4},{4,3},{5,6},{6,5},{7,8},{8,7},{9,10},{10,... | collective-permute-start | bytes 1388552 | tf_op jit(solution)/shard_map/ppermute | solution.py:567
  4.7 10.0 %all-to-all-start.1 = ((f32[128,1,128]{2,1,0:T(1,128)}), f32[128,1,128]{2,1,0:T(1,128)S(1)}, u32[]{:S(2)}, u32[]{:S(2)}) async-start(f32[128,1,128]{2,1,0:T(1,128)} %get-tuple-element.88), calls=%async_computation.1 | async-start | bytes 131072 | tf_op jit(solution)/shard_map/all_to_all | solution.py:568
  15.3 0.0 collective-permute-done.first
  15.3 0.0 collective-permute-done.1.second
  15.3 0.5 %shard_map.131 = (f32[2,8,16,128]{3,2,1,0:T(8,128)S(1)}, f32[8,16,128]{2,1,0:T(8,128)S(1)}, s32[16,128]{1,0:T(8,128)S(1)}, f32[16,128]{1,0:T(8,128)S(1)}, f32[29...) custom-call(f32[113,8,128]{2,1,0:T(8,128)S(1)} %get-tuple-element.73.own_y, f32[32,8,128]{2,1,0:T(8,128)S(1)} %get-tuple-element.77.sm, ...), custom_call_target="tpu_custom_call" | custom-call | tf_op jit(solution)/shard_map/pallas_call | solution.py:519
  15.8 1.4 %collective-permute-start.2 = (f32[29,8,128]{2,1,0:T(8,128)S(1)}, f32[29,8,128]{2,1,0:T(8,128)S(1)}, u32[]{:S(2)}, u32[]{:S(2)}) collective-permute-start(f32[29,8,128]{2,1,0:T(8,128)S(1)} %get-tuple-element.80), channel_id=1, source_target_pairs={{0,16},{16,32},{32,48},{48,64},{64,80},{80,96},{96,112},{112,0},{1... | collective-permute-start | bytes 356360 | tf_op jit(solution)/shard_map/ppermute | solution.py:534
  17.2 1.7 %collective-permute-start.3 = (f32[29,8,128]{2,1,0:T(8,128)S(1)}, f32[29,8,128]{2,1,0:T(8,128)S(1)}, u32[]{:S(2)}, u32[]{:S(2)}) collective-permute-start(f32[29,8,128]{2,1,0:T(8,128)S(1)} %get-tuple-element.81), channel_id=1, source_target_pairs={{16,0},{32,16},{48,32},{64,48},{80,64},{96,80},{112,96},{0,112},{1... | collective-permute-start | bytes 356360 | tf_op jit(solution)/shard_map/ppermute | solution.py:535
  18.9 3.5 %all-to-all-done.1 = f32[128,1,128]{2,1,0:T(1,128)S(1)} async-done(((f32[128,1,128]{2,1,0:T(1,128)}), f32[128,1,128]{2,1,0:T(1,128)S(1)}, u32[]{:S(2)}, u32[]{:S(2)}) %all-to-all-start.1) | async-done | bytes 65568 | tf_op jit(solution)/shard_map/all_to_all | solution.py:568
  22.4 1.2 %shard_map.132 = (f32[2,24,16,128]{3,2,1,0:T(8,128)S(1)}, f32[24,16,128]{2,1,0:T(8,128)S(1)}) custom-call(s32[1]{0:T(128)S(6)} %copy.31.source_cell, f32[1,2]{1,0:T(1,128)S(1)} %get-tuple-element.72.wavelet, f32[113,8,128]{2,1,0:T(8,128)S(1)} %get-tuple-element.73.own_y, f32[32,8,128]{2,1,0:T(8,128)S(1)} %get-tuple-element.77.sm, ...), custom_call_target="tpu_custom_call" | custom-call | tf_op jit(solution)/shard_map/pallas_call | solution.py:519
  23.6 1.9 %shard_map.133 = (f32[2,32,8,128]{3,2,1,0:T(8,128)S(1)}, f32[32,8,128]{2,1,0:T(8,128)S(1)}, f32[8,8,128]{2,1,0:T(8,128)S(1)}, s32[1]{0:T(128)}) custom-call(f32[128,128]{1,0:T(8,128)S(1)} %maximum_bitcast_fusion.got_ref, f32[24,16,128]{2,1,0:T(8,128)S(1)} %get-tuple-element.87.inner_courant), custom_call_target="tpu_custom_call" | custom-call | bytes 1000 | tf_op jit(solution)/shard_map/pallas_call | solution.py:519
  25.5 0.7 %while.14 = (s32[]{:T(128)}, f32[2,32,8,128]{3,2,1,0:T(8,128)S(1)}, f32[32,8,128]{2,1,0:T(8,128)S(1)}, f32[8,8,128]{2,1,0:T(8,128)S(1)}, s32[1]{0:T(128)}, /*ind...) while((s32[]{:T(128)}, f32[2,32,8,128]{3,2,1,0:T(8,128)S(1)}, f32[32,8,128]{2,1,0:T(8,128)S(1)}, ...), condition=%wide.region_1.0_spmd, body=%wide.region_0.0_spmd.sunk | while | flops 3 | bytes 1048713 | solution.py:609
  26.1 0.0 collective-permute-done.2.left
  26.2 0.0 collective-permute-done.3.right
  26.2 1.5 %shard_map.134 = (f32[32,8,128]{2,1,0:T(8,128)}, f32[32,8,128]{2,1,0:T(8,128)}, f32[4,32,128]{2,1,0:T(8,128)S(1)}, f32[2,16,128]{2,1,0:T(8,128)S(1)}, f32[2,16,128]{2,1,0:T(8,128)S(1)}) custom-call(s32[1]{0:T(128)S(6)} %copy.31.source_cell, f32[1,2]{1,0:T(1,128)S(1)} %get-tuple-element.72.wavelet, f32[113,8,128]{2,1,0:T(8,128)S(1)} %get-tuple-element.73.own_y, ...), custom_call_target="tpu_custom_call" | custom-call | tf_op jit(solution)/shard_map/pallas_call | solution.py:519
  27.7 1.9 %collective-permute-start.4 = (f32[2,16,128]{2,1,0:T(8,128)S(1)}, f32[2,16,128]{2,1,0:T(8,128)S(1)}, u32[]{:S(2)}, u32[]{:S(2)}) collective-permute-start(f32[2,16,128]{2,1,0:T(8,128)S(1)} %get-tuple-element.99), channel_id=1, source_target_pairs={{0,16},{16,32},{32,48},{48,64},{64,80},{80,96},{96,112},{112,0},{1... | collective-permute-start | bytes 49160 | tf_op jit(solution)/shard_map/ppermute | solution.py:534
  29.6 1.2 %collective-permute-start.5 = (f32[2,16,128]{2,1,0:T(8,128)S(1)}, f32[2,16,128]{2,1,0:T(8,128)S(1)}, u32[]{:S(2)}, u32[]{:S(2)}) collective-permute-start(f32[2,16,128]{2,1,0:T(8,128)S(1)} %get-tuple-element.100), channel_id=1, source_target_pairs={{16,0},{32,16},{48,32},{64,48},{80,64},{96,80},{112,96},{0,112},{1... | collective-permute-start | bytes 49160 | tf_op jit(solution)/shard_map/ppermute | solution.py:535
  30.7 1.1 %collective-permute-done.4.left = f32[2,16,128]{2,1,0:T(8,128)S(1)} collective-permute-done((f32[2,16,128]{2,1,0:T(8,128)S(1)}, f32[2,16,128]{2,1,0:T(8,128)S(1)}, u32[]{:S(2)}, u32[]{:S(2)}) %collective-permute-start.4) | collective-permute-done | bytes 16416 | tf_op jit(solution)/shard_map/ppermute | solution.py:534
  31.9 2.7 %collective-permute-done.5.right = f32[2,16,128]{2,1,0:T(8,128)S(1)} collective-permute-done((f32[2,16,128]{2,1,0:T(8,128)S(1)}, f32[2,16,128]{2,1,0:T(8,128)S(1)}, u32[]{:S(2)}, u32[]{:S(2)}) %collective-permute-start.5) | collective-permute-done | bytes 16416 | tf_op jit(solution)/shard_map/ppermute | solution.py:535
  34.6 0.8 %shard_map.135 = f32[16,8,128]{2,1,0:T(8,128)S(1)} custom-call(f32[4,32,128]{2,1,0:T(8,128)S(1)} %get-tuple-element.98.near, f32[2,16,128]{2,1,0:T(8,128)S(1)} %collective-permute-done.4.left, f32[2,16,128]{2,1,0:T(8,128)S(1)} %collective-permute-done.5.right), custom_call_target="tpu_custom_call" | custom-call | tf_op jit(solution)/shard_map/pallas_call | solution.py:519
  35.4 13.1 %all_to_all.16.got = f32[16,8,128]{2,1,0:T(8,128)S(1)} all-to-all(f32[16,8,128]{2,1,0:T(8,128)S(1)} %shard_map.135), channel_id=1, replica_groups=mesh['gx'=8,'gy'=16] {'gy'}, dimensions={0} | all-to-all | bytes 131072 | tf_op jit(solution)/shard_map/all_to_all | solution.py:636
  48.4 0.7 %shard_map.136 = f32[2,8,1024]{2,1,0:T(8,128)} custom-call(f32[16,8,128]{2,1,0:T(8,128)S(1)} %all_to_all.16.got), custom_call_target="tpu_custom_call" | custom-call | tf_op jit(solution)/shard_map/pallas_call | solution.py:519
  (1 shorter events, 0.0 us)
Async XLA Ops:
  2.6 12.7 %collective-permute-start = (f32[113,8,128]{2,1,0:T(8,128)S(1)}, f32[113,8,128]{2,1,0:T(8,128)S(1)}, u32[]{:S(2)}, u32[]{:S(2)}) collective-permute-start(f32[113,8,128]{2,1,0:T(8,128)S(1)} %get-tuple-element.73.own_y), channel_id=1, source_target_pairs={{0,1},{1,0},{2,3},{3,2},{4,5},{5,4},{6,7},{7,6},{8,9},{9,8},{10,11... | collective-permute-start | bytes 1388552 | tf_op jit(solution)/shard_map/ppermute | solution.py:566
  3.4 11.9 %collective-permute-start.1 = (f32[113,8,128]{2,1,0:T(8,128)S(1)}, f32[113,8,128]{2,1,0:T(8,128)S(1)}, u32[]{:S(2)}, u32[]{:S(2)}) collective-permute-start(f32[113,8,128]{2,1,0:T(8,128)S(1)} %get-tuple-element.79), channel_id=1, source_target_pairs={{0,15},{1,2},{2,1},{3,4},{4,3},{5,6},{6,5},{7,8},{8,7},{9,10},{10,... | collective-permute-start | bytes 1388552 | tf_op jit(solution)/shard_map/ppermute | solution.py:567
  4.7 17.7 %all-to-all-start.1 = ((f32[128,1,128]{2,1,0:T(1,128)}), f32[128,1,128]{2,1,0:T(1,128)S(1)}, u32[]{:S(2)}, u32[]{:S(2)}) async-start(f32[128,1,128]{2,1,0:T(1,128)} %get-tuple-element.88), calls=%async_computation.1 | async-start | bytes 131072 | tf_op jit(solution)/shard_map/all_to_all | solution.py:568
  15.8 10.3 %collective-permute-start.2 = (f32[29,8,128]{2,1,0:T(8,128)S(1)}, f32[29,8,128]{2,1,0:T(8,128)S(1)}, u32[]{:S(2)}, u32[]{:S(2)}) collective-permute-start(f32[29,8,128]{2,1,0:T(8,128)S(1)} %get-tuple-element.80), channel_id=1, source_target_pairs={{0,16},{16,32},{32,48},{48,64},{64,80},{80,96},{96,112},{112,0},{1... | collective-permute-start | bytes 356360 | tf_op jit(solution)/shard_map/ppermute | solution.py:534
  17.2 9.0 %collective-permute-start.3 = (f32[29,8,128]{2,1,0:T(8,128)S(1)}, f32[29,8,128]{2,1,0:T(8,128)S(1)}, u32[]{:S(2)}, u32[]{:S(2)}) collective-permute-start(f32[29,8,128]{2,1,0:T(8,128)S(1)} %get-tuple-element.81), channel_id=1, source_target_pairs={{16,0},{32,16},{48,32},{64,48},{80,64},{96,80},{112,96},{0,112},{1... | collective-permute-start | bytes 356360 | tf_op jit(solution)/shard_map/ppermute | solution.py:535
  27.7 4.2 %collective-permute-start.4 = (f32[2,16,128]{2,1,0:T(8,128)S(1)}, f32[2,16,128]{2,1,0:T(8,128)S(1)}, u32[]{:S(2)}, u32[]{:S(2)}) collective-permute-start(f32[2,16,128]{2,1,0:T(8,128)S(1)} %get-tuple-element.99), channel_id=1, source_target_pairs={{0,16},{16,32},{32,48},{48,64},{64,80},{80,96},{96,112},{112,0},{1... | collective-permute-start | bytes 49160 | tf_op jit(solution)/shard_map/ppermute | solution.py:534
  29.6 5.0 %collective-permute-start.5 = (f32[2,16,128]{2,1,0:T(8,128)S(1)}, f32[2,16,128]{2,1,0:T(8,128)S(1)}, u32[]{:S(2)}, u32[]{:S(2)}) collective-permute-start(f32[2,16,128]{2,1,0:T(8,128)S(1)} %get-tuple-element.100), channel_id=1, source_target_pairs={{16,0},{32,16},{48,32},{64,48},{80,64},{96,80},{112,96},{0,112},{1... | collective-permute-start | bytes 49160 | tf_op jit(solution)/shard_map/ppermute | solution.py:535

commit v6 on v5

--- a/solution.py
+++ b/solution.py
@@ -355,23 +355,72 @@
     return jnp.where((relative >= 0) & (relative < 4), 0.0, amount)
 
 
+def late_layer(x, at, i, o_ref, z_ref, s0, r0, c, own, depths, values, late_pulse, source_x, s_v, r_v, sub_ref, to):
+    now, total = curvature(o_ref, 0, at, 8, z_ref[0, i])
+    total = total - jnp.where(x == source_x, late_pulse, 0.0)
+    new = 2.0 * now - s0[x] + c[x] * total
+    new = overwritten(new, depths, values, x)
+    s_v[i] = new
+    for j in range(2):
+        sub_ref[0, j, pl.ds(to, 1)] = now[4 * j : 4 * j + 1]
+        sub_ref[1, j, pl.ds(to, 1)] = new[4 * j : 4 * j + 1]
+    now, total = curvature(o_ref, 1, at, 8, z_ref[1, i])
+    new = 2.0 * now - r0[x] + c[x] * (total + own[1, x])
+    r_v[i] = new
+    for j in range(2):
+        sub_ref[2, j, pl.ds(to, 1)] = now[4 * j : 4 * j + 1]
+        sub_ref[3, j, pl.ds(to, 1)] = new[4 * j : 4 * j + 1]
+
+
+def middle_kernel(
+    source_cell,
+    wavelet, own_y, c, depth, values, inner, inner_courant, own, rim_y,
+    r1_ref, s_v, r_v, sub_ref,
+    o_ref, z_ref,
+):
+    o_ref[0, :, 4:20] = inner[0]
+    o_ref[1, :, 8:16] = inner[1, :, 4:12] + inner_courant[:, 4:12] * own[0, 4:28]
+    o_ref[1, :, 4:8] = inner[1, :, 0:4] + inner_courant[:, 0:4] * rim_y[4:28, 0:4]
+    o_ref[1, :, 16:20] = inner[1, :, 12:16] + inner_courant[:, 12:16] * rim_y[4:28, 4:8]
+    for half in range(2):
+        r1_ref[8 * half : 8 * half + 8] = o_ref[1, 16 * half : 16 * half + 8, 4:20]
+    matrix = depth_matrix()
+    for f in range(2):
+        rows = o_ref[f, 4:20, 8:16].reshape(128, 128)
+        z_ref[f] = depth_sums(rows, matrix).reshape(16, 8, 128)
+    late_values = strip_values_tile(values, 1, slice(0, 8))
+    near_depth = wide(depth[...])
+    late_pulse, source_x = pulse(source_cell, wavelet, 1, 0), source_layer(source_cell)
+
+    def layer(i, carry):
+        late_layer(
+            i + 8, i + 4, i, o_ref, z_ref, own_y.at[0:32], own_y.at[32:64], c, own,
+            near_depth, late_values, late_pulse, source_x, s_v, r_v, sub_ref, i,
+        )
+        return carry
+
+    lax.fori_loop(0, 16, layer, 0, unroll=16)
+
+
 def steps_kernel(
     source_cell,
-    wavelet, own_y, c, depth, values, left, right, edge, edge_courant, inner, inner_courant, depths,
-    own, rim_y, rim_x,
-    s_out, r_out, near_ref, up_ref, down_ref,
-    o_ref, h_ref, z_ref, sub_ref, s_v, r_v, sems,
+    wavelet, own_y, c, depth, values, left, right, edge, edge_courant, inner, depths,
+    own, rim_y, rim_x, r1, sub_mid,
+    s_v, r_v, near_ref, up_ref, down_ref,
+    o_ref, h_ref, z_ref, sub_ref,
 ):
     keep_left, keep_right = keeps("gx", GX)
     s0, r0 = own_y.at[0:32], own_y.at[32:64]
-    for new1, courant, start, first, size in (
-        (edge, edge_courant, 0, 0, 4), (inner, inner_courant, 0, 4, 24), (edge, edge_courant, 4, 28, 4)
-    ):
-        to, part, x = slice(first + 4, first + 4 + size), slice(start, start + size), slice(first, first + size)
-        o_ref[0, to, 4:20] = new1[0, part]
-        o_ref[1, to, 8:16] = new1[1, part, 4:12] + courant[part, 4:12] * own[0, x]
-        o_ref[1, to, 4:8] = new1[1, part, 0:4] + courant[part, 0:4] * rim_y[x, 0:4]
-        o_ref[1, to, 16:20] = new1[1, part, 12:16] + courant[part, 12:16] * rim_y[x, 4:8]
+    for start, first in ((0, 0), (4, 28)):
+        to, part, x = slice(first + 4, first + 8), slice(start, start + 4), slice(first, first + 4)
+        o_ref[0, to, 4:20] = edge[0, part]
+        o_ref[1, to, 8:16] = edge[1, part, 4:12] + edge_courant[part, 4:12] * own[0, x]
+        o_ref[1, to, 4:8] = edge[1, part, 0:4] + edge_courant[part, 0:4] * rim_y[x, 0:4]
+        o_ref[1, to, 16:20] = edge[1, part, 12:16] + edge_courant[part, 12:16] * rim_y[x, 4:8]
+    for half in range(2):
+        to = slice(8 + 16 * half, 16 + 16 * half)
+        o_ref[0, to, 4:20] = inner[0, 16 * half : 16 * half + 8]
+        o_ref[1, to, 4:20] = r1[8 * half : 8 * half + 8]
     source_x = source_layer(source_cell)
     pulses = [pulse(source_cell, wavelet, 0, row) for row in (-4, 4, 0)]
     for side, ref, keep in ((0, left, keep_left), (1, right, keep_right)):
@@ -415,31 +464,21 @@
                 o_ref[f, 36 + n if side else 3 - n, 8:16] = (ref[4 * f + k] + amount) * keep
     matrix = depth_matrix()
     for f in range(2):
-        rows = o_ref[f, 4:36, 8:16].reshape(256, 128)
-        z_ref[f] = depth_sums(rows, matrix).reshape(32, 8, 128)
+        for half in range(2):
+            rows = o_ref[f, 4 + 24 * half : 12 + 24 * half, 8:16].reshape(64, 128)
+            z_ref[f, 8 * half : 8 * half + 8] = depth_sums(rows, matrix).reshape(8, 8, 128)
     late_values = strip_values_tile(values, 1, slice(0, 8))
     near_depth = wide(depth[...])
     late_pulse = pulse(source_cell, wavelet, 1, 0)
-
-    def second(x, carry):
-        now, total = curvature(o_ref, 0, x + 4, 8, z_ref[0, x])
-        total = total - jnp.where(x == source_x, late_pulse, 0.0)
-        new = 2.0 * now - s0[x] + c[x] * total
-        new = overwritten(new, near_depth, late_values, x)
-        s_v[x] = new
+    for k in range(4):
         for j in range(2):
-            sub_ref[0, j, pl.ds(x, 1)] = now[4 * j : 4 * j + 1]
-            sub_ref[1, j, pl.ds(x, 1)] = new[4 * j : 4 * j + 1]
-        now, total = curvature(o_ref, 1, x + 4, 8, z_ref[1, x])
-        new = 2.0 * now - r0[x] + c[x] * (total + own[1, x])
-        r_v[x] = new
-        for j in range(2):
-            sub_ref[2, j, pl.ds(x, 1)] = now[4 * j : 4 * j + 1]
-            sub_ref[3, j, pl.ds(x, 1)] = new[4 * j : 4 * j + 1]
-        return carry
-
-    lax.fori_loop(0, 32, second, 0, unroll=16)
-    copies = started([(s_v, s_out), (r_v, r_out)], sems)
+            sub_ref[k, j, 8:24] = sub_mid[k, j]
+    for i in range(16):
+        x = i if i < 8 else i + 16
+        late_layer(
+            x, x + 4, i, o_ref, z_ref, s0, r0, c, own,
+            near_depth, late_values, late_pulse, source_x, s_v, r_v, sub_ref, x,
+        )
     z, to = iota((TZ, 128), 0), iota((TZ, 128), 1)
     totals = []
     for k in range(4):
@@ -456,11 +495,19 @@
         packed = totals[2 * f] + pltpu.roll(totals[2 * f + 1], 32, 1)
         up_ref[f] = packed[16:32]
         down_ref[f] = packed[0:16]
-    for copy in copies:
+
+
+def store_kernel(s_mid, r_mid, s_edge, r_edge, s_out, r_out, sems):
+    ends = [
+        pair
+        for mid, edge, to in ((s_mid, s_edge, s_out), (r_mid, r_edge, r_out))
+        for pair in ((mid, to.at[8:24]), (edge.at[0:8], to.at[0:8]), (edge.at[8:16], to.at[24:32]))
+    ]
+    for copy in started(ends, sems):
         copy.wait()
 
 
-def angles_kernel(near, left, right, out_ref, g_ref):
+def angles_kernel(stored, near, left, right, out_ref, g_ref):
     keep_left, keep_right = keeps("gx", GX)
     lane = iota((16, 128), 1)
     held = ((lane >= 16) & (lane < 48)) | ((lane >= 80) & (lane < 112))
@@ -609,28 +656,40 @@
     _, own, rim_y, rim_x = lax.while_loop(
         lambda state: state[0] < rounds[0], another, (jnp.int32(1), own, rim_y, rim_x)
     )
-    source_field, receiver_field, near, up, down = call(
+    part = (16, TY, TZ)
+    r1, s_mid, r_mid, sub_mid = call(
+        middle_kernel,
+        [((16, 16, 128), F32), (part, F32), (part, F32), ((4, 2, 16, 128), F32)],
+        [near_wavelet, first_y, near_c, near_depth, near_values, inner, inner_courant, own, rim_y],
+        scalars=[source_cell],
+        scratch=[pltpu.VMEM((2, 24, 24, 128), F32), pltpu.VMEM((2, 16, 8, 128), F32)],
+    )
+    s_edge, r_edge, near, up, down = call(
         steps_kernel,
-        [(tile, F32), (tile, F32), ((4, 32, 128), F32), ((2, 16, 128), F32), ((2, 16, 128), F32)],
+        [(part, F32), (part, F32), ((4, 32, 128), F32), ((2, 16, 128), F32), ((2, 16, 128), F32)],
         [
-            near_wavelet, first_y, near_c, near_depth, near_values,
-            left, right, edge, edge_courant, inner, inner_courant, depths, own, rim_y, rim_x,
+            near_wavelet, first_y, near_c, near_depth, near_values, left, right, edge, edge_courant,
+            inner, depths, own, rim_y, rim_x, r1, sub_mid,
         ],
-        out_hbm=(0, 1),
         scalars=[source_cell],
         scratch=[
             pltpu.VMEM((2, 40, 24, 128), F32),
             pltpu.VMEM((2, 2, 4, 16, 128), F32),
-            pltpu.VMEM((2, 32, 8, 128), F32),
+            pltpu.VMEM((2, 16, 8, 128), F32),
             pltpu.VMEM((4, 2, 32, 128), F32),
-            pltpu.VMEM(tile, F32),
-            pltpu.VMEM(tile, F32),
-            pltpu.SemaphoreType.DMA((2,)),
         ],
     )
     near_left, near_right = both_ways(up, down, "gx")
+    source_field, receiver_field = call(
+        store_kernel,
+        [(tile, F32), (tile, F32)],
+        [s_mid, r_mid, s_edge, r_edge],
+        out_hbm=(0, 1),
+        scratch=[pltpu.SemaphoreType.DMA((6,))],
+        weight=1_000_000,
+    )
     (angles,) = call(
-        angles_kernel, [((16, 8, 128), F32)], [near, near_left, near_right],
+        angles_kernel, [((16, 8, 128), F32)], [near, near_left, near_right], hbm=[source_field],
         scratch=[pltpu.VMEM((4, 64, 128), F32)],
     )
     angles = lax.all_to_all(angles, "gy", 0, 0, tiled=True)

time: 49.4 us -> 48.7 us (0.986)
  waiting for transfers between devices: 7.33 us -> 6.58 us
  Pallas kernels: 8.6 us -> 9.14 us
    ppermute x2, waiting for transfers between devices: 1.13 us -> 0.38 us  [both_ways(): lax.ppermute(to_next, axis, [(i, (i + 1) % size) for i in range(size)])]
    pallas_call x7 -> x9, Pallas kernels: 8.6 us -> 9.14 us  [call(): pl.pallas_call(kernel, out_shape=[jax.ShapeDtypeStruct(shape, kind) for s...]
  transfers between devices with their start and end apart: 7 -> 7, of which waited for: 3 -> 3; matrix products, arithmetic and copies ran while one was open for 0% -> 0% of each run, Pallas kernels for 7% -> 10%
where the time goes in v6:
time: 48.7 us; the launch traced here: 48.5 us
  starting transfers between devices  18.1 us (37%)
  blocking collectives  12.7 us (26%)
  Pallas kernels  9.14 us (19%)
  waiting for transfers between devices  6.58 us (14%)
  between operations  1.38 us (3%)
  loops' own time  0.65 us (1%)
    all_to_all x1, blocking collectives, body(): angles = lax.all_to_all(angles, 'gy', 0, 0, tiled=True)  12.7 us
    all_to_all x1, starting transfers between devices, body(): got = lax.all_to_all(sent, ('gx', 'gy'), 0, 0, tiled=True)  10 us
    pallas_call x9, Pallas kernels, call(): pl.pallas_call(kernel, out_shape=[jax.ShapeDtypeStruct(shape, kind) for s...  9.14 us
    all_to_all x1, waiting for transfers between devices, body(): got = lax.all_to_all(sent, ('gx', 'gy'), 0, 0, tiled=True)  3.51 us
    ppermute x2, starting transfers between devices, both_ways(): lax.ppermute(to_next, axis, [(i, (i + 1) % size) for i in range(size)])  3.18 us
    ppermute x2, starting transfers between devices, both_ways(): lax.ppermute(to_last, axis, [((i + 1) % size, i) for i in range(size)])  2.85 us
    ppermute x2, waiting for transfers between devices, both_ways(): lax.ppermute(to_last, axis, [((i + 1) % size, i) for i in range(size)])  2.69 us
    ppermute x1, starting transfers between devices, body(): lax.ppermute(second_y, 'gy', [(i, (i + 1 if i % 2 else i - 1) % GY) for i...  1.27 us
  transfers between devices with their start and end apart: 7, of which 3 were waited for; matrix products, arithmetic and copies ran while one was open for 0% of the time, Pallas kernels for 10%

profile of v6, /device:TPU:5, one launch (start us, length us, event | category | flops | bytes accessed | tf_op | source)
XLA Modules:
  0.0 48.5 jit_solution(15843570092233030597)
XLA Ops:
  0.6 2.0 %shard_map.130 = (f32[113,8,128]{2,1,0:T(8,128)S(1)}, f32[113,8,128]{2,1,0:T(8,128)S(1)}, f32[1,2]{1,0:T(1,128)S(1)}, f32[32,8,128]{2,1,0:T(8,128)S(1)}, f32[32,...) custom-call(s32[1,256]{1,0:T(1,128)} %bitcast.11, ...), custom_call_target="tpu_custom_call" | custom-call | tf_op jit(solution)/shard_map/pallas_call | solution.py:566
  2.6 0.8 %collective-permute-start = (f32[113,8,128]{2,1,0:T(8,128)S(1)}, f32[113,8,128]{2,1,0:T(8,128)S(1)}, u32[]{:S(2)}, u32[]{:S(2)}) collective-permute-start(f32[113,8,128]{2,1,0:T(8,128)S(1)} %get-tuple-element.79.own_y), channel_id=1, source_target_pairs={{0,1},{1,0},{2,3},{3,2},{4,5},{5,4},{6,7},{7,6},{8,9},{9,8},{10,11... | collective-permute-start | bytes 1388552 | tf_op jit(solution)/shard_map/ppermute | solution.py:613
  3.4 1.3 %collective-permute-start.1 = (f32[113,8,128]{2,1,0:T(8,128)S(1)}, f32[113,8,128]{2,1,0:T(8,128)S(1)}, u32[]{:S(2)}, u32[]{:S(2)}) collective-permute-start(f32[113,8,128]{2,1,0:T(8,128)S(1)} %get-tuple-element.85), channel_id=1, source_target_pairs={{0,15},{1,2},{2,1},{3,4},{4,3},{5,6},{6,5},{7,8},{8,7},{9,10},{10,... | collective-permute-start | bytes 1388552 | tf_op jit(solution)/shard_map/ppermute | solution.py:614
  4.7 10.0 %all-to-all-start.1 = ((f32[128,1,128]{2,1,0:T(1,128)}), f32[128,1,128]{2,1,0:T(1,128)S(1)}, u32[]{:S(2)}, u32[]{:S(2)}) async-start(f32[128,1,128]{2,1,0:T(1,128)} %get-tuple-element.90), calls=%async_computation.1 | async-start | bytes 131072 | tf_op jit(solution)/shard_map/all_to_all | solution.py:615
  15.3 0.0 collective-permute-done.1.second
  15.3 0.5 %shard_map.131 = (f32[2,8,16,128]{3,2,1,0:T(8,128)S(1)}, f32[8,16,128]{2,1,0:T(8,128)S(1)}, s32[16,128]{1,0:T(8,128)S(1)}, f32[16,128]{1,0:T(8,128)S(1)}, f32[29...) custom-call(f32[113,8,128]{2,1,0:T(8,128)S(1)} %get-tuple-element.79.own_y, f32[32,8,128]{2,1,0:T(8,128)S(1)} %get-tuple-element.83.sm, ...), custom_call_target="tpu_custom_call" | custom-call | tf_op jit(solution)/shard_map/pallas_call | solution.py:566
  15.8 1.4 %collective-permute-start.2 = (f32[29,8,128]{2,1,0:T(8,128)S(1)}, f32[29,8,128]{2,1,0:T(8,128)S(1)}, u32[]{:S(2)}, u32[]{:S(2)}) collective-permute-start(f32[29,8,128]{2,1,0:T(8,128)S(1)} %get-tuple-element.99), channel_id=1, source_target_pairs={{0,16},{16,32},{32,48},{48,64},{64,80},{80,96},{96,112},{112,0},{1... | collective-permute-start | bytes 356360 | tf_op jit(solution)/shard_map/ppermute | solution.py:581
  17.2 1.7 %collective-permute-start.3 = (f32[29,8,128]{2,1,0:T(8,128)S(1)}, f32[29,8,128]{2,1,0:T(8,128)S(1)}, u32[]{:S(2)}, u32[]{:S(2)}) collective-permute-start(f32[29,8,128]{2,1,0:T(8,128)S(1)} %get-tuple-element.100), channel_id=1, source_target_pairs={{16,0},{32,16},{48,32},{64,48},{80,64},{96,80},{112,96},{0,112},{1... | collective-permute-start | bytes 356360 | tf_op jit(solution)/shard_map/ppermute | solution.py:582
  18.9 3.5 %all-to-all-done.1 = f32[128,1,128]{2,1,0:T(1,128)S(1)} async-done(((f32[128,1,128]{2,1,0:T(1,128)}), f32[128,1,128]{2,1,0:T(1,128)S(1)}, u32[]{:S(2)}, u32[]{:S(2)}) %all-to-all-start.1) | async-done | bytes 65568 | tf_op jit(solution)/shard_map/all_to_all | solution.py:615
  22.4 1.2 %shard_map.132 = (f32[2,24,16,128]{3,2,1,0:T(8,128)S(1)}, f32[24,16,128]{2,1,0:T(8,128)S(1)}) custom-call(s32[1]{0:T(128)S(6)} %copy.31.source_cell, f32[1,2]{1,0:T(1,128)S(1)} %get-tuple-element.78.wavelet, f32[113,8,128]{2,1,0:T(8,128)S(1)} %get-tuple-element.79.own_y, f32[32,8,128]{2,1,0:T(8,128)S(1)} %get-tuple-element.83.sm, ...), custom_call_target="tpu_custom_call" | custom-call | tf_op jit(solution)/shard_map/pallas_call | solution.py:566
  23.6 1.9 %shard_map.133 = (f32[2,32,8,128]{3,2,1,0:T(8,128)S(1)}, f32[32,8,128]{2,1,0:T(8,128)S(1)}, f32[8,8,128]{2,1,0:T(8,128)S(1)}, s32[1]{0:T(128)}) custom-call(f32[128,128]{1,0:T(8,128)S(1)} %maximum_bitcast_fusion.got_ref, f32[24,16,128]{2,1,0:T(8,128)S(1)} %get-tuple-element.89.inner_courant), custom_call_target="tpu_custom_call" | custom-call | bytes 1000 | tf_op jit(solution)/shard_map/pallas_call | solution.py:566
  25.5 0.7 %while.14 = (s32[]{:T(128)}, f32[2,32,8,128]{3,2,1,0:T(8,128)S(1)}, f32[32,8,128]{2,1,0:T(8,128)S(1)}, f32[8,8,128]{2,1,0:T(8,128)S(1)}, s32[1]{0:T(128)}, /*ind...) while((s32[]{:T(128)}, f32[2,32,8,128]{3,2,1,0:T(8,128)S(1)}, f32[32,8,128]{2,1,0:T(8,128)S(1)}, ...), condition=%wide.region_1.0_spmd, body=%wide.region_0.0_spmd.sunk | while | flops 3 | bytes 1048713 | solution.py:656
  26.1 0.4 shard_map.134
  26.5 0.0 collective-permute-done.2.left
  26.5 0.0 collective-permute-done.3.right
  26.5 0.9 %shard_map.135 = (f32[16,8,128]{2,1,0:T(8,128)S(1)}, f32[16,8,128]{2,1,0:T(8,128)S(1)}, f32[4,32,128]{2,1,0:T(8,128)S(1)}, f32[2,16,128]{2,1,0:T(8,128)S(1)}, f32[2,16,128]{2,1,0:T(8,128)S(1)}) custom-call(s32[1]{0:T(128)S(6)} %copy.31.source_cell, f32[1,2]{1,0:T(1,128)S(1)} %get-tuple-element.78.wavelet, f32[113,8,128]{2,1,0:T(8,128)S(1)} %get-tuple-element.79.own_y, ...), custom_call_target="tpu_custom_call" | custom-call | tf_op jit(solution)/shard_map/pallas_call | solution.py:566
  27.5 1.8 %collective-permute-start.4 = (f32[2,16,128]{2,1,0:T(8,128)S(1)}, f32[2,16,128]{2,1,0:T(8,128)S(1)}, u32[]{:S(2)}, u32[]{:S(2)}) collective-permute-start(f32[2,16,128]{2,1,0:T(8,128)S(1)} %get-tuple-element.111), channel_id=1, source_target_pairs={{0,16},{16,32},{32,48},{48,64},{64,80},{80,96},{96,112},{112,0},{1... | collective-permute-start | bytes 49160 | tf_op jit(solution)/shard_map/ppermute | solution.py:581
  29.3 1.2 %collective-permute-start.5 = (f32[2,16,128]{2,1,0:T(8,128)S(1)}, f32[2,16,128]{2,1,0:T(8,128)S(1)}, u32[]{:S(2)}, u32[]{:S(2)}) collective-permute-start(f32[2,16,128]{2,1,0:T(8,128)S(1)} %get-tuple-element.112), channel_id=1, source_target_pairs={{16,0},{32,16},{48,32},{64,48},{80,64},{96,80},{112,96},{0,112},{1... | collective-permute-start | bytes 49160 | tf_op jit(solution)/shard_map/ppermute | solution.py:582
  30.5 0.7 %shard_map.136 = (f32[32,8,128]{2,1,0:T(8,128)}, f32[32,8,128]{2,1,0:T(8,128)}) custom-call(f32[16,8,128]{2,1,0:T(8,128)S(1)} %get-tuple-element.97.s_mid, f32[16,8,128]{2,1,0:T(8,128)S(1)} %get-tuple-element.98.r_mid, f32[16,8,128]{2,1,0:T(8,128)S(1)} %get-tuple-element.106.s_edge, f32[16,8,128]{2,1,0:T(8,128)S(1)} %get-tuple-element.107.r_edge), custom_call_target="tpu_custom_call" | custom-call | bytes 1000000 | tf_op jit(solution)/shard_map/pallas_call | solution.py:566
  31.2 0.4 collective-permute-done.4.left
  31.6 2.7 %collective-permute-done.5.right = f32[2,16,128]{2,1,0:T(8,128)S(1)} collective-permute-done((f32[2,16,128]{2,1,0:T(8,128)S(1)}, f32[2,16,128]{2,1,0:T(8,128)S(1)}, u32[]{:S(2)}, u32[]{:S(2)}) %collective-permute-start.5) | collective-permute-done | bytes 16416 | tf_op jit(solution)/shard_map/ppermute | solution.py:582
  34.3 0.8 %shard_map.137 = f32[16,8,128]{2,1,0:T(8,128)S(1)} custom-call(f32[32,8,128]{2,1,0:T(8,128)} %get-tuple-element.75.stored, f32[4,32,128]{2,1,0:T(8,128)S(1)} %get-tuple-element.110.near, f32[2,16,128]{2,1,0:T(8,128)S(1)} %collective-permute-done.4.left, f32[2,16,128]{2,1,0:T(8,128)S(1)} %collective-permute-done.5.right), custom_call_target="tpu_custom_call" | custom-call | tf_op jit(solution)/shard_map/pallas_call | solution.py:566
  35.1 12.7 %all_to_all.16.got = f32[16,8,128]{2,1,0:T(8,128)S(1)} all-to-all(f32[16,8,128]{2,1,0:T(8,128)S(1)} %shard_map.137), channel_id=1, replica_groups=mesh['gx'=8,'gy'=16] {'gy'}, dimensions={0} | all-to-all | bytes 131072 | tf_op jit(solution)/shard_map/all_to_all | solution.py:695
  47.8 0.7 %shard_map.138 = f32[2,8,1024]{2,1,0:T(8,128)} custom-call(f32[16,8,128]{2,1,0:T(8,128)S(1)} %all_to_all.16.got), custom_call_target="tpu_custom_call" | custom-call | tf_op jit(solution)/shard_map/pallas_call | solution.py:566
  (2 shorter events, 0.0 us)
Async XLA Ops:
  2.6 12.7 %collective-permute-start = (f32[113,8,128]{2,1,0:T(8,128)S(1)}, f32[113,8,128]{2,1,0:T(8,128)S(1)}, u32[]{:S(2)}, u32[]{:S(2)}) collective-permute-start(f32[113,8,128]{2,1,0:T(8,128)S(1)} %get-tuple-element.79.own_y), channel_id=1, source_target_pairs={{0,1},{1,0},{2,3},{3,2},{4,5},{5,4},{6,7},{7,6},{8,9},{9,8},{10,11... | collective-permute-start | bytes 1388552 | tf_op jit(solution)/shard_map/ppermute | solution.py:613
  3.4 11.9 %collective-permute-start.1 = (f32[113,8,128]{2,1,0:T(8,128)S(1)}, f32[113,8,128]{2,1,0:T(8,128)S(1)}, u32[]{:S(2)}, u32[]{:S(2)}) collective-permute-start(f32[113,8,128]{2,1,0:T(8,128)S(1)} %get-tuple-element.85), channel_id=1, source_target_pairs={{0,15},{1,2},{2,1},{3,4},{4,3},{5,6},{6,5},{7,8},{8,7},{9,10},{10,... | collective-permute-start | bytes 1388552 | tf_op jit(solution)/shard_map/ppermute | solution.py:614
  4.7 17.7 %all-to-all-start.1 = ((f32[128,1,128]{2,1,0:T(1,128)}), f32[128,1,128]{2,1,0:T(1,128)S(1)}, u32[]{:S(2)}, u32[]{:S(2)}) async-start(f32[128,1,128]{2,1,0:T(1,128)} %get-tuple-element.90), calls=%async_computation.1 | async-start | bytes 131072 | tf_op jit(solution)/shard_map/all_to_all | solution.py:615
  15.8 10.7 %collective-permute-start.2 = (f32[29,8,128]{2,1,0:T(8,128)S(1)}, f32[29,8,128]{2,1,0:T(8,128)S(1)}, u32[]{:S(2)}, u32[]{:S(2)}) collective-permute-start(f32[29,8,128]{2,1,0:T(8,128)S(1)} %get-tuple-element.99), channel_id=1, source_target_pairs={{0,16},{16,32},{32,48},{48,64},{64,80},{80,96},{96,112},{112,0},{1... | collective-permute-start | bytes 356360 | tf_op jit(solution)/shard_map/ppermute | solution.py:581
  17.2 9.3 %collective-permute-start.3 = (f32[29,8,128]{2,1,0:T(8,128)S(1)}, f32[29,8,128]{2,1,0:T(8,128)S(1)}, u32[]{:S(2)}, u32[]{:S(2)}) collective-permute-start(f32[29,8,128]{2,1,0:T(8,128)S(1)} %get-tuple-element.100), channel_id=1, source_target_pairs={{16,0},{32,16},{48,32},{64,48},{80,64},{96,80},{112,96},{0,112},{1... | collective-permute-start | bytes 356360 | tf_op jit(solution)/shard_map/ppermute | solution.py:582
  27.5 4.1 %collective-permute-start.4 = (f32[2,16,128]{2,1,0:T(8,128)S(1)}, f32[2,16,128]{2,1,0:T(8,128)S(1)}, u32[]{:S(2)}, u32[]{:S(2)}) collective-permute-start(f32[2,16,128]{2,1,0:T(8,128)S(1)} %get-tuple-element.111), channel_id=1, source_target_pairs={{0,16},{16,32},{32,48},{48,64},{64,80},{80,96},{96,112},{112,0},{1... | collective-permute-start | bytes 49160 | tf_op jit(solution)/shard_map/ppermute | solution.py:581
  29.3 5.0 %collective-permute-start.5 = (f32[2,16,128]{2,1,0:T(8,128)S(1)}, f32[2,16,128]{2,1,0:T(8,128)S(1)}, u32[]{:S(2)}, u32[]{:S(2)}) collective-permute-start(f32[2,16,128]{2,1,0:T(8,128)S(1)} %get-tuple-element.112), channel_id=1, source_target_pairs={{16,0},{32,16},{48,32},{64,48},{80,64},{96,80},{112,96},{0,112},{1... | collective-permute-start | bytes 49160 | tf_op jit(solution)/shard_map/ppermute | solution.py:582

commit v7 on v6

--- a/solution.py
+++ b/solution.py
@@ -218,23 +218,21 @@
 
 
 def pulse(source_cell, wavelet, step, row):
-    cell = source_cell[0]
+    cell = source_cell[0, 0]
     lane, sublane = iota((8, 128), 1), iota((8, 128), 0)
     at_row = sublane + (row + lax.axis_index("gy") * TY) == (cell >> 7) & 127
     return jnp.where((lane == cell & 127) & at_row, wavelet[0:1, step : step + 1], 0.0)
 
 
 def source_layer(source_cell):
-    return (source_cell[0] >> 14) - lax.axis_index("gx") * TX
-
-
-def advanced(i, at, x, e_ref, z_ref, m_ref, courant_ref, depth_ref, v_ref, pulses, source_x, new_ref):
+    return (source_cell[0, 0] >> 14) - lax.axis_index("gx") * TX
+
+
+def advanced(i, at, x, e_ref, z_ref, m_ref, courant_ref, depth_ref, v_ref, new_ref):
     for t in range(2):
         rows = slice(8 * t, 8 * t + 8)
         courant = courant_ref[i, rows]
         now, total = curvature(e_ref, 0, at, 8 + 8 * t, z_ref[0, i, rows])
-        if pulses is not None:
-            total = total - jnp.where(x == source_x, pulses[t], 0.0)
         new = 2.0 * now - m_ref[0, i, rows] + courant * total
         new_ref[0, i, rows] = overwritten(new, depth_ref[rows], v_ref[rows], x)
         now, total = curvature(e_ref, 1, at, 8 + 8 * t, z_ref[1, i, rows])
@@ -298,7 +296,7 @@
     for i in range(8):
         at, x = (i + 4, i) if i < 4 else (i + 12, i + 24)
         advanced(
-            i, at, x, e_ref, z_ref, m_ref, courant_ref, depth_ref, v_ref, None, None, new_ref
+            i, at, x, e_ref, z_ref, m_ref, courant_ref, depth_ref, v_ref, new_ref
         )
     for ref, to, rim, at in ((up_ref, 4, 28, 16), (down_ref, 0, 0, 4)):
         for f in range(2):
@@ -311,8 +309,7 @@
 
 
 def inner_kernel(
-    source_cell,
-    wavelet, own_y, sm, rm, c, first, second, depths, values,
+    own_y, sm, rm, c, first, second, depths, values,
     new_ref, courant_ref,
     e_ref, m_ref, z_ref,
 ):
@@ -334,8 +331,6 @@
             courant_ref[12:24, rows] = ref[96:108, 4:8] * keep
 
     in_order(beside, first, second)
-    pulses = [pulse(source_cell, wavelet, 0, 8 * t - 4) for t in range(2)]
-    source_x = source_layer(source_cell)
     matrix = depth_matrix()
     for f in range(2):
         rows = e_ref[f, 4:28, 8:24].reshape(384, 128)
@@ -343,7 +338,7 @@
 
     def layer(i, carry):
         advanced(
-            i, i + 4, i + 4, e_ref, z_ref, m_ref, courant_ref, depths, values, pulses, source_x, new_ref
+            i, i + 4, i + 4, e_ref, z_ref, m_ref, courant_ref, depths, values, new_ref
         )
         return carry
 
@@ -374,16 +369,29 @@
 
 def middle_kernel(
     source_cell,
-    wavelet, own_y, c, depth, values, inner, inner_courant, own, rim_y,
-    r1_ref, s_v, r_v, sub_ref,
+    wavelet, own_y, c, depth, values, inner, inner_courant, depths, own, rim_y,
+    new_ref, s_v, r_v, sub_ref,
     o_ref, z_ref,
 ):
     o_ref[0, :, 4:20] = inner[0]
     o_ref[1, :, 8:16] = inner[1, :, 4:12] + inner_courant[:, 4:12] * own[0, 4:28]
     o_ref[1, :, 4:8] = inner[1, :, 0:4] + inner_courant[:, 0:4] * rim_y[4:28, 0:4]
     o_ref[1, :, 16:20] = inner[1, :, 12:16] + inner_courant[:, 12:16] * rim_y[4:28, 4:8]
-    for half in range(2):
-        r1_ref[8 * half : 8 * half + 8] = o_ref[1, 16 * half : 16 * half + 8, 4:20]
+    k = (source_cell[0, 0] >> 14) - lax.axis_index("gx") * TX - 4
+
+    @pl.when((k >= 0) & (k < 24))
+    def _():
+        for t in range(2):
+            rows, at = slice(8 * t, 8 * t + 8), slice(4 + 8 * t, 12 + 8 * t)
+            column = jnp.full((8, 128), k + 4, I32)
+            relative = iota((8, 128), 1) - jnp.take_along_axis(depths[rows], column, axis=1)
+            amount = inner_courant[k, rows] * pulse(source_cell, wavelet, 0, 8 * t - 4)
+            free = (relative < 0) | (relative >= 4)
+            o_ref[0, k, at] = o_ref[0, k, at] - jnp.where(free, amount, 0.0)
+
+    for f in range(2):
+        for half in range(2):
+            new_ref[f, 8 * half : 8 * half + 8] = o_ref[f, 16 * half : 16 * half + 8, 4:20]
     matrix = depth_matrix()
     for f in range(2):
         rows = o_ref[f, 4:20, 8:16].reshape(128, 128)
@@ -404,8 +412,8 @@
 
 def steps_kernel(
     source_cell,
-    wavelet, own_y, c, depth, values, left, right, edge, edge_courant, inner, depths,
-    own, rim_y, rim_x, r1, sub_mid,
+    wavelet, own_y, c, depth, values, left, right, edge, edge_courant, depths,
+    own, rim_y, rim_x, inner, sub_mid,
     s_v, r_v, near_ref, up_ref, down_ref,
     o_ref, h_ref, z_ref, sub_ref,
 ):
@@ -419,8 +427,8 @@
         o_ref[1, to, 16:20] = edge[1, part, 12:16] + edge_courant[part, 12:16] * rim_y[x, 4:8]
     for half in range(2):
         to = slice(8 + 16 * half, 16 + 16 * half)
-        o_ref[0, to, 4:20] = inner[0, 16 * half : 16 * half + 8]
-        o_ref[1, to, 4:20] = r1[8 * half : 8 * half + 8]
+        for f in range(2):
+            o_ref[f, to, 4:20] = inner[f, 8 * half : 8 * half + 8]
     source_x = source_layer(source_cell)
     pulses = [pulse(source_cell, wavelet, 0, row) for row in (-4, 4, 0)]
     for side, ref, keep in ((0, left, keep_left), (1, right, keep_right)):
@@ -597,6 +605,7 @@
     strip_values,
 ):
     cells = receiver_cells.reshape(1, RECEIVERS)
+    near_cell = source_cell.reshape(1, 1)
     tile, sent_shape = (TX, TY, TZ), ((DEVICES, 1, 128), F32)
     listed = [((1, RECEIVERS), I32), ((2, RECEIVERS), F32)]
     fields = (source_now, receiver_now, source_next, receiver_next, courant, strip_depth, strip_values)
@@ -629,8 +638,7 @@
     inner, inner_courant = call(
         inner_kernel,
         [((2, 24, 16, 128), F32), ((24, 16, 128), F32)],
-        [near_wavelet, first_y, near_sm, near_rm, near_c, first, second, depths, strips],
-        scalars=[source_cell],
+        [first_y, near_sm, near_rm, near_c, first, second, depths, strips],
         scratch=[
             pltpu.VMEM((2, 32, 32, 128), F32),
             pltpu.VMEM((2, 24, 16, 128), F32),
@@ -641,37 +649,37 @@
     own, rim_y, rim_x, rounds = call(collect_kernel, [*sums, ((1,), I32)], [got, inner_courant], out_scalars=1, weight=1000)
 
     def another(state):
-        turn, *partial = state
+        left_over, *partial = state
         (more,) = call(
             route_more_kernel,
             [sent_shape],
             [],
-            scalars=[(turn * SLOTS).reshape(1)],
+            scalars=[(left_over - 1) * SLOTS],
             hbm=[cells, receiver_traces],
             scratch=[pltpu.VMEM(*shape) for shape in listed] + [pltpu.SemaphoreType.DMA((2,))],
         )
         more = lax.all_to_all(more, ("gx", "gy"), 0, 0, tiled=True)
-        return (turn + 1, *call(collect_more_kernel, sums, [more, *partial]))
+        return (left_over - 1, *call(collect_more_kernel, sums, [more, *partial]))
 
     _, own, rim_y, rim_x = lax.while_loop(
-        lambda state: state[0] < rounds[0], another, (jnp.int32(1), own, rim_y, rim_x)
+        lambda state: state[0][0] > 1, another, (rounds, own, rim_y, rim_x)
     )
     part = (16, TY, TZ)
-    r1, s_mid, r_mid, sub_mid = call(
+    new1, s_mid, r_mid, sub_mid = call(
         middle_kernel,
-        [((16, 16, 128), F32), (part, F32), (part, F32), ((4, 2, 16, 128), F32)],
-        [near_wavelet, first_y, near_c, near_depth, near_values, inner, inner_courant, own, rim_y],
-        scalars=[source_cell],
+        [((2, 16, 16, 128), F32), (part, F32), (part, F32), ((4, 2, 16, 128), F32)],
+        [
+            near_cell, near_wavelet, first_y, near_c, near_depth, near_values, inner, inner_courant, depths, own, rim_y,
+        ],
         scratch=[pltpu.VMEM((2, 24, 24, 128), F32), pltpu.VMEM((2, 16, 8, 128), F32)],
     )
     s_edge, r_edge, near, up, down = call(
         steps_kernel,
         [(part, F32), (part, F32), ((4, 32, 128), F32), ((2, 16, 128), F32), ((2, 16, 128), F32)],
         [
-            near_wavelet, first_y, near_c, near_depth, near_values, left, right, edge, edge_courant,
-            inner, depths, own, rim_y, rim_x, r1, sub_mid,
+            near_cell, near_wavelet, first_y, near_c, near_depth, near_values, left, right, edge, edge_courant,
+            depths, own, rim_y, rim_x, new1, sub_mid,
         ],
-        scalars=[source_cell],
         scratch=[
             pltpu.VMEM((2, 40, 24, 128), F32),
             pltpu.VMEM((2, 2, 4, 16, 128), F32),

time: 48.7 us -> 48.8 us (level)
  no operation moved by 1% of the time
where the time goes in v7:
time: 48.8 us; the launch traced here: 48.5 us
  starting transfers between devices  18.1 us (37%)
  blocking collectives  12.7 us (26%)
  Pallas kernels  9.17 us (19%)
  waiting for transfers between devices  6.58 us (13%)
  between operations  1.38 us (3%)
  loops' own time  0.65 us (1%)
    all_to_all x1, blocking collectives, body(): angles = lax.all_to_all(angles, 'gy', 0, 0, tiled=True)  12.7 us
    all_to_all x1, starting transfers between devices, body(): got = lax.all_to_all(sent, ('gx', 'gy'), 0, 0, tiled=True)  10 us
    pallas_call x9, Pallas kernels, call(): pl.pallas_call(kernel, out_shape=[jax.ShapeDtypeStruct(shape, kind) for s...  9.17 us
    all_to_all x1, waiting for transfers between devices, body(): got = lax.all_to_all(sent, ('gx', 'gy'), 0, 0, tiled=True)  3.5 us
    ppermute x2, starting transfers between devices, both_ways(): lax.ppermute(to_next, axis, [(i, (i + 1) % size) for i in range(size)])  3.18 us
    ppermute x2, starting transfers between devices, both_ways(): lax.ppermute(to_last, axis, [((i + 1) % size, i) for i in range(size)])  2.84 us
    ppermute x2, waiting for transfers between devices, both_ways(): lax.ppermute(to_last, axis, [((i + 1) % size, i) for i in range(size)])  2.7 us
    ppermute x1, starting transfers between devices, body(): lax.ppermute(second_y, 'gy', [(i, (i + 1 if i % 2 else i - 1) % GY) for i...  1.27 us
  transfers between devices with their start and end apart: 7, of which 3 were waited for; matrix products, arithmetic and copies ran while one was open for 0% of the time, Pallas kernels for 10%

profile of v7, /device:TPU:5, one launch (start us, length us, event | category | flops | bytes accessed | tf_op | source)
XLA Modules:
  0.0 48.5 jit_solution(11057144610361287333)
XLA Ops:
  0.6 2.0 %shard_map.130 = (f32[113,8,128]{2,1,0:T(8,128)S(1)}, f32[113,8,128]{2,1,0:T(8,128)S(1)}, f32[1,2]{1,0:T(1,128)S(1)}, f32[32,8,128]{2,1,0:T(8,128)S(1)}, f32[32,...) custom-call(s32[1,256]{1,0:T(1,128)} %bitcast.11, ...), custom_call_target="tpu_custom_call" | custom-call | tf_op jit(solution)/shard_map/pallas_call | solution.py:574
  2.6 0.8 %collective-permute-start = (f32[113,8,128]{2,1,0:T(8,128)S(1)}, f32[113,8,128]{2,1,0:T(8,128)S(1)}, u32[]{:S(2)}, u32[]{:S(2)}) collective-permute-start(f32[113,8,128]{2,1,0:T(8,128)S(1)} %get-tuple-element.116.own_y), channel_id=1, source_target_pairs={{0,1},{1,0},{2,3},{3,2},{4,5},{5,4},{6,7},{7,6},{8,9},{9,8},{10,11... | collective-permute-start | bytes 1388552 | tf_op jit(solution)/shard_map/ppermute | solution.py:622
  3.4 1.3 %collective-permute-start.1 = (f32[113,8,128]{2,1,0:T(8,128)S(1)}, f32[113,8,128]{2,1,0:T(8,128)S(1)}, u32[]{:S(2)}, u32[]{:S(2)}) collective-permute-start(f32[113,8,128]{2,1,0:T(8,128)S(1)} %get-tuple-element.122), channel_id=1, source_target_pairs={{0,15},{1,2},{2,1},{3,4},{4,3},{5,6},{6,5},{7,8},{8,7},{9,10},{10,... | collective-permute-start | bytes 1388552 | tf_op jit(solution)/shard_map/ppermute | solution.py:623
  4.7 10.0 %all-to-all-start.1 = ((f32[128,1,128]{2,1,0:T(1,128)}), f32[128,1,128]{2,1,0:T(1,128)S(1)}, u32[]{:S(2)}, u32[]{:S(2)}) async-start(f32[128,1,128]{2,1,0:T(1,128)} %get-tuple-element.127), calls=%async_computation.1 | async-start | bytes 131072 | tf_op jit(solution)/shard_map/all_to_all | solution.py:624
  15.3 0.0 collective-permute-done.first
  15.3 0.0 collective-permute-done.1.second
  15.3 0.5 %shard_map.131 = (f32[2,8,16,128]{3,2,1,0:T(8,128)S(1)}, f32[8,16,128]{2,1,0:T(8,128)S(1)}, s32[16,128]{1,0:T(8,128)S(1)}, f32[16,128]{1,0:T(8,128)S(1)}, f32[29...) custom-call(f32[113,8,128]{2,1,0:T(8,128)S(1)} %get-tuple-element.116.own_y, f32[32,8,128]{2,1,0:T(8,128)S(1)} %get-tuple-element.120.sm, ...), custom_call_target="tpu_custom_call" | custom-call | tf_op jit(solution)/shard_map/pallas_call | solution.py:574
  15.8 1.4 %collective-permute-start.2 = (f32[29,8,128]{2,1,0:T(8,128)S(1)}, f32[29,8,128]{2,1,0:T(8,128)S(1)}, u32[]{:S(2)}, u32[]{:S(2)}) collective-permute-start(f32[29,8,128]{2,1,0:T(8,128)S(1)} %get-tuple-element.136), channel_id=1, source_target_pairs={{0,16},{16,32},{32,48},{48,64},{64,80},{80,96},{96,112},{112,0},{1... | collective-permute-start | bytes 356360 | tf_op jit(solution)/shard_map/ppermute | solution.py:589
  17.2 1.7 %collective-permute-start.3 = (f32[29,8,128]{2,1,0:T(8,128)S(1)}, f32[29,8,128]{2,1,0:T(8,128)S(1)}, u32[]{:S(2)}, u32[]{:S(2)}) collective-permute-start(f32[29,8,128]{2,1,0:T(8,128)S(1)} %get-tuple-element.137), channel_id=1, source_target_pairs={{16,0},{32,16},{48,32},{64,48},{80,64},{96,80},{112,96},{0,112},{1... | collective-permute-start | bytes 356360 | tf_op jit(solution)/shard_map/ppermute | solution.py:590
  18.9 3.5 %all-to-all-done.1 = f32[128,1,128]{2,1,0:T(1,128)S(1)} async-done(((f32[128,1,128]{2,1,0:T(1,128)}), f32[128,1,128]{2,1,0:T(1,128)S(1)}, u32[]{:S(2)}, u32[]{:S(2)}) %all-to-all-start.1) | async-done | bytes 65568 | tf_op jit(solution)/shard_map/all_to_all | solution.py:624
  22.4 1.2 %shard_map.132 = (f32[2,24,16,128]{3,2,1,0:T(8,128)S(1)}, f32[24,16,128]{2,1,0:T(8,128)S(1)}) custom-call(f32[113,8,128]{2,1,0:T(8,128)S(1)} %get-tuple-element.116.own_y, f32[32,8,128]{2,1,0:T(8,128)S(1)} %get-tuple-element.120.sm, f32[32,8,128]{2,1,0:T(8,128)S(1)} %get-tuple-element.121.rm, f32[32,8,128]{2,1,0:T(8,128)S(1)} %get-tuple-element.117.c, ...), custom_call_target="tpu_custom_call" | custom-call | tf_op jit(solution)/shard_map/pallas_call | solution.py:574
  23.6 1.9 %shard_map.133 = (f32[2,32,8,128]{3,2,1,0:T(8,128)S(1)}, f32[32,8,128]{2,1,0:T(8,128)S(1)}, f32[8,8,128]{2,1,0:T(8,128)S(1)}, s32[1]{0:T(128)}) custom-call(f32[128,128]{1,0:T(8,128)S(1)} %maximum_bitcast_fusion.got_ref, f32[24,16,128]{2,1,0:T(8,128)S(1)} %get-tuple-element.126.inner_courant), custom_call_target="tpu_custom_call" | custom-call | bytes 1000 | tf_op jit(solution)/shard_map/pallas_call | solution.py:574
  25.4 0.7 %while.16 = (s32[1]{0:T(128)}, f32[2,32,8,128]{3,2,1,0:T(8,128)S(1)}, f32[32,8,128]{2,1,0:T(8,128)S(1)}, f32[8,8,128]{2,1,0:T(8,128)S(1)}, s32[1,256]{1,0:T(1,12...) while((s32[1]{0:T(128)}, f32[2,32,8,128]{3,2,1,0:T(8,128)S(1)}, f32[32,8,128]{2,1,0:T(8,128)S(1)}, ...), condition=%wide.region_1.0_spmd, body=%wide.region_0.0_spmd | while | flops 3 | bytes 1048705 | solution.py:664
  26.1 0.4 shard_map.134
  26.5 0.0 collective-permute-done.3.right
  26.5 1.0 %shard_map.135 = (f32[16,8,128]{2,1,0:T(8,128)S(1)}, f32[16,8,128]{2,1,0:T(8,128)S(1)}, f32[4,32,128]{2,1,0:T(8,128)S(1)}, f32[2,16,128]{2,1,0:T(8,128)S(1)}, f32[2,16,128]{2,1,0:T(8,128)S(1)}) custom-call(s32[1,1]{1,0:T(1,128)} %bitcast.9.source_cell, f32[1,2]{1,0:T(1,128)S(1)} %get-tuple-element.115.wavelet, f32[113,8,128]{2,1,0:T(8,128)S(1)} %get-tuple-element.116.own_y, ...), custom_call_target="tpu_custom_call" | custom-call | tf_op jit(solution)/shard_map/pallas_call | solution.py:574
  27.5 1.8 %collective-permute-start.4 = (f32[2,16,128]{2,1,0:T(8,128)S(1)}, f32[2,16,128]{2,1,0:T(8,128)S(1)}, u32[]{:S(2)}, u32[]{:S(2)}) collective-permute-start(f32[2,16,128]{2,1,0:T(8,128)S(1)} %get-tuple-element.148), channel_id=1, source_target_pairs={{0,16},{16,32},{32,48},{48,64},{64,80},{80,96},{96,112},{112,0},{1... | collective-permute-start | bytes 49160 | tf_op jit(solution)/shard_map/ppermute | solution.py:589
  29.3 1.2 %collective-permute-start.5 = (f32[2,16,128]{2,1,0:T(8,128)S(1)}, f32[2,16,128]{2,1,0:T(8,128)S(1)}, u32[]{:S(2)}, u32[]{:S(2)}) collective-permute-start(f32[2,16,128]{2,1,0:T(8,128)S(1)} %get-tuple-element.149), channel_id=1, source_target_pairs={{16,0},{32,16},{48,32},{64,48},{80,64},{96,80},{112,96},{0,112},{1... | collective-permute-start | bytes 49160 | tf_op jit(solution)/shard_map/ppermute | solution.py:590
  30.5 0.7 %shard_map.136 = (f32[32,8,128]{2,1,0:T(8,128)}, f32[32,8,128]{2,1,0:T(8,128)}) custom-call(f32[16,8,128]{2,1,0:T(8,128)S(1)} %get-tuple-element.134.s_mid, f32[16,8,128]{2,1,0:T(8,128)S(1)} %get-tuple-element.135.r_mid, f32[16,8,128]{2,1,0:T(8,128)S(1)} %get-tuple-element.143.s_edge, f32[16,8,128]{2,1,0:T(8,128)S(1)} %get-tuple-element.144.r_edge), custom_call_target="tpu_custom_call" | custom-call | bytes 1000000 | tf_op jit(solution)/shard_map/pallas_call | solution.py:574
  31.3 0.4 collective-permute-done.4.left
  31.6 2.7 %collective-permute-done.5.right = f32[2,16,128]{2,1,0:T(8,128)S(1)} collective-permute-done((f32[2,16,128]{2,1,0:T(8,128)S(1)}, f32[2,16,128]{2,1,0:T(8,128)S(1)}, u32[]{:S(2)}, u32[]{:S(2)}) %collective-permute-start.5) | collective-permute-done | bytes 16416 | tf_op jit(solution)/shard_map/ppermute | solution.py:590
  34.3 0.8 %shard_map.137 = f32[16,8,128]{2,1,0:T(8,128)S(1)} custom-call(f32[32,8,128]{2,1,0:T(8,128)} %get-tuple-element.112.stored, f32[4,32,128]{2,1,0:T(8,128)S(1)} %get-tuple-element.147.near, f32[2,16,128]{2,1,0:T(8,128)S(1)} %collective-permute-done.4.left, f32[2,16,128]{2,1,0:T(8,128)S(1)} %collective-permute-done.5.right), custom_call_target="tpu_custom_call" | custom-call | tf_op jit(solution)/shard_map/pallas_call | solution.py:574
  35.1 12.7 %all_to_all.15.got = f32[16,8,128]{2,1,0:T(8,128)S(1)} all-to-all(f32[16,8,128]{2,1,0:T(8,128)S(1)} %shard_map.137), channel_id=1, replica_groups=mesh['gx'=8,'gy'=16] {'gy'}, dimensions={0} | all-to-all | bytes 131072 | tf_op jit(solution)/shard_map/all_to_all | solution.py:703
  47.8 0.7 %shard_map.138 = f32[2,8,1024]{2,1,0:T(8,128)} custom-call(f32[16,8,128]{2,1,0:T(8,128)S(1)} %all_to_all.15.got), custom_call_target="tpu_custom_call" | custom-call | tf_op jit(solution)/shard_map/pallas_call | solution.py:574
  (2 shorter events, 0.0 us)
Async XLA Ops:
  2.6 12.7 %collective-permute-start = (f32[113,8,128]{2,1,0:T(8,128)S(1)}, f32[113,8,128]{2,1,0:T(8,128)S(1)}, u32[]{:S(2)}, u32[]{:S(2)}) collective-permute-start(f32[113,8,128]{2,1,0:T(8,128)S(1)} %get-tuple-element.116.own_y), channel_id=1, source_target_pairs={{0,1},{1,0},{2,3},{3,2},{4,5},{5,4},{6,7},{7,6},{8,9},{9,8},{10,11... | collective-permute-start | bytes 1388552 | tf_op jit(solution)/shard_map/ppermute | solution.py:622
  3.4 11.9 %collective-permute-start.1 = (f32[113,8,128]{2,1,0:T(8,128)S(1)}, f32[113,8,128]{2,1,0:T(8,128)S(1)}, u32[]{:S(2)}, u32[]{:S(2)}) collective-permute-start(f32[113,8,128]{2,1,0:T(8,128)S(1)} %get-tuple-element.122), channel_id=1, source_target_pairs={{0,15},{1,2},{2,1},{3,4},{4,3},{5,6},{6,5},{7,8},{8,7},{9,10},{10,... | collective-permute-start | bytes 1388552 | tf_op jit(solution)/shard_map/ppermute | solution.py:623
  4.7 17.7 %all-to-all-start.1 = ((f32[128,1,128]{2,1,0:T(1,128)}), f32[128,1,128]{2,1,0:T(1,128)S(1)}, u32[]{:S(2)}, u32[]{:S(2)}) async-start(f32[128,1,128]{2,1,0:T(1,128)} %get-tuple-element.127), calls=%async_computation.1 | async-start | bytes 131072 | tf_op jit(solution)/shard_map/all_to_all | solution.py:624
  15.8 10.7 %collective-permute-start.2 = (f32[29,8,128]{2,1,0:T(8,128)S(1)}, f32[29,8,128]{2,1,0:T(8,128)S(1)}, u32[]{:S(2)}, u32[]{:S(2)}) collective-permute-start(f32[29,8,128]{2,1,0:T(8,128)S(1)} %get-tuple-element.136), channel_id=1, source_target_pairs={{0,16},{16,32},{32,48},{48,64},{64,80},{80,96},{96,112},{112,0},{1... | collective-permute-start | bytes 356360 | tf_op jit(solution)/shard_map/ppermute | solution.py:589
  17.2 9.3 %collective-permute-start.3 = (f32[29,8,128]{2,1,0:T(8,128)S(1)}, f32[29,8,128]{2,1,0:T(8,128)S(1)}, u32[]{:S(2)}, u32[]{:S(2)}) collective-permute-start(f32[29,8,128]{2,1,0:T(8,128)S(1)} %get-tuple-element.137), channel_id=1, source_target_pairs={{16,0},{32,16},{48,32},{64,48},{80,64},{96,80},{112,96},{0,112},{1... | collective-permute-start | bytes 356360 | tf_op jit(solution)/shard_map/ppermute | solution.py:590
  27.5 4.1 %collective-permute-start.4 = (f32[2,16,128]{2,1,0:T(8,128)S(1)}, f32[2,16,128]{2,1,0:T(8,128)S(1)}, u32[]{:S(2)}, u32[]{:S(2)}) collective-permute-start(f32[2,16,128]{2,1,0:T(8,128)S(1)} %get-tuple-element.148), channel_id=1, source_target_pairs={{0,16},{16,32},{32,48},{48,64},{64,80},{80,96},{96,112},{112,0},{1... | collective-permute-start | bytes 49160 | tf_op jit(solution)/shard_map/ppermute | solution.py:589
  29.3 5.0 %collective-permute-start.5 = (f32[2,16,128]{2,1,0:T(8,128)S(1)}, f32[2,16,128]{2,1,0:T(8,128)S(1)}, u32[]{:S(2)}, u32[]{:S(2)}) collective-permute-start(f32[2,16,128]{2,1,0:T(8,128)S(1)} %get-tuple-element.149), channel_id=1, source_target_pairs={{16,0},{32,16},{48,32},{64,48},{80,64},{96,80},{112,96},{0,112},{1... | collective-permute-start | bytes 49160 | tf_op jit(solution)/shard_map/ppermute | solution.py:590

commit v8 on v6

--- a/solution.py
+++ b/solution.py
@@ -549,12 +549,21 @@
         out_ref[b] = jnp.where(lane < 64, packed, other)
 
 
-def arrange_kernel(got, out_ref):
+def arrange_kernel(got, image, out_v, sems):
     lane = iota((8, 128), 1)
-    for t in range(8):
-        even, odd = got[2 * t], got[2 * t + 1]
-        out_ref[0, :, 128 * t : 128 * t + 128] = jnp.where(lane < 64, even, pltpu.roll(odd, 64, 1))
-        out_ref[1, :, 128 * t : 128 * t + 128] = jnp.where(lane < 64, pltpu.roll(even, 64, 1), odd)
+    copies = []
+    for a in range(2):
+        for t in range(8):
+            even, odd = got[2 * t], got[2 * t + 1]
+            if a == 0:
+                odd = pltpu.roll(odd, 64, 1)
+            else:
+                even = pltpu.roll(even, 64, 1)
+            out_v[a, :, 128 * t : 128 * t + 128] = jnp.where(lane < 64, even, odd)
+        copies.append(pltpu.make_async_copy(out_v.at[a], image.at[a], sems.at[a]))
+        copies[a].start()
+    for copy in copies:
+        copy.wait()
 
 
 def call(kernel, outs, arrays, scalars=(), hbm=(), out_scalars=0, out_hbm=(), scratch=(), weight=0):
@@ -693,7 +702,14 @@
         scratch=[pltpu.VMEM((4, 64, 128), F32)],
     )
     angles = lax.all_to_all(angles, "gy", 0, 0, tiled=True)
-    (image,) = call(arrange_kernel, [((2, 8, 1024), F32)], [angles])
+    image_shape = ((2, 8, 1024), F32)
+    (image,) = call(
+        arrange_kernel,
+        [image_shape],
+        [angles],
+        out_hbm=(0,),
+        scratch=[pltpu.VMEM(*image_shape), pltpu.SemaphoreType.DMA((2,))],
+    )
     return source_field, receiver_field, image
 
 

time: 48.7 us -> 48.7 us (level)
  no operation moved by 1% of the time
where the time goes in v8:
time: 48.7 us; the launch traced here: 48.5 us
  starting transfers between devices  18 us (37%)
  blocking collectives  12.7 us (26%)
  Pallas kernels  9.14 us (19%)
  waiting for transfers between devices  6.58 us (14%)
  between operations  1.38 us (3%)
  loops' own time  0.65 us (1%)
    all_to_all x1, blocking collectives, body(): angles = lax.all_to_all(angles, 'gy', 0, 0, tiled=True)  12.7 us
    all_to_all x1, starting transfers between devices, body(): got = lax.all_to_all(sent, ('gx', 'gy'), 0, 0, tiled=True)  10 us
    pallas_call x9, Pallas kernels, call(): pl.pallas_call(kernel, out_shape=[jax.ShapeDtypeStruct(shape, kind) for s...  9.14 us
    all_to_all x1, waiting for transfers between devices, body(): got = lax.all_to_all(sent, ('gx', 'gy'), 0, 0, tiled=True)  3.51 us
    ppermute x2, starting transfers between devices, both_ways(): lax.ppermute(to_next, axis, [(i, (i + 1) % size) for i in range(size)])  3.18 us
    ppermute x2, starting transfers between devices, both_ways(): lax.ppermute(to_last, axis, [((i + 1) % size, i) for i in range(size)])  2.85 us
    ppermute x2, waiting for transfers between devices, both_ways(): lax.ppermute(to_last, axis, [((i + 1) % size, i) for i in range(size)])  2.69 us
    ppermute x1, starting transfers between devices, body(): lax.ppermute(second_y, 'gy', [(i, (i + 1 if i % 2 else i - 1) % GY) for i...  1.27 us
  transfers between devices with their start and end apart: 7, of which 3 were waited for; matrix products, arithmetic and copies ran while one was open for 0% of the time, Pallas kernels for 10%

profile of v8, /device:TPU:5, one launch (start us, length us, event | category | flops | bytes accessed | tf_op | source)
XLA Modules:
  0.0 48.5 jit_solution(6436896907690042452)
XLA Ops:
  0.6 2.0 %shard_map.130 = (f32[113,8,128]{2,1,0:T(8,128)S(1)}, f32[113,8,128]{2,1,0:T(8,128)S(1)}, f32[1,2]{1,0:T(1,128)S(1)}, f32[32,8,128]{2,1,0:T(8,128)S(1)}, f32[32,...) custom-call(s32[1,256]{1,0:T(1,128)} %bitcast.11, ...), custom_call_target="tpu_custom_call" | custom-call | tf_op jit(solution)/shard_map/pallas_call | solution.py:575
  2.6 0.8 %collective-permute-start = (f32[113,8,128]{2,1,0:T(8,128)S(1)}, f32[113,8,128]{2,1,0:T(8,128)S(1)}, u32[]{:S(2)}, u32[]{:S(2)}) collective-permute-start(f32[113,8,128]{2,1,0:T(8,128)S(1)} %get-tuple-element.79.own_y), channel_id=1, source_target_pairs={{0,1},{1,0},{2,3},{3,2},{4,5},{5,4},{6,7},{7,6},{8,9},{9,8},{10,11... | collective-permute-start | bytes 1388552 | tf_op jit(solution)/shard_map/ppermute | solution.py:622
  3.4 1.3 %collective-permute-start.1 = (f32[113,8,128]{2,1,0:T(8,128)S(1)}, f32[113,8,128]{2,1,0:T(8,128)S(1)}, u32[]{:S(2)}, u32[]{:S(2)}) collective-permute-start(f32[113,8,128]{2,1,0:T(8,128)S(1)} %get-tuple-element.85), channel_id=1, source_target_pairs={{0,15},{1,2},{2,1},{3,4},{4,3},{5,6},{6,5},{7,8},{8,7},{9,10},{10,... | collective-permute-start | bytes 1388552 | tf_op jit(solution)/shard_map/ppermute | solution.py:623
  4.7 10.0 %all-to-all-start.1 = ((f32[128,1,128]{2,1,0:T(1,128)}), f32[128,1,128]{2,1,0:T(1,128)S(1)}, u32[]{:S(2)}, u32[]{:S(2)}) async-start(f32[128,1,128]{2,1,0:T(1,128)} %get-tuple-element.90), calls=%async_computation.1 | async-start | bytes 131072 | tf_op jit(solution)/shard_map/all_to_all | solution.py:624
  15.3 0.0 collective-permute-done.first
  15.3 0.0 collective-permute-done.1.second
  15.3 0.5 %shard_map.131 = (f32[2,8,16,128]{3,2,1,0:T(8,128)S(1)}, f32[8,16,128]{2,1,0:T(8,128)S(1)}, s32[16,128]{1,0:T(8,128)S(1)}, f32[16,128]{1,0:T(8,128)S(1)}, f32[29...) custom-call(f32[113,8,128]{2,1,0:T(8,128)S(1)} %get-tuple-element.79.own_y, f32[32,8,128]{2,1,0:T(8,128)S(1)} %get-tuple-element.83.sm, ...), custom_call_target="tpu_custom_call" | custom-call | tf_op jit(solution)/shard_map/pallas_call | solution.py:575
  15.8 1.4 %collective-permute-start.2 = (f32[29,8,128]{2,1,0:T(8,128)S(1)}, f32[29,8,128]{2,1,0:T(8,128)S(1)}, u32[]{:S(2)}, u32[]{:S(2)}) collective-permute-start(f32[29,8,128]{2,1,0:T(8,128)S(1)} %get-tuple-element.99), channel_id=1, source_target_pairs={{0,16},{16,32},{32,48},{48,64},{64,80},{80,96},{96,112},{112,0},{1... | collective-permute-start | bytes 356360 | tf_op jit(solution)/shard_map/ppermute | solution.py:590
  17.2 1.7 %collective-permute-start.3 = (f32[29,8,128]{2,1,0:T(8,128)S(1)}, f32[29,8,128]{2,1,0:T(8,128)S(1)}, u32[]{:S(2)}, u32[]{:S(2)}) collective-permute-start(f32[29,8,128]{2,1,0:T(8,128)S(1)} %get-tuple-element.100), channel_id=1, source_target_pairs={{16,0},{32,16},{48,32},{64,48},{80,64},{96,80},{112,96},{0,112},{1... | collective-permute-start | bytes 356360 | tf_op jit(solution)/shard_map/ppermute | solution.py:591
  18.9 3.5 %all-to-all-done.1 = f32[128,1,128]{2,1,0:T(1,128)S(1)} async-done(((f32[128,1,128]{2,1,0:T(1,128)}), f32[128,1,128]{2,1,0:T(1,128)S(1)}, u32[]{:S(2)}, u32[]{:S(2)}) %all-to-all-start.1) | async-done | bytes 65568 | tf_op jit(solution)/shard_map/all_to_all | solution.py:624
  22.4 1.2 %shard_map.132 = (f32[2,24,16,128]{3,2,1,0:T(8,128)S(1)}, f32[24,16,128]{2,1,0:T(8,128)S(1)}) custom-call(s32[1]{0:T(128)S(6)} %copy.31.source_cell, f32[1,2]{1,0:T(1,128)S(1)} %get-tuple-element.78.wavelet, f32[113,8,128]{2,1,0:T(8,128)S(1)} %get-tuple-element.79.own_y, f32[32,8,128]{2,1,0:T(8,128)S(1)} %get-tuple-element.83.sm, ...), custom_call_target="tpu_custom_call" | custom-call | tf_op jit(solution)/shard_map/pallas_call | solution.py:575
  23.6 1.9 %shard_map.133 = (f32[2,32,8,128]{3,2,1,0:T(8,128)S(1)}, f32[32,8,128]{2,1,0:T(8,128)S(1)}, f32[8,8,128]{2,1,0:T(8,128)S(1)}, s32[1]{0:T(128)}) custom-call(f32[128,128]{1,0:T(8,128)S(1)} %maximum_bitcast_fusion.got_ref, f32[24,16,128]{2,1,0:T(8,128)S(1)} %get-tuple-element.89.inner_courant), custom_call_target="tpu_custom_call" | custom-call | bytes 1000 | tf_op jit(solution)/shard_map/pallas_call | solution.py:575
  25.5 0.7 %while.14 = (s32[]{:T(128)}, f32[2,32,8,128]{3,2,1,0:T(8,128)S(1)}, f32[32,8,128]{2,1,0:T(8,128)S(1)}, f32[8,8,128]{2,1,0:T(8,128)S(1)}, s32[1]{0:T(128)}, /*ind...) while((s32[]{:T(128)}, f32[2,32,8,128]{3,2,1,0:T(8,128)S(1)}, f32[32,8,128]{2,1,0:T(8,128)S(1)}, ...), condition=%wide.region_1.0_spmd, body=%wide.region_0.0_spmd.sunk | while | flops 3 | bytes 1048713 | solution.py:665
  26.1 0.4 shard_map.134
  26.5 0.0 collective-permute-done.3.right
  26.5 0.9 %shard_map.135 = (f32[16,8,128]{2,1,0:T(8,128)S(1)}, f32[16,8,128]{2,1,0:T(8,128)S(1)}, f32[4,32,128]{2,1,0:T(8,128)S(1)}, f32[2,16,128]{2,1,0:T(8,128)S(1)}, f32[2,16,128]{2,1,0:T(8,128)S(1)}) custom-call(s32[1]{0:T(128)S(6)} %copy.31.source_cell, f32[1,2]{1,0:T(1,128)S(1)} %get-tuple-element.78.wavelet, f32[113,8,128]{2,1,0:T(8,128)S(1)} %get-tuple-element.79.own_y, ...), custom_call_target="tpu_custom_call" | custom-call | tf_op jit(solution)/shard_map/pallas_call | solution.py:575
  27.5 1.8 %collective-permute-start.4 = (f32[2,16,128]{2,1,0:T(8,128)S(1)}, f32[2,16,128]{2,1,0:T(8,128)S(1)}, u32[]{:S(2)}, u32[]{:S(2)}) collective-permute-start(f32[2,16,128]{2,1,0:T(8,128)S(1)} %get-tuple-element.111), channel_id=1, source_target_pairs={{0,16},{16,32},{32,48},{48,64},{64,80},{80,96},{96,112},{112,0},{1... | collective-permute-start | bytes 49160 | tf_op jit(solution)/shard_map/ppermute | solution.py:590
  29.3 1.2 %collective-permute-start.5 = (f32[2,16,128]{2,1,0:T(8,128)S(1)}, f32[2,16,128]{2,1,0:T(8,128)S(1)}, u32[]{:S(2)}, u32[]{:S(2)}) collective-permute-start(f32[2,16,128]{2,1,0:T(8,128)S(1)} %get-tuple-element.112), channel_id=1, source_target_pairs={{16,0},{32,16},{48,32},{64,48},{80,64},{96,80},{112,96},{0,112},{1... | collective-permute-start | bytes 49160 | tf_op jit(solution)/shard_map/ppermute | solution.py:591
  30.5 0.7 %shard_map.136 = (f32[32,8,128]{2,1,0:T(8,128)}, f32[32,8,128]{2,1,0:T(8,128)}) custom-call(f32[16,8,128]{2,1,0:T(8,128)S(1)} %get-tuple-element.97.s_mid, f32[16,8,128]{2,1,0:T(8,128)S(1)} %get-tuple-element.98.r_mid, f32[16,8,128]{2,1,0:T(8,128)S(1)} %get-tuple-element.106.s_edge, f32[16,8,128]{2,1,0:T(8,128)S(1)} %get-tuple-element.107.r_edge), custom_call_target="tpu_custom_call" | custom-call | bytes 1000000 | tf_op jit(solution)/shard_map/pallas_call | solution.py:575
  31.2 0.4 collective-permute-done.4.left
  31.6 2.7 %collective-permute-done.5.right = f32[2,16,128]{2,1,0:T(8,128)S(1)} collective-permute-done((f32[2,16,128]{2,1,0:T(8,128)S(1)}, f32[2,16,128]{2,1,0:T(8,128)S(1)}, u32[]{:S(2)}, u32[]{:S(2)}) %collective-permute-start.5) | collective-permute-done | bytes 16416 | tf_op jit(solution)/shard_map/ppermute | solution.py:591
  34.3 0.8 %shard_map.137 = f32[16,8,128]{2,1,0:T(8,128)S(1)} custom-call(f32[32,8,128]{2,1,0:T(8,128)} %get-tuple-element.75.stored, f32[4,32,128]{2,1,0:T(8,128)S(1)} %get-tuple-element.110.near, f32[2,16,128]{2,1,0:T(8,128)S(1)} %collective-permute-done.4.left, f32[2,16,128]{2,1,0:T(8,128)S(1)} %collective-permute-done.5.right), custom_call_target="tpu_custom_call" | custom-call | tf_op jit(solution)/shard_map/pallas_call | solution.py:575
  35.1 12.7 %all_to_all.16.got = f32[16,8,128]{2,1,0:T(8,128)S(1)} all-to-all(f32[16,8,128]{2,1,0:T(8,128)S(1)} %shard_map.137), channel_id=1, replica_groups=mesh['gx'=8,'gy'=16] {'gy'}, dimensions={0} | all-to-all | bytes 131072 | tf_op jit(solution)/shard_map/all_to_all | solution.py:704
  47.8 0.7 %shard_map.138 = f32[2,8,1024]{2,1,0:T(8,128)} custom-call(f32[16,8,128]{2,1,0:T(8,128)S(1)} %all_to_all.16.got), custom_call_target="tpu_custom_call" | custom-call | tf_op jit(solution)/shard_map/pallas_call | solution.py:575
  (2 shorter events, 0.0 us)
Async XLA Ops:
  2.6 12.7 %collective-permute-start = (f32[113,8,128]{2,1,0:T(8,128)S(1)}, f32[113,8,128]{2,1,0:T(8,128)S(1)}, u32[]{:S(2)}, u32[]{:S(2)}) collective-permute-start(f32[113,8,128]{2,1,0:T(8,128)S(1)} %get-tuple-element.79.own_y), channel_id=1, source_target_pairs={{0,1},{1,0},{2,3},{3,2},{4,5},{5,4},{6,7},{7,6},{8,9},{9,8},{10,11... | collective-permute-start | bytes 1388552 | tf_op jit(solution)/shard_map/ppermute | solution.py:622
  3.4 11.9 %collective-permute-start.1 = (f32[113,8,128]{2,1,0:T(8,128)S(1)}, f32[113,8,128]{2,1,0:T(8,128)S(1)}, u32[]{:S(2)}, u32[]{:S(2)}) collective-permute-start(f32[113,8,128]{2,1,0:T(8,128)S(1)} %get-tuple-element.85), channel_id=1, source_target_pairs={{0,15},{1,2},{2,1},{3,4},{4,3},{5,6},{6,5},{7,8},{8,7},{9,10},{10,... | collective-permute-start | bytes 1388552 | tf_op jit(solution)/shard_map/ppermute | solution.py:623
  4.7 17.7 %all-to-all-start.1 = ((f32[128,1,128]{2,1,0:T(1,128)}), f32[128,1,128]{2,1,0:T(1,128)S(1)}, u32[]{:S(2)}, u32[]{:S(2)}) async-start(f32[128,1,128]{2,1,0:T(1,128)} %get-tuple-element.90), calls=%async_computation.1 | async-start | bytes 131072 | tf_op jit(solution)/shard_map/all_to_all | solution.py:624
  15.8 10.7 %collective-permute-start.2 = (f32[29,8,128]{2,1,0:T(8,128)S(1)}, f32[29,8,128]{2,1,0:T(8,128)S(1)}, u32[]{:S(2)}, u32[]{:S(2)}) collective-permute-start(f32[29,8,128]{2,1,0:T(8,128)S(1)} %get-tuple-element.99), channel_id=1, source_target_pairs={{0,16},{16,32},{32,48},{48,64},{64,80},{80,96},{96,112},{112,0},{1... | collective-permute-start | bytes 356360 | tf_op jit(solution)/shard_map/ppermute | solution.py:590
  17.2 9.3 %collective-permute-start.3 = (f32[29,8,128]{2,1,0:T(8,128)S(1)}, f32[29,8,128]{2,1,0:T(8,128)S(1)}, u32[]{:S(2)}, u32[]{:S(2)}) collective-permute-start(f32[29,8,128]{2,1,0:T(8,128)S(1)} %get-tuple-element.100), channel_id=1, source_target_pairs={{16,0},{32,16},{48,32},{64,48},{80,64},{96,80},{112,96},{0,112},{1... | collective-permute-start | bytes 356360 | tf_op jit(solution)/shard_map/ppermute | solution.py:591
  27.5 4.1 %collective-permute-start.4 = (f32[2,16,128]{2,1,0:T(8,128)S(1)}, f32[2,16,128]{2,1,0:T(8,128)S(1)}, u32[]{:S(2)}, u32[]{:S(2)}) collective-permute-start(f32[2,16,128]{2,1,0:T(8,128)S(1)} %get-tuple-element.111), channel_id=1, source_target_pairs={{0,16},{16,32},{32,48},{48,64},{64,80},{80,96},{96,112},{112,0},{1... | collective-permute-start | bytes 49160 | tf_op jit(solution)/shard_map/ppermute | solution.py:590
  29.3 5.0 %collective-permute-start.5 = (f32[2,16,128]{2,1,0:T(8,128)S(1)}, f32[2,16,128]{2,1,0:T(8,128)S(1)}, u32[]{:S(2)}, u32[]{:S(2)}) collective-permute-start(f32[2,16,128]{2,1,0:T(8,128)S(1)} %get-tuple-element.112), channel_id=1, source_target_pairs={{16,0},{32,16},{48,32},{64,48},{80,64},{96,80},{112,96},{0,112},{1... | collective-permute-start | bytes 49160 | tf_op jit(solution)/shard_map/ppermute | solution.py:591

commit v9 on v7

--- a/solution.py
+++ b/solution.py
@@ -557,12 +557,21 @@
         out_ref[b] = jnp.where(lane < 64, packed, other)
 
 
-def arrange_kernel(got, out_ref):
+def arrange_kernel(got, image, out_v, sems):
     lane = iota((8, 128), 1)
-    for t in range(8):
-        even, odd = got[2 * t], got[2 * t + 1]
-        out_ref[0, :, 128 * t : 128 * t + 128] = jnp.where(lane < 64, even, pltpu.roll(odd, 64, 1))
-        out_ref[1, :, 128 * t : 128 * t + 128] = jnp.where(lane < 64, pltpu.roll(even, 64, 1), odd)
+    copies = []
+    for a in range(2):
+        for t in range(8):
+            even, odd = got[2 * t], got[2 * t + 1]
+            if a == 0:
+                odd = pltpu.roll(odd, 64, 1)
+            else:
+                even = pltpu.roll(even, 64, 1)
+            out_v[a, :, 128 * t : 128 * t + 128] = jnp.where(lane < 64, even, odd)
+        copies.append(pltpu.make_async_copy(out_v.at[a], image.at[a], sems.at[a]))
+        copies[a].start()
+    for copy in copies:
+        copy.wait()
 
 
 def call(kernel, outs, arrays, scalars=(), hbm=(), out_scalars=0, out_hbm=(), scratch=(), weight=0):
@@ -701,7 +710,14 @@
         scratch=[pltpu.VMEM((4, 64, 128), F32)],
     )
     angles = lax.all_to_all(angles, "gy", 0, 0, tiled=True)
-    (image,) = call(arrange_kernel, [((2, 8, 1024), F32)], [angles])
+    image_shape = ((2, 8, 1024), F32)
+    (image,) = call(
+        arrange_kernel,
+        [image_shape],
+        [angles],
+        out_hbm=(0,),
+        scratch=[pltpu.VMEM(*image_shape), pltpu.SemaphoreType.DMA((2,))],
+    )
     return source_field, receiver_field, image
 
 

time: 48.8 us -> 48.8 us (level)
  no operation moved by 1% of the time
where the time goes in v9:
time: 48.8 us; the launch traced here: 48.5 us
  starting transfers between devices  18 us (37%)
  blocking collectives  12.7 us (26%)
  Pallas kernels  9.17 us (19%)
  waiting for transfers between devices  6.58 us (13%)
  between operations  1.38 us (3%)
  loops' own time  0.65 us (1%)
    all_to_all x1, blocking collectives, body(): angles = lax.all_to_all(angles, 'gy', 0, 0, tiled=True)  12.7 us
    all_to_all x1, starting transfers between devices, body(): got = lax.all_to_all(sent, ('gx', 'gy'), 0, 0, tiled=True)  10 us
    pallas_call x9, Pallas kernels, call(): pl.pallas_call(kernel, out_shape=[jax.ShapeDtypeStruct(shape, kind) for s...  9.17 us
    all_to_all x1, waiting for transfers between devices, body(): got = lax.all_to_all(sent, ('gx', 'gy'), 0, 0, tiled=True)  3.5 us
    ppermute x2, starting transfers between devices, both_ways(): lax.ppermute(to_next, axis, [(i, (i + 1) % size) for i in range(size)])  3.18 us
    ppermute x2, starting transfers between devices, both_ways(): lax.ppermute(to_last, axis, [((i + 1) % size, i) for i in range(size)])  2.84 us
    ppermute x2, waiting for transfers between devices, both_ways(): lax.ppermute(to_last, axis, [((i + 1) % size, i) for i in range(size)])  2.7 us
    ppermute x1, starting transfers between devices, body(): lax.ppermute(second_y, 'gy', [(i, (i + 1 if i % 2 else i - 1) % GY) for i...  1.27 us
  transfers between devices with their start and end apart: 7, of which 3 were waited for; matrix products, arithmetic and copies ran while one was open for 0% of the time, Pallas kernels for 10%

profile of v9, /device:TPU:5, one launch (start us, length us, event | category | flops | bytes accessed | tf_op | source)
XLA Modules:
  0.0 48.5 jit_solution(7501026606111898907)
XLA Ops:
  0.6 2.0 %shard_map.130 = (f32[113,8,128]{2,1,0:T(8,128)S(1)}, f32[113,8,128]{2,1,0:T(8,128)S(1)}, f32[1,2]{1,0:T(1,128)S(1)}, f32[32,8,128]{2,1,0:T(8,128)S(1)}, f32[32,...) custom-call(s32[1,256]{1,0:T(1,128)} %bitcast.11, ...), custom_call_target="tpu_custom_call" | custom-call | tf_op jit(solution)/shard_map/pallas_call | solution.py:583
  2.6 0.8 %collective-permute-start = (f32[113,8,128]{2,1,0:T(8,128)S(1)}, f32[113,8,128]{2,1,0:T(8,128)S(1)}, u32[]{:S(2)}, u32[]{:S(2)}) collective-permute-start(f32[113,8,128]{2,1,0:T(8,128)S(1)} %get-tuple-element.116.own_y), channel_id=1, source_target_pairs={{0,1},{1,0},{2,3},{3,2},{4,5},{5,4},{6,7},{7,6},{8,9},{9,8},{10,11... | collective-permute-start | bytes 1388552 | tf_op jit(solution)/shard_map/ppermute | solution.py:631
  3.4 1.3 %collective-permute-start.1 = (f32[113,8,128]{2,1,0:T(8,128)S(1)}, f32[113,8,128]{2,1,0:T(8,128)S(1)}, u32[]{:S(2)}, u32[]{:S(2)}) collective-permute-start(f32[113,8,128]{2,1,0:T(8,128)S(1)} %get-tuple-element.122), channel_id=1, source_target_pairs={{0,15},{1,2},{2,1},{3,4},{4,3},{5,6},{6,5},{7,8},{8,7},{9,10},{10,... | collective-permute-start | bytes 1388552 | tf_op jit(solution)/shard_map/ppermute | solution.py:632
  4.7 10.0 %all-to-all-start.1 = ((f32[128,1,128]{2,1,0:T(1,128)}), f32[128,1,128]{2,1,0:T(1,128)S(1)}, u32[]{:S(2)}, u32[]{:S(2)}) async-start(f32[128,1,128]{2,1,0:T(1,128)} %get-tuple-element.127), calls=%async_computation.1 | async-start | bytes 131072 | tf_op jit(solution)/shard_map/all_to_all | solution.py:633
  15.3 0.0 collective-permute-done.first
  15.3 0.0 collective-permute-done.1.second
  15.3 0.5 %shard_map.131 = (f32[2,8,16,128]{3,2,1,0:T(8,128)S(1)}, f32[8,16,128]{2,1,0:T(8,128)S(1)}, s32[16,128]{1,0:T(8,128)S(1)}, f32[16,128]{1,0:T(8,128)S(1)}, f32[29...) custom-call(f32[113,8,128]{2,1,0:T(8,128)S(1)} %get-tuple-element.116.own_y, f32[32,8,128]{2,1,0:T(8,128)S(1)} %get-tuple-element.120.sm, ...), custom_call_target="tpu_custom_call" | custom-call | tf_op jit(solution)/shard_map/pallas_call | solution.py:583
  15.8 1.4 %collective-permute-start.2 = (f32[29,8,128]{2,1,0:T(8,128)S(1)}, f32[29,8,128]{2,1,0:T(8,128)S(1)}, u32[]{:S(2)}, u32[]{:S(2)}) collective-permute-start(f32[29,8,128]{2,1,0:T(8,128)S(1)} %get-tuple-element.136), channel_id=1, source_target_pairs={{0,16},{16,32},{32,48},{48,64},{64,80},{80,96},{96,112},{112,0},{1... | collective-permute-start | bytes 356360 | tf_op jit(solution)/shard_map/ppermute | solution.py:598
  17.2 1.7 %collective-permute-start.3 = (f32[29,8,128]{2,1,0:T(8,128)S(1)}, f32[29,8,128]{2,1,0:T(8,128)S(1)}, u32[]{:S(2)}, u32[]{:S(2)}) collective-permute-start(f32[29,8,128]{2,1,0:T(8,128)S(1)} %get-tuple-element.137), channel_id=1, source_target_pairs={{16,0},{32,16},{48,32},{64,48},{80,64},{96,80},{112,96},{0,112},{1... | collective-permute-start | bytes 356360 | tf_op jit(solution)/shard_map/ppermute | solution.py:599
  18.9 3.5 %all-to-all-done.1 = f32[128,1,128]{2,1,0:T(1,128)S(1)} async-done(((f32[128,1,128]{2,1,0:T(1,128)}), f32[128,1,128]{2,1,0:T(1,128)S(1)}, u32[]{:S(2)}, u32[]{:S(2)}) %all-to-all-start.1) | async-done | bytes 65568 | tf_op jit(solution)/shard_map/all_to_all | solution.py:633
  22.4 1.2 %shard_map.132 = (f32[2,24,16,128]{3,2,1,0:T(8,128)S(1)}, f32[24,16,128]{2,1,0:T(8,128)S(1)}) custom-call(f32[113,8,128]{2,1,0:T(8,128)S(1)} %get-tuple-element.116.own_y, f32[32,8,128]{2,1,0:T(8,128)S(1)} %get-tuple-element.120.sm, f32[32,8,128]{2,1,0:T(8,128)S(1)} %get-tuple-element.121.rm, f32[32,8,128]{2,1,0:T(8,128)S(1)} %get-tuple-element.117.c, ...), custom_call_target="tpu_custom_call" | custom-call | tf_op jit(solution)/shard_map/pallas_call | solution.py:583
  23.6 1.9 %shard_map.133 = (f32[2,32,8,128]{3,2,1,0:T(8,128)S(1)}, f32[32,8,128]{2,1,0:T(8,128)S(1)}, f32[8,8,128]{2,1,0:T(8,128)S(1)}, s32[1]{0:T(128)}) custom-call(f32[128,128]{1,0:T(8,128)S(1)} %maximum_bitcast_fusion.got_ref, f32[24,16,128]{2,1,0:T(8,128)S(1)} %get-tuple-element.126.inner_courant), custom_call_target="tpu_custom_call" | custom-call | bytes 1000 | tf_op jit(solution)/shard_map/pallas_call | solution.py:583
  25.4 0.7 %while.16 = (s32[1]{0:T(128)}, f32[2,32,8,128]{3,2,1,0:T(8,128)S(1)}, f32[32,8,128]{2,1,0:T(8,128)S(1)}, f32[8,8,128]{2,1,0:T(8,128)S(1)}, s32[1,256]{1,0:T(1,12...) while((s32[1]{0:T(128)}, f32[2,32,8,128]{3,2,1,0:T(8,128)S(1)}, f32[32,8,128]{2,1,0:T(8,128)S(1)}, ...), condition=%wide.region_1.0_spmd, body=%wide.region_0.0_spmd | while | flops 3 | bytes 1048705 | solution.py:673
  26.1 0.4 shard_map.134
  26.5 0.0 collective-permute-done.2.left
  26.5 1.0 %shard_map.135 = (f32[16,8,128]{2,1,0:T(8,128)S(1)}, f32[16,8,128]{2,1,0:T(8,128)S(1)}, f32[4,32,128]{2,1,0:T(8,128)S(1)}, f32[2,16,128]{2,1,0:T(8,128)S(1)}, f32[2,16,128]{2,1,0:T(8,128)S(1)}) custom-call(s32[1,1]{1,0:T(1,128)} %bitcast.9.source_cell, f32[1,2]{1,0:T(1,128)S(1)} %get-tuple-element.115.wavelet, f32[113,8,128]{2,1,0:T(8,128)S(1)} %get-tuple-element.116.own_y, ...), custom_call_target="tpu_custom_call" | custom-call | tf_op jit(solution)/shard_map/pallas_call | solution.py:583
  27.5 1.8 %collective-permute-start.4 = (f32[2,16,128]{2,1,0:T(8,128)S(1)}, f32[2,16,128]{2,1,0:T(8,128)S(1)}, u32[]{:S(2)}, u32[]{:S(2)}) collective-permute-start(f32[2,16,128]{2,1,0:T(8,128)S(1)} %get-tuple-element.148), channel_id=1, source_target_pairs={{0,16},{16,32},{32,48},{48,64},{64,80},{80,96},{96,112},{112,0},{1... | collective-permute-start | bytes 49160 | tf_op jit(solution)/shard_map/ppermute | solution.py:598
  29.3 1.2 %collective-permute-start.5 = (f32[2,16,128]{2,1,0:T(8,128)S(1)}, f32[2,16,128]{2,1,0:T(8,128)S(1)}, u32[]{:S(2)}, u32[]{:S(2)}) collective-permute-start(f32[2,16,128]{2,1,0:T(8,128)S(1)} %get-tuple-element.149), channel_id=1, source_target_pairs={{16,0},{32,16},{48,32},{64,48},{80,64},{96,80},{112,96},{0,112},{1... | collective-permute-start | bytes 49160 | tf_op jit(solution)/shard_map/ppermute | solution.py:599
  30.5 0.7 %shard_map.136 = (f32[32,8,128]{2,1,0:T(8,128)}, f32[32,8,128]{2,1,0:T(8,128)}) custom-call(f32[16,8,128]{2,1,0:T(8,128)S(1)} %get-tuple-element.134.s_mid, f32[16,8,128]{2,1,0:T(8,128)S(1)} %get-tuple-element.135.r_mid, f32[16,8,128]{2,1,0:T(8,128)S(1)} %get-tuple-element.143.s_edge, f32[16,8,128]{2,1,0:T(8,128)S(1)} %get-tuple-element.144.r_edge), custom_call_target="tpu_custom_call" | custom-call | bytes 1000000 | tf_op jit(solution)/shard_map/pallas_call | solution.py:583
  31.3 0.4 collective-permute-done.4.left
  31.6 2.7 %collective-permute-done.5.right = f32[2,16,128]{2,1,0:T(8,128)S(1)} collective-permute-done((f32[2,16,128]{2,1,0:T(8,128)S(1)}, f32[2,16,128]{2,1,0:T(8,128)S(1)}, u32[]{:S(2)}, u32[]{:S(2)}) %collective-permute-start.5) | collective-permute-done | bytes 16416 | tf_op jit(solution)/shard_map/ppermute | solution.py:599
  34.3 0.8 %shard_map.137 = f32[16,8,128]{2,1,0:T(8,128)S(1)} custom-call(f32[32,8,128]{2,1,0:T(8,128)} %get-tuple-element.112.stored, f32[4,32,128]{2,1,0:T(8,128)S(1)} %get-tuple-element.147.near, f32[2,16,128]{2,1,0:T(8,128)S(1)} %collective-permute-done.4.left, f32[2,16,128]{2,1,0:T(8,128)S(1)} %collective-permute-done.5.right), custom_call_target="tpu_custom_call" | custom-call | tf_op jit(solution)/shard_map/pallas_call | solution.py:583
  35.1 12.7 %all_to_all.15.got = f32[16,8,128]{2,1,0:T(8,128)S(1)} all-to-all(f32[16,8,128]{2,1,0:T(8,128)S(1)} %shard_map.137), channel_id=1, replica_groups=mesh['gx'=8,'gy'=16] {'gy'}, dimensions={0} | all-to-all | bytes 131072 | tf_op jit(solution)/shard_map/all_to_all | solution.py:712
  47.8 0.7 %shard_map.138 = f32[2,8,1024]{2,1,0:T(8,128)} custom-call(f32[16,8,128]{2,1,0:T(8,128)S(1)} %all_to_all.15.got), custom_call_target="tpu_custom_call" | custom-call | tf_op jit(solution)/shard_map/pallas_call | solution.py:583
  (2 shorter events, 0.0 us)
Async XLA Ops:
  2.6 12.7 %collective-permute-start = (f32[113,8,128]{2,1,0:T(8,128)S(1)}, f32[113,8,128]{2,1,0:T(8,128)S(1)}, u32[]{:S(2)}, u32[]{:S(2)}) collective-permute-start(f32[113,8,128]{2,1,0:T(8,128)S(1)} %get-tuple-element.116.own_y), channel_id=1, source_target_pairs={{0,1},{1,0},{2,3},{3,2},{4,5},{5,4},{6,7},{7,6},{8,9},{9,8},{10,11... | collective-permute-start | bytes 1388552 | tf_op jit(solution)/shard_map/ppermute | solution.py:631
  3.4 11.9 %collective-permute-start.1 = (f32[113,8,128]{2,1,0:T(8,128)S(1)}, f32[113,8,128]{2,1,0:T(8,128)S(1)}, u32[]{:S(2)}, u32[]{:S(2)}) collective-permute-start(f32[113,8,128]{2,1,0:T(8,128)S(1)} %get-tuple-element.122), channel_id=1, source_target_pairs={{0,15},{1,2},{2,1},{3,4},{4,3},{5,6},{6,5},{7,8},{8,7},{9,10},{10,... | collective-permute-start | bytes 1388552 | tf_op jit(solution)/shard_map/ppermute | solution.py:632
  4.7 17.7 %all-to-all-start.1 = ((f32[128,1,128]{2,1,0:T(1,128)}), f32[128,1,128]{2,1,0:T(1,128)S(1)}, u32[]{:S(2)}, u32[]{:S(2)}) async-start(f32[128,1,128]{2,1,0:T(1,128)} %get-tuple-element.127), calls=%async_computation.1 | async-start | bytes 131072 | tf_op jit(solution)/shard_map/all_to_all | solution.py:633
  15.8 10.7 %collective-permute-start.2 = (f32[29,8,128]{2,1,0:T(8,128)S(1)}, f32[29,8,128]{2,1,0:T(8,128)S(1)}, u32[]{:S(2)}, u32[]{:S(2)}) collective-permute-start(f32[29,8,128]{2,1,0:T(8,128)S(1)} %get-tuple-element.136), channel_id=1, source_target_pairs={{0,16},{16,32},{32,48},{48,64},{64,80},{80,96},{96,112},{112,0},{1... | collective-permute-start | bytes 356360 | tf_op jit(solution)/shard_map/ppermute | solution.py:598
  17.2 9.3 %collective-permute-start.3 = (f32[29,8,128]{2,1,0:T(8,128)S(1)}, f32[29,8,128]{2,1,0:T(8,128)S(1)}, u32[]{:S(2)}, u32[]{:S(2)}) collective-permute-start(f32[29,8,128]{2,1,0:T(8,128)S(1)} %get-tuple-element.137), channel_id=1, source_target_pairs={{16,0},{32,16},{48,32},{64,48},{80,64},{96,80},{112,96},{0,112},{1... | collective-permute-start | bytes 356360 | tf_op jit(solution)/shard_map/ppermute | solution.py:599
  27.5 4.1 %collective-permute-start.4 = (f32[2,16,128]{2,1,0:T(8,128)S(1)}, f32[2,16,128]{2,1,0:T(8,128)S(1)}, u32[]{:S(2)}, u32[]{:S(2)}) collective-permute-start(f32[2,16,128]{2,1,0:T(8,128)S(1)} %get-tuple-element.148), channel_id=1, source_target_pairs={{0,16},{16,32},{32,48},{48,64},{64,80},{80,96},{96,112},{112,0},{1... | collective-permute-start | bytes 49160 | tf_op jit(solution)/shard_map/ppermute | solution.py:598
  29.3 5.0 %collective-permute-start.5 = (f32[2,16,128]{2,1,0:T(8,128)S(1)}, f32[2,16,128]{2,1,0:T(8,128)S(1)}, u32[]{:S(2)}, u32[]{:S(2)}) collective-permute-start(f32[2,16,128]{2,1,0:T(8,128)S(1)} %get-tuple-element.149), channel_id=1, source_target_pairs={{16,0},{32,16},{48,32},{64,48},{80,64},{96,80},{112,96},{0,112},{1... | collective-permute-start | bytes 49160 | tf_op jit(solution)/shard_map/ppermute | solution.py:599
